TPU v7x, 32 devices: a whole 2x2x4 slice. The times are simulated.
32 devices in a mesh: dp: 16 (over z, y, x), mp: 2 (over core).
Axes of the slice: x: 2, y: 2, z: 4, core: 2. Of those that a mesh axis runs over, the one named last changes fastest.
Arguments:
- lang: bfloat16 [512, 20, 768], P(('dp', 'mp')), may hold values from -6 to 6
- vis: bfloat16 [512, 36, 768], P(('dp', 'mp')), may hold values from -6 to 6
- word_mask: int32 [512, 20], P(('dp', 'mp')), may hold values from 0 to 1, as said below
- region_count: int32 [512], P(('dp', 'mp')), may hold values from 10 to 36, as said below
- cot_lang: bfloat16 [512, 20, 768], P(('dp', 'mp')), may hold values from -6 to 6
- cot_vis: bfloat16 [512, 36, 768], P(('dp', 'mp')), may hold values from -6 to 6
- attn_w: float32 [3, 4, 768, 768], P(None, None, 'dp', 'mp'), may hold values from -0.4330127 to 0.4330127
- attn_m: float32 [3, 4, 768, 768], P(None, None, 'dp', 'mp'), may hold values from -0.0010301495 to 0.0010301495
- attn_v: float32 [3, 4, 768, 768], P(None, None, 'dp', 'mp'), may hold values from 0 to 6.75028755e-07
- attn_ema: float32 [3, 4, 768, 768], P(None, None, 'dp', 'mp'), may hold values from -0.4330127 to 0.4330127
- ffn_w: float32 [2, 2, 768, 3072], P(None, None, 'dp', 'mp'), may hold values from -0.14433757 to 0.14433757
- ffn_m: float32 [2, 2, 768, 3072], P(None, None, 'dp', 'mp'), may hold values from -0.00040017346 to 0.00040017346
- ffn_v: float32 [2, 2, 768, 3072], P(None, None, 'dp', 'mp'), may hold values from 0 to 1.09888402e-07
- ffn_ema: float32 [2, 2, 768, 3072], P(None, None, 'dp', 'mp'), may hold values from -0.14433757 to 0.14433757
- gains: float32 [5, 768], P(None, 'dp'), may hold values from 0.35 to 1.9
- gains_m: float32 [5, 768], P(None, 'dp'), may hold values from -0.0048828125 to 0.0048828125
- gains_v: float32 [5, 768], P(None, 'dp'), may hold values from 7.535205e-08 to 3.02978e-07
- gains_ema: float32 [5, 768], P(None, 'dp'), may hold values from 0.5 to 1.5
- biases: float32 [16, 768], P(None, 'dp'), may hold values from -3 to 3
- biases_m: float32 [16, 768], P(None, 'dp'), may hold values from -0.0048828125 to 0.0048828125
- biases_v: float32 [16, 768], P(None, 'dp'), may hold values from 7.535205e-08 to 3.02978e-07
- biases_ema: float32 [16, 768], P(None, 'dp'), may hold values from -3 to 3
- bias_up: float32 [2, 3072], P(None, 'dp'), may hold values from -3 to 3
- bias_up_m: float32 [2, 3072], P(None, 'dp'), may hold values from -0.0014648438 to 0.0014648438
- bias_up_v: float32 [2, 3072], P(None, 'dp'), may hold values from 7.0642545e-09 to 2.8257018e-08
- bias_up_ema: float32 [2, 3072], P(None, 'dp'), may hold values from -3 to 3
Outputs:
- out_lang: float32 [512, 20, 768], P(('dp', 'mp'))
- out_vis: float32 [512, 36, 768], P(('dp', 'mp'))
- grad_lang: float32 [512, 20, 768], P(('dp', 'mp'))
- grad_vis: float32 [512, 36, 768], P(('dp', 'mp'))
- grad_norm: float32 [], replicated
- attn_w_new: float32 [3, 4, 768, 768], P(None, None, 'dp', 'mp')
- attn_m_new: float32 [3, 4, 768, 768], P(None, None, 'dp', 'mp')
- attn_v_new: float32 [3, 4, 768, 768], P(None, None, 'dp', 'mp')
- attn_ema_new: float32 [3, 4, 768, 768], P(None, None, 'dp', 'mp')
- ffn_w_new: float32 [2, 2, 768, 3072], P(None, None, 'dp', 'mp')
- ffn_m_new: float32 [2, 2, 768, 3072], P(None, None, 'dp', 'mp')
- ffn_v_new: float32 [2, 2, 768, 3072], P(None, None, 'dp', 'mp')
- ffn_ema_new: float32 [2, 2, 768, 3072], P(None, None, 'dp', 'mp')
- gains_new: float32 [5, 768], P(None, 'dp')
- gains_m_new: float32 [5, 768], P(None, 'dp')
- gains_v_new: float32 [5, 768], P(None, 'dp')
- gains_ema_new: float32 [5, 768], P(None, 'dp')
- biases_new: float32 [16, 768], P(None, 'dp')
- biases_m_new: float32 [16, 768], P(None, 'dp')
- biases_v_new: float32 [16, 768], P(None, 'dp')
- biases_ema_new: float32 [16, 768], P(None, 'dp')
- bias_up_new: float32 [2, 3072], P(None, 'dp')
- bias_up_m_new: float32 [2, 3072], P(None, 'dp')
- bias_up_v_new: float32 [2, 3072], P(None, 'dp')
- bias_up_ema_new: float32 [2, 3072], P(None, 'dp')
Inputs may be any that keep to these rules, and one draw needn't show every extreme that they name: `word_mask`: each row is 1 on its first l positions and 0 after them, with l from 6 to 20; some row has l = 20 and some l = 6. `region_count`: some item has 36 regions and some 10.
All inputs are finite; a program needn't handle non-finite values.
Results may differ from a plain program's by a relative error of at most 0.019.
The roundings to bfloat16 on the way count: a program that leaves them out, or rounds other values in their place, can miss the bound.
Values may be sent and summed in bfloat16 or wider, within the bound.
No kernel may reach another device: no remote copies, remote signals or barrier semaphores. Data moves between devices by JAX's collectives and lax.ppermute only.
A program may use at most 256 MiB of HBM per device.

v0:
```python
import jax
import jax.numpy as jnp
from jax import lax
from jax.sharding import PartitionSpec as P

HEAD_DIM = 64
STEP = 7


norm_eps = 1e-12
mask_fill = -1000000000.0
beta_one = 0.5
beta_two = 0.6
ema_decay = 0.5
adam_eps = 1e-08
weight_decay = 0.01
rate_mats = 0.02
rate_small = 0.2
clip_norm = 1.0


def exact_gelu(values):
    return jax.nn.gelu(values, approximate=False)


def norm_forward(summed, gain, shift):
    average = jnp.mean(summed, axis=-1, keepdims=True)
    centered = summed - average
    inverse = lax.rsqrt(jnp.mean(centered * centered, axis=-1, keepdims=True) + norm_eps)
    normed = centered * inverse
    return (normed * gain + shift, (normed, inverse))


def norm_backward(grad_out, stored, gain):
    normed, inverse = stored
    scaled = grad_out * gain
    grad_in = inverse * (
        scaled
        - jnp.mean(scaled, axis=-1, keepdims=True)
        - normed * jnp.mean(scaled * normed, axis=-1, keepdims=True)
    )
    return (grad_in, jnp.sum(grad_out * normed, axis=(0, 1)), jnp.sum(grad_out, axis=(0, 1)))


def split_heads(values):
    return values.reshape(values.shape[0], values.shape[1], values.shape[2] // HEAD_DIM, HEAD_DIM)


def masked_scores(queries, keys, key_live):
    scores = jnp.einsum(
        "gnhe,gmhe->ghnm",
        split_heads(queries),
        split_heads(keys),
        preferred_element_type=jnp.float32,
    )
    return scores * HEAD_DIM ** (-0.5) + mask_fill * (1.0 - key_live)[:, None, None, :]


def attend_forward(query_in, context_in, key_live, matrices, bias_query, bias_value):
    queries = (
        jnp.einsum("gnd,dk->gnk", query_in, matrices[0], preferred_element_type=jnp.float32)
        + bias_query
    ).astype(jnp.bfloat16)
    keys = jnp.einsum(
        "gnd,dk->gnk", context_in, matrices[1], preferred_element_type=jnp.float32
    ).astype(jnp.bfloat16)
    values = (
        jnp.einsum("gnd,dk->gnk", context_in, matrices[2], preferred_element_type=jnp.float32)
        + bias_value
    ).astype(jnp.bfloat16)
    scores = masked_scores(queries, keys, key_live)
    row_max = jnp.max(scores, axis=-1, keepdims=True)
    powers = jnp.exp(scores - row_max)
    totals = jnp.sum(powers, axis=-1, keepdims=True)
    weights_low = (powers / totals).astype(jnp.bfloat16)
    context = jnp.einsum(
        "ghnm,gmhe->gnhe", weights_low, split_heads(values), preferred_element_type=jnp.float32
    )
    context = context.reshape(queries.shape).astype(jnp.bfloat16)
    summand = jnp.einsum("gnk,dk->gnd", context, matrices[3], preferred_element_type=jnp.float32)
    return (summand, (queries, keys, values, row_max + jnp.log(totals), weights_low, context))


def attend_backward(grad_out, query_in, context_in, key_live, matrices, stored):
    queries, keys, values, log_total, weights_low, context = stored
    grad_context = jnp.einsum(
        "gnd,dk->gnk", grad_out, matrices[3], preferred_element_type=jnp.float32
    ).astype(jnp.bfloat16)
    grad_output = jnp.einsum("gnd,gnk->dk", grad_out, context, preferred_element_type=jnp.float32)
    weights = jnp.exp(masked_scores(queries, keys, key_live) - log_total)
    grad_weights = jnp.einsum(
        "gnhe,gmhe->ghnm",
        split_heads(grad_context),
        split_heads(values),
        preferred_element_type=jnp.float32,
    )
    grad_scores = (
        weights * (grad_weights - jnp.sum(grad_weights * weights, axis=-1, keepdims=True))
    ).astype(jnp.bfloat16)
    grad_queries = jnp.einsum(
        "ghnm,gmhe->gnhe", grad_scores, split_heads(keys), preferred_element_type=jnp.float32
    ) * HEAD_DIM ** (-0.5)
    grad_queries = grad_queries.reshape(queries.shape).astype(jnp.bfloat16)
    grad_keys = jnp.einsum(
        "ghnm,gnhe->gmhe", grad_scores, split_heads(queries), preferred_element_type=jnp.float32
    ) * HEAD_DIM ** (-0.5)
    grad_keys = grad_keys.reshape(keys.shape).astype(jnp.bfloat16)
    grad_values = jnp.einsum(
        "ghnm,gnhe->gmhe",
        weights_low,
        split_heads(grad_context),
        preferred_element_type=jnp.float32,
    )
    grad_values = grad_values.reshape(values.shape).astype(jnp.bfloat16)
    grad_mats = jnp.stack(
        [
            jnp.einsum("gnd,gnk->dk", query_in, grad_queries, preferred_element_type=jnp.float32),
            jnp.einsum("gnd,gnk->dk", context_in, grad_keys, preferred_element_type=jnp.float32),
            jnp.einsum("gnd,gnk->dk", context_in, grad_values, preferred_element_type=jnp.float32),
            grad_output,
        ]
    )
    query_bias = jnp.sum(grad_queries.astype(jnp.float32), axis=(0, 1))
    value_bias = jnp.sum(grad_values.astype(jnp.float32), axis=(0, 1))
    grad_query_in = jnp.einsum(
        "gnk,dk->gnd", grad_queries, matrices[0], preferred_element_type=jnp.float32
    )
    grad_context_in = jnp.einsum(
        "gnk,dk->gnd", grad_keys, matrices[1], preferred_element_type=jnp.float32
    )
    grad_context_in = grad_context_in + jnp.einsum(
        "gnk,dk->gnd", grad_values, matrices[2], preferred_element_type=jnp.float32
    )
    return (grad_mats, query_bias, value_bias, grad_query_in, grad_context_in)


def feed_forward(rows_in, matrices, bias_hidden):
    hidden = (
        jnp.einsum("gnd,df->gnf", rows_in, matrices[0], preferred_element_type=jnp.float32)
        + bias_hidden
    )
    active = exact_gelu(hidden).astype(jnp.bfloat16)
    summand = jnp.einsum("gnf,df->gnd", active, matrices[1], preferred_element_type=jnp.float32)
    return (summand, (hidden, active))


def feed_backward(grad_out, rows_in, matrices, stored):
    hidden, active = stored
    grad_down = jnp.einsum("gnd,gnf->df", grad_out, active, preferred_element_type=jnp.float32)
    grad_active = jnp.einsum(
        "gnd,df->gnf", grad_out, matrices[1], preferred_element_type=jnp.float32
    )
    _, pullback = jax.vjp(exact_gelu, hidden)
    grad_hidden = pullback(grad_active)[0].astype(jnp.bfloat16)
    grad_up = jnp.einsum("gnd,gnf->df", rows_in, grad_hidden, preferred_element_type=jnp.float32)
    bias_grad = jnp.sum(grad_hidden.astype(jnp.float32), axis=(0, 1))
    grad_in = jnp.einsum(
        "gnf,df->gnd", grad_hidden, matrices[0], preferred_element_type=jnp.float32
    )
    return (jnp.stack([grad_up, grad_down]), bias_grad, grad_in)


def spread_rows(former, latter):
    return (
        lax.all_gather(former, "mp", axis=0, tiled=True),
        lax.all_gather(latter, "mp", axis=0, tiled=True),
    )


def sum_rows(former, latter):
    return (
        lax.psum_scatter(former, "mp", scatter_dimension=0, tiled=True),
        lax.psum_scatter(latter, "mp", scatter_dimension=0, tiled=True),
    )


def spread_grads(former, latter):
    return (
        lax.all_gather(former, "mp", axis=0, tiled=True),
        lax.all_gather(latter, "mp", axis=0, tiled=True),
    )


def sum_grads(former, latter):
    return (
        lax.psum_scatter(former, "mp", scatter_dimension=0, tiled=True),
        lax.psum_scatter(latter, "mp", scatter_dimension=0, tiled=True),
    )


def adam_update(weight, moment_one, moment_two, average, grad, clip, rate):
    clipped = grad * clip
    new_one = beta_one * moment_one + (1.0 - beta_one) * clipped
    new_two = beta_two * moment_two + (1.0 - beta_two) * clipped * clipped
    direction = (
        new_one / (1.0 - beta_one**STEP) / (jnp.sqrt(new_two / (1.0 - beta_two**STEP)) + adam_eps)
    )
    new_weight = weight - rate * (direction + weight_decay * weight)
    new_average = ema_decay * average + (1.0 - ema_decay) * new_weight
    return (new_weight, new_one, new_two, new_average)


def local(
    lang,
    vis,
    word_mask,
    region_count,
    cot_lang,
    cot_vis,
    attn_w,
    attn_m,
    attn_v,
    attn_ema,
    ffn_w,
    ffn_m,
    ffn_v,
    ffn_ema,
    gains,
    gains_m,
    gains_v,
    gains_ema,
    biases,
    biases_m,
    biases_v,
    biases_ema,
    bias_up,
    bias_up_m,
    bias_up_v,
    bias_up_ema,
):
    core_index = lax.axis_index("mp")
    batch_index = lax.axis_index("dp")
    head_width = attn_w.shape[3]
    unit_width = ffn_w.shape[3]
    model_share = gains.shape[1]
    hidden_share = bias_up.shape[1]
    matrices, ffn_mats = (
        lax.all_gather(attn_w.astype(jnp.bfloat16), "dp", axis=2, tiled=True),
        lax.all_gather(ffn_w.astype(jnp.bfloat16), "dp", axis=2, tiled=True),
    )
    gain_all, bias_all, up_all = (
        lax.all_gather(gains, "dp", axis=1, tiled=True),
        lax.all_gather(biases, "dp", axis=1, tiled=True),
        lax.all_gather(bias_up, "dp", axis=1, tiled=True),
    )
    model_width = gain_all.shape[1]
    hidden_width = up_all.shape[1]

    def own_heads(vector):
        return lax.dynamic_slice_in_dim(vector, core_index * head_width, head_width)

    def place_heads(vector):
        return lax.dynamic_update_slice_in_dim(
            jnp.zeros((model_width,), jnp.float32), vector, core_index * head_width, 0
        )

    word_live = word_mask.astype(jnp.float32)
    region_live = (jnp.arange(vis.shape[1])[None, :] < region_count[:, None]).astype(jnp.float32)
    group_lang, group_vis, word_group, region_group = (
        lax.all_gather(lang, "mp", axis=0, tiled=True),
        lax.all_gather(vis, "mp", axis=0, tiled=True),
        lax.all_gather(word_live.astype(jnp.bfloat16), "mp", axis=0, tiled=True),
        lax.all_gather(region_live.astype(jnp.bfloat16), "mp", axis=0, tiled=True),
    )
    live_rows = [word_live, region_live]
    live_keys = [word_group.astype(jnp.float32), region_group.astype(jnp.float32)]
    residual = [lang.astype(jnp.float32), vis.astype(jnp.float32)]
    grouped_one = [group_lang, group_vis]
    cross_parts = []
    cross_kept = []
    for stream in range(2):
        summand, stored = attend_forward(
            grouped_one[stream],
            grouped_one[1 - stream],
            live_keys[1 - stream],
            matrices[0],
            own_heads(bias_all[0]),
            own_heads(bias_all[1]),
        )
        cross_parts.append(summand)
        cross_kept.append(stored)
    added_lang, added_vis = sum_rows(cross_parts[0], cross_parts[1])
    added_rows = [added_lang, added_vis]
    stream_one = []
    norm_one = []
    for stream in range(2):
        normed, stored = norm_forward(
            residual[stream] + added_rows[stream] + bias_all[2], gain_all[0], bias_all[11]
        )
        stream_one.append(normed)
        norm_one.append(stored)
    group_lang2, group_vis2 = spread_rows(
        stream_one[0].astype(jnp.bfloat16), stream_one[1].astype(jnp.bfloat16)
    )
    grouped_two = [group_lang2, group_vis2]
    self_parts = []
    self_kept = []
    for stream in range(2):
        summand, stored = attend_forward(
            grouped_two[stream],
            grouped_two[stream],
            live_keys[stream],
            matrices[1 + stream],
            own_heads(bias_all[3 + 3 * stream]),
            own_heads(bias_all[4 + 3 * stream]),
        )
        self_parts.append(summand)
        self_kept.append(stored)
    added_lang, added_vis = sum_rows(self_parts[0], self_parts[1])
    added_rows = [added_lang, added_vis]
    stream_two = []
    norm_two = []
    for stream in range(2):
        normed, stored = norm_forward(
            stream_one[stream] + added_rows[stream] + bias_all[5 + 3 * stream],
            gain_all[1 + stream],
            bias_all[12 + stream],
        )
        stream_two.append(normed)
        norm_two.append(stored)
    group_lang3, group_vis3 = spread_rows(
        stream_two[0].astype(jnp.bfloat16), stream_two[1].astype(jnp.bfloat16)
    )
    grouped_three = [group_lang3, group_vis3]
    feed_parts = []
    feed_kept = []
    for stream in range(2):
        bias_hidden = lax.dynamic_slice_in_dim(up_all[stream], core_index * unit_width, unit_width)
        summand, stored = feed_forward(grouped_three[stream], ffn_mats[stream], bias_hidden)
        feed_parts.append(summand)
        feed_kept.append(stored)
    added_lang, added_vis = sum_rows(feed_parts[0], feed_parts[1])
    added_rows = [added_lang, added_vis]
    outputs = []
    norm_three = []
    for stream in range(2):
        normed, stored = norm_forward(
            stream_two[stream] + added_rows[stream] + bias_all[9 + stream],
            gain_all[3 + stream],
            bias_all[14 + stream],
        )
        outputs.append(normed * live_rows[stream][..., None])
        norm_three.append(stored)
    cotangents = [
        cot_lang.astype(jnp.float32) * word_live[..., None],
        cot_vis.astype(jnp.float32) * region_live[..., None],
    ]
    gain_rows = [None] * 5
    bias_rows = [None] * 16
    up_rows = []
    sent_three = []
    grad_three = []
    for stream in range(2):
        grad_sum, grad_gain, grad_shift = norm_backward(
            cotangents[stream], norm_three[stream], gain_all[3 + stream]
        )
        sent = grad_sum.astype(jnp.bfloat16)
        grad_three.append(grad_sum)
        sent_three.append(sent)
        gain_rows[3 + stream] = grad_gain
        bias_rows[14 + stream] = grad_shift
        bias_rows[9 + stream] = jnp.sum(sent.astype(jnp.float32), axis=(0, 1))
    grad_group_l, grad_group_v = spread_grads(sent_three[0], sent_three[1])
    grad_groups = [grad_group_l, grad_group_v]
    feed_mats = []
    feed_inputs = []
    for stream in range(2):
        grad_mats, bias_grad, grad_in = feed_backward(
            grad_groups[stream], grouped_three[stream], ffn_mats[stream], feed_kept[stream]
        )
        feed_mats.append(grad_mats)
        feed_inputs.append(grad_in)
        up_rows.append(
            lax.dynamic_update_slice_in_dim(
                jnp.zeros((hidden_width,), jnp.float32), bias_grad, core_index * unit_width, 0
            )
        )
    back_lang, back_vis = sum_grads(feed_inputs[0], feed_inputs[1])
    carried = [grad_three[0] + back_lang, grad_three[1] + back_vis]
    ffn_grad = jnp.stack(feed_mats)
    sent_two = []
    grad_two = []
    for stream in range(2):
        grad_sum, grad_gain, grad_shift = norm_backward(
            carried[stream], norm_two[stream], gain_all[1 + stream]
        )
        sent = grad_sum.astype(jnp.bfloat16)
        grad_two.append(grad_sum)
        sent_two.append(sent)
        gain_rows[1 + stream] = grad_gain
        bias_rows[12 + stream] = grad_shift
        bias_rows[5 + 3 * stream] = jnp.sum(sent.astype(jnp.float32), axis=(0, 1))
    grad_group_l, grad_group_v = spread_grads(sent_two[0], sent_two[1])
    grad_groups = [grad_group_l, grad_group_v]
    self_mats = []
    self_inputs = []
    for stream in range(2):
        grad_mats, query_bias, value_bias, grad_query, grad_context = attend_backward(
            grad_groups[stream],
            grouped_two[stream],
            grouped_two[stream],
            live_keys[stream],
            matrices[1 + stream],
            self_kept[stream],
        )
        self_mats.append(grad_mats)
        self_inputs.append(grad_query + grad_context)
        bias_rows[3 + 3 * stream] = place_heads(query_bias)
        bias_rows[4 + 3 * stream] = place_heads(value_bias)
    back_lang, back_vis = sum_grads(self_inputs[0], self_inputs[1])
    carried = [grad_two[0] + back_lang, grad_two[1] + back_vis]
    sent_one = []
    grad_one = []
    cross_gain = jnp.zeros((model_width,), jnp.float32)
    cross_shift = jnp.zeros((model_width,), jnp.float32)
    cross_out = jnp.zeros((model_width,), jnp.float32)
    for stream in range(2):
        grad_sum, grad_gain, grad_shift = norm_backward(
            carried[stream], norm_one[stream], gain_all[0]
        )
        sent = grad_sum.astype(jnp.bfloat16)
        grad_one.append(grad_sum)
        sent_one.append(sent)
        cross_gain = cross_gain + grad_gain
        cross_shift = cross_shift + grad_shift
        cross_out = cross_out + jnp.sum(sent.astype(jnp.float32), axis=(0, 1))
    grad_group_l, grad_group_v = spread_grads(sent_one[0], sent_one[1])
    grad_groups = [grad_group_l, grad_group_v]
    cross_results = []
    for stream in range(2):
        cross_results.append(
            attend_backward(
                grad_groups[stream],
                grouped_one[stream],
                grouped_one[1 - stream],
                live_keys[1 - stream],
                matrices[0],
                cross_kept[stream],
            )
        )
    cross_inputs = [
        cross_results[0][3] + cross_results[1][4],
        cross_results[1][3] + cross_results[0][4],
    ]
    back_lang, back_vis = sum_grads(cross_inputs[0], cross_inputs[1])
    grad_lang = grad_one[0] + back_lang
    grad_vis = grad_one[1] + back_vis
    gain_rows[0] = cross_gain
    bias_rows[11] = cross_shift
    bias_rows[2] = cross_out
    bias_rows[0] = place_heads(cross_results[0][1] + cross_results[1][1])
    bias_rows[1] = place_heads(cross_results[0][2] + cross_results[1][2])
    attn_grad = jnp.stack([cross_results[0][0] + cross_results[1][0], self_mats[0], self_mats[1]])
    attn_shard, ffn_shard = (
        lax.psum_scatter(attn_grad, "dp", scatter_dimension=2, tiled=True),
        lax.psum_scatter(ffn_grad, "dp", scatter_dimension=2, tiled=True),
    )
    gains_whole, biases_whole, up_whole = lax.psum(
        (jnp.stack(gain_rows), jnp.stack(bias_rows), jnp.stack(up_rows)), ("dp", "mp")
    )
    gains_shard = lax.dynamic_slice_in_dim(gains_whole, batch_index * model_share, model_share, 1)
    biases_shard = lax.dynamic_slice_in_dim(biases_whole, batch_index * model_share, model_share, 1)
    up_shard = lax.dynamic_slice_in_dim(up_whole, batch_index * hidden_share, hidden_share, 1)
    small_squares = (
        jnp.sum(gains_shard * gains_shard)
        + jnp.sum(biases_shard * biases_shard)
        + jnp.sum(up_shard * up_shard)
    )
    squares = jnp.sum(attn_shard * attn_shard) + jnp.sum(ffn_shard * ffn_shard)
    squares = squares + jnp.where(core_index == 0, small_squares, 0.0)
    grad_norm = jnp.sqrt(lax.psum(squares, ("dp", "mp")))
    clip = jnp.minimum(1.0, clip_norm / (grad_norm + 1e-06))
    attn_new = adam_update(attn_w, attn_m, attn_v, attn_ema, attn_shard, clip, rate_mats)
    ffn_new = adam_update(ffn_w, ffn_m, ffn_v, ffn_ema, ffn_shard, clip, rate_mats)
    gains_new = adam_update(gains, gains_m, gains_v, gains_ema, gains_shard, clip, rate_small)
    biases_new = adam_update(biases, biases_m, biases_v, biases_ema, biases_shard, clip, rate_small)
    up_new = adam_update(bias_up, bias_up_m, bias_up_v, bias_up_ema, up_shard, clip, rate_small)
    return (
        outputs[0],
        outputs[1],
        grad_lang,
        grad_vis,
        grad_norm,
        attn_new[0],
        attn_new[1],
        attn_new[2],
        attn_new[3],
        ffn_new[0],
        ffn_new[1],
        ffn_new[2],
        ffn_new[3],
        gains_new[0],
        gains_new[1],
        gains_new[2],
        gains_new[3],
        biases_new[0],
        biases_new[1],
        biases_new[2],
        biases_new[3],
        up_new[0],
        up_new[1],
        up_new[2],
        up_new[3],
    )


def solution(mesh):
    return jax.shard_map(
        local,
        mesh=mesh,
        in_specs=(
            P(("dp", "mp"), None, None),
            P(("dp", "mp"), None, None),
            P(("dp", "mp"), None),
            P(("dp", "mp")),
            P(("dp", "mp"), None, None),
            P(("dp", "mp"), None, None),
            P(None, None, "dp", "mp"),
            P(None, None, "dp", "mp"),
            P(None, None, "dp", "mp"),
            P(None, None, "dp", "mp"),
            P(None, None, "dp", "mp"),
            P(None, None, "dp", "mp"),
            P(None, None, "dp", "mp"),
            P(None, None, "dp", "mp"),
            P(None, "dp"),
            P(None, "dp"),
            P(None, "dp"),
            P(None, "dp"),
            P(None, "dp"),
            P(None, "dp"),
            P(None, "dp"),
            P(None, "dp"),
            P(None, "dp"),
            P(None, "dp"),
            P(None, "dp"),
            P(None, "dp"),
        ),
        out_specs=(
            P(("dp", "mp"), None, None),
            P(("dp", "mp"), None, None),
            P(("dp", "mp"), None, None),
            P(("dp", "mp"), None, None),
            P(),
            P(None, None, "dp", "mp"),
            P(None, None, "dp", "mp"),
            P(None, None, "dp", "mp"),
            P(None, None, "dp", "mp"),
            P(None, None, "dp", "mp"),
            P(None, None, "dp", "mp"),
            P(None, None, "dp", "mp"),
            P(None, None, "dp", "mp"),
            P(None, "dp"),
            P(None, "dp"),
            P(None, "dp"),
            P(None, "dp"),
            P(None, "dp"),
            P(None, "dp"),
            P(None, "dp"),
            P(None, "dp"),
            P(None, "dp"),
            P(None, "dp"),
            P(None, "dp"),
            P(None, "dp"),
        ),
        check_vma=False,
    )
```

profile of v0, /device:TPU:0, one launch (start us, length us, event | category | flops | bytes accessed | tf_op | source)
XLA Modules:
  0.0 1635.1 jit_solution(2634377010804659437)
XLA Ops:
  10.2 43.5 %all-gather = f32[16,48,16]{1,2,0:T(8,128)S(1)} all-gather(f32[1,48,16]{1,2,0:T(8,128)S(1)} %bitcast.370), channel_id=1, replica_groups=mesh['dp'=16,'mp'=2] {'dp'}, dimensions={0}, use_global_device_ids=true | all-gather | bytes 52224 | tf_op jit(solution)/shard_map/all_gather | solution.py:243
  60.1 55.5 %all-gather.14.cloned.1.call-done = bf16[3,4,768,384]{3,2,1,0:T(8,128)(2,1)} async-done(((bf16[3,4,48,384]{3,2,1,0:T(8,128)(2,1)}), bf16[3,4,768,384]{3,2,1,0:T(8,128)(2,1)}) %all-gather.14.cloned.1.call-update) | async-done | bytes 7077904 | tf_op jit(solution)/shard_map/all_gather | solution.py:238
  118.0 7.3 all-gather.12.cloned.1.call-done
  183.8 41.1 %all-gather.1 = f32[16,48,5]{1,2,0:T(8,128)S(1)} all-gather(f32[1,48,5]{1,2,0:T(8,128)S(1)} %bitcast.371), channel_id=1, replica_groups=mesh['dp'=16,'mp'=2] {'dp'}, dimensions={0}, use_global_device_ids=true | all-gather | bytes 16320 | tf_op jit(solution)/shard_map/all_gather | solution.py:242
  308.0 36.5 %all-gather.2 = f32[16,192,2]{1,2,0:T(2,128)S(1)} all-gather(f32[1,192,2]{1,2,0:T(2,128)S(1)} %bitcast.372), channel_id=1, replica_groups=mesh['dp'=16,'mp'=2] {'dp'}, dimensions={0}, use_global_device_ids=true | all-gather | bytes 26112 | tf_op jit(solution)/shard_map/all_gather | solution.py:244
  350.2 43.6 %all-gather.16.cloned.1.call-done = bf16[2,2,768,1536]{3,2,1,0:T(8,128)(2,1)} async-done(((bf16[2,2,48,1536]{3,2,1,0:T(8,128)(2,1)}), bf16[2,2,768,1536]{3,2,1,0:T(8,128)(2,1)}) %all-gather.16.cloned.1.call-update) | async-done | bytes 9437200 | tf_op jit(solution)/shard_map/all_gather | solution.py:239
  393.8 6.3 convert_reduce_fusion.4
  400.1 6.2 reduce-scatter.22.cloned.1.call-done
  411.0 11.0 multiply_convert_fusion.6
  428.2 8.0 convert_reduce_fusion.1
  436.3 18.7 %multiply_convert_fusion = (bf16[32,36,1536]{2,1,0:T(8,128)(2,1)S(1)}, f32[32,36,1536]{2,1,0:T(8,128)}) fusion(f32[32,36,1536]{2,1,0:T(8,128)S(1)} %get-tuple-element.248, f32[1536]{0:T(1024)S(1)} %dynamic-slice_reduce_fusion, u32[36,1536]{1,0:T(8,128)S(1)} %get-tuple-element.126, u32[36,1536]{1,0:T(8,128)S(1)} %get-tuple-element.125), kind=kLoop, calls=%fused_computation.13 | loop fusion | flops 122093568 | bytes 18143232 | tf_op jit(solution)/shard_map/convert_element_type | solution.py:142
  456.9 7.0 fusion.23
  469.8 7.3 reduce-scatter.24.cloned.1.call-done
  491.4 7.0 convert_reduce_fusion.5
  499.7 4.7 fusion.18
  504.7 13.1 convert_reduce_fusion.2
  519.8 6.9 fusion.21
  544.3 5.8 multiply_reduce_fusion.3
  553.1 5.6 multiply_reduce_fusion.5
  598.8 5.0 convert_reduce_fusion.6
  610.0 5.4 multiply_reduce_fusion
  690.8 5.9 convert_reduce_fusion.8
  793.5 11.1 pad_maximum_fusion.1
  804.7 18.7 %copy.438 = f32[3,4,768,384]{3,1,0,2:T(4,128)} copy(f32[3,4,768,384]{2,3,1,0:T(8,128)} %pad_maximum_fusion.1) | data formatting | bytes 28311552 | tf_op jit(solution)/shard_map/stack | solution.py:453
  835.8 5.7 convolution_bitcast_fusion
  841.5 5.5 convolution_bitcast_fusion.1
  847.0 6.7 maximum_bitcast_fusion.1
  853.7 10.5 pad_maximum_fusion
  881.5 398.2 %all-reduce.5.cloned.1.call-done = f32[3,4,768,384]{3,1,0,2:T(4,128)} async-done(((f32[3,4,768,384]{3,1,0,2:T(4,128)}), f32[3,4,768,384]{3,1,0,2:T(4,128)}) %all-reduce.5.cloned.1.call-update) | async-done | bytes 14155792
  1282.0 287.2 %reduce-scatter.38.cloned.1.call-done = f32[2,2,48,1536]{3,2,1,0:T(8,128)} async-done(((f32[2,2,768,1536]{3,2,1,0:T(8,128)}), f32[2,2,48,1536]{3,2,1,0:T(8,128)}) %reduce-scatter.38.cloned.1.call-update) | async-done | bytes 1179664 | tf_op jit(solution)/shard_map/reduce_scatter | solution.py:456
  1574.5 39.4 %psum.31 = f32[]{:T(128)} all-reduce(f32[]{:T(128)S(6)} %add.773), channel_id=1, replica_groups=mesh['dp'=16,'mp'=2] {'dp','mp'}, use_global_device_ids=true, to_apply=%region_86.87 | all-reduce | flops 1 | bytes 8 | tf_op jit(solution)/shard_map/psum | solution.py:471
  1618.9 4.8 add_multiply_fusion.3
  (801 shorter events, 472.6 us)
Async XLA Ops:
  7.2 108.3 %all-gather.14.cloned.1.call-start = ((), (), s32[]{:S(2)}) async-start(), calls=%async_computation.14 | async-start | bytes 7520256 | tf_op jit(solution)/shard_map/all_gather | solution.py:238
  9.3 116.1 %all-gather.12.cloned.1.call-start = ((), (), s32[]{:S(2)}) async-start(), calls=%async_computation.13 | async-start | bytes 2654208 | tf_op jit(solution)/shard_map/all_gather | solution.py:261
  10.1 216.2 %reduce-scatter.14.cloned.1.call-start = ((), (), s32[]{:S(2)}) async-start(), calls=%async_computation.15 | async-start | bytes 2949120 | tf_op jit(solution)/shard_map/reduce_scatter | solution.py:172
  154.1 80.9 %reduce-scatter.20.cloned.1.call-start = ((), (), s32[]{:S(2)}) async-start(), calls=%async_computation.19 | async-start | bytes 5898240 | tf_op jit(solution)/shard_map/reduce_scatter | solution.py:173
  183.1 79.8 %all-gather.18.cloned.1.call-start = ((), (), s32[]{:S(2)}) async-start(), calls=%async_computation.20 | async-start | bytes 2654208 | tf_op jit(solution)/shard_map/all_gather | solution.py:166
  226.2 454.4 %copy-start.120 = (f32[768]{0:T(1024)}, f32[768]{0:T(1024)S(1)}, u32[]{:S(2)}) copy-start(f32[768]{0:T(1024)S(1)} %get-tuple-element.167) | copy-start | bytes 9220
  227.7 433.3 %copy-start.7 = (f32[16,20,768]{2,0,1:T(8,128)}, f32[16,20,768]{2,0,1:T(8,128)S(1)}, u32[]{:S(2)}) copy-start(f32[16,20,768]{2,0,1:T(8,128)S(1)} %get-tuple-element.219) | copy-start | bytes 2949124
  227.7 433.3 %copy-start.104 = (f32[16,20]{0,1:T(8,128)}, f32[16,20]{0,1:T(8,128)S(1)}, u32[]{:S(2)}) copy-start(f32[16,20]{0,1:T(8,128)S(1)} %broadcast_multiply_fusion.10) | copy-start | bytes 3844
  237.2 443.4 %copy-start = (f32[16,36,768]{2,1,0:T(8,128)}, f32[16,36,768]{2,1,0:T(8,128)S(1)}, u32[]{:S(2)}) copy-start(f32[16,36,768]{2,1,0:T(8,128)S(1)} %get-tuple-element.211) | copy-start | bytes 5308420
  239.1 105.6 %reduce-scatter.16.cloned.1.call-start = ((), (), s32[]{:S(2)}) async-start(), calls=%async_computation.16 | async-start | bytes 2949120 | tf_op jit(solution)/shard_map/reduce_scatter | solution.py:172
  260.6 133.2 %all-gather.16.cloned.1.call-start = ((), (), s32[]{:S(2)}) async-start(), calls=%async_computation.17 | async-start | bytes 10027008 | tf_op jit(solution)/shard_map/all_gather | solution.py:239
  262.8 143.4 %reduce-scatter.22.cloned.1.call-start = ((), (), s32[]{:S(2)}) async-start(), calls=%async_computation.21 | async-start | bytes 5898240 | tf_op jit(solution)/shard_map/reduce_scatter | solution.py:173
  307.3 120.9 %all-gather.20.cloned.1.call-start = ((), (), s32[]{:S(2)}) async-start(), calls=%async_computation.22 | async-start | bytes 2654208 | tf_op jit(solution)/shard_map/all_gather | solution.py:166
  410.9 53.8 %reduce-scatter.18.cloned.1.call-start = ((), (), s32[]{:S(2)}) async-start(), calls=%async_computation.18 | async-start | bytes 2949120 | tf_op jit(solution)/shard_map/reduce_scatter | solution.py:172
  427.9 49.2 %reduce-scatter.24.cloned.1.call-start = ((), (), s32[]{:S(2)}) async-start(), calls=%async_computation.23 | async-start | bytes 5898240 | tf_op jit(solution)/shard_map/reduce_scatter | solution.py:173
  463.9 40.8 %all-gather.22.cloned.1.call-start = ((), (), s32[]{:S(2)}) async-start(), calls=%async_computation.26 | async-start | bytes 2654208 | tf_op jit(solution)/shard_map/all_gather | solution.py:180
  486.6 43.5 %reduce-scatter.26.cloned.1.call-start = ((), (), s32[]{:S(2)}) async-start(), calls=%async_computation.24 | async-start | bytes 2949120 | tf_op jit(solution)/shard_map/reduce_scatter | solution.py:186
  504.5 48.6 %reduce-scatter.30.cloned.1.call-start = ((), (), s32[]{:S(2)}) async-start(), calls=%async_computation.27 | async-start | bytes 5898240 | tf_op jit(solution)/shard_map/reduce_scatter | solution.py:187
  526.8 63.9 %all-gather.24.cloned.1.call-start = ((), (), s32[]{:S(2)}) async-start(), calls=%async_computation.28 | async-start | bytes 2654208 | tf_op jit(solution)/shard_map/all_gather | solution.py:180
  561.1 96.5 %reduce-scatter.28.cloned.1.call-start = ((), (), s32[]{:S(2)}) async-start(), calls=%async_computation.25 | async-start | bytes 2949120 | tf_op jit(solution)/shard_map/reduce_scatter | solution.py:186
  590.1 86.3 %reduce-scatter.32.cloned.1.call-start = ((), (), s32[]{:S(2)}) async-start(), calls=%async_computation.29 | async-start | bytes 5898240 | tf_op jit(solution)/shard_map/reduce_scatter | solution.py:187
  644.7 56.4 %all-gather.26.cloned.1.call-start = ((), (), s32[]{:S(2)}) async-start(), calls=%async_computation.30 | async-start | bytes 2654208 | tf_op jit(solution)/shard_map/all_gather | solution.py:180
  683.1 184.8 %all-reduce.7.cloned.1.call-start = ((), (), s32[]{:S(2)}) async-start(), calls=%async_computation.35 | async-start | bytes 196608 | tf_op jit(solution)/shard_map/psum | solution.py:458
  726.2 148.0 %reduce-scatter.34.cloned.1.call-start = ((), (), s32[]{:S(2)}) async-start(), calls=%async_computation.31 | async-start | bytes 2949120 | tf_op jit(solution)/shard_map/reduce_scatter | solution.py:186
  731.3 146.1 %reduce-scatter.36.cloned.1.call-start = ((), (), s32[]{:S(2)}) async-start(), calls=%async_computation.32 | async-start | bytes 5898240 | tf_op jit(solution)/shard_map/reduce_scatter | solution.py:187
  766.8 512.8 %all-reduce.5.cloned.1.call-start = ((), (), s32[]{:S(2)}) async-start(), calls=%async_computation.34 | async-start | bytes 28311552
  823.4 745.9 %reduce-scatter.38.cloned.1.call-start = ((), (), s32[]{:S(2)}) async-start(), calls=%async_computation.33 | async-start | bytes 20054016 | tf_op jit(solution)/shard_map/reduce_scatter | solution.py:456
  881.5 691.3 %copy-start.42 = (f32[16,36,768]{2,1,0:T(8,128)S(1)}, f32[16,36,768]{2,1,0:T(8,128)}, u32[]{:S(2)}) copy-start(f32[16,36,768]{2,1,0:T(8,128)} %fusion.161) | copy-start | bytes 5308420
  1281.9 335.5 %copy-start.191 = (f32[5,48]{1,0:T(8,128)S(1)}, f32[5,48]{1,0:T(8,128)}, u32[]{:S(2)}) copy-start(f32[5,48]{1,0:T(8,128)} %param.40) | copy-start | bytes 2884
  1282.0 335.5 %copy-start.210 = (f32[5,48]{1,0:T(8,128)S(1)}, f32[5,48]{1,0:T(8,128)}, u32[]{:S(2)}) copy-start(f32[5,48]{1,0:T(8,128)} %param.43) | copy-start | bytes 2884
  1282.0 335.5 %copy-start.211 = (f32[5,48]{1,0:T(8,128)S(1)}, f32[5,48]{1,0:T(8,128)}, u32[]{:S(2)}) copy-start(f32[5,48]{1,0:T(8,128)} %param.41) | copy-start | bytes 2884
  1282.0 335.5 %copy-start.212 = (f32[5,48]{1,0:T(8,128)S(1)}, f32[5,48]{1,0:T(8,128)}, u32[]{:S(2)}) copy-start(f32[5,48]{1,0:T(8,128)} %param.42) | copy-start | bytes 2884
  (221 other events, 5746.6 us)
Sparse Core Ops, SparseCore 0:
  11.3 104.2 all-gather.13
  117.1 8.2 all-gather.11
  154.2 10.6 reduce-scatter.13
  183.2 12.9 reduce-scatter.19
  239.2 5.9 all-gather.17
  260.7 5.3 reduce-scatter.15
  269.8 123.9 all-gather.15
  396.1 10.0 reduce-scatter.21
  411.0 11.2 all-gather.19
  428.0 10.6 reduce-scatter.17
  464.0 13.0 reduce-scatter.23
  486.7 11.2 all-gather.21
  504.6 10.5 reduce-scatter.25
  526.9 12.9 reduce-scatter.29
  561.3 11.2 all-gather.23
  590.2 10.5 reduce-scatter.27
  644.8 12.9 reduce-scatter.31
  683.2 11.1 all-gather.25
  726.3 123.0 all-reduce.6
  851.5 10.3 reduce-scatter.33
  864.3 13.0 reduce-scatter.35
  883.8 395.7 all-reduce.4
  1285.4 283.7 reduce-scatter.37
where the time goes:
time: 1650 us; the launch traced here: 1640 us
  waiting for transfers between devices  807 us (49%)
  matrix products  268 us (16%)
  local copies, waits for them, and re-layouts  188 us (11%)
  blocking collectives  180 us (11%)
  other arithmetic  166 us (10%)
  between operations  23.2 us (1%)
    unnamed x24, waiting for transfers between devices  399 us
    reduce_scatter x1, waiting for transfers between devices, local(): lax.psum_scatter(ffn_grad, 'dp', scatter_dimension=2, tiled=True)  287 us
    all_gather x1, waiting for transfers between devices, local(): lax.all_gather(attn_w.astype(jnp.bfloat16), 'dp', axis=2, tiled=True)  55.5 us
    all_gather x1, waiting for transfers between devices, local(): lax.all_gather(ffn_w.astype(jnp.bfloat16), 'dp', axis=2, tiled=True)  43.6 us
    all_gather x1, blocking collectives, local(): lax.all_gather(biases, 'dp', axis=1, tiled=True)  43.5 us
    all_gather x1, blocking collectives, local(): lax.all_gather(gains, 'dp', axis=1, tiled=True)  41.1 us
    reshape x16, local copies, waits for them, and re-layouts, split_heads(): values.reshape(values.shape[0], values.shape[1], values.shape[2] // HEAD_...  40.8 us
    psum x1, blocking collectives, local(): grad_norm = jnp.sqrt(lax.psum(squares, ('dp', 'mp')))  39.4 us
  transfers between devices with their start and end apart: 23, of which 8 were waited for; matrix products, arithmetic and copies ran while one was open for 30% of the time, Pallas kernels for 0%

commit v1 on v0

v1 whole, which is shorter than its diff:
```python
import functools
import math
import jax
import jax.numpy as jnp
from jax import lax
from jax.experimental import pallas as pl
from jax.experimental.pallas import tpu as pltpu
from jax.sharding import PartitionSpec as P

HEAD_DIM = 64
STEP = 7


norm_eps = 1e-12
mask_fill = -1000000000.0
beta_one = 0.5
beta_two = 0.6
ema_decay = 0.5
adam_eps = 1e-08
weight_decay = 0.01
rate_mats = 0.02
rate_small = 0.2
clip_norm = 1.0

GROUP = 4
low = jnp.bfloat16
LINE = 4
CHIPS = 16
PAIR = 2 * HEAD_DIM
TILE = 256
CHUNK = 32
FEED = 512
FEED_ROWS = 64
SQRT_HALF = 0.5**0.5
BELL = (2.0 * math.pi) ** -0.5


def moves(target):
    pairs = []
    for z in range(LINE):
        for y in range(2):
            for x in range(2):
                there = target(z, y, x)
                pairs.append((z * 4 + y * 2 + x, there[0] * 4 + there[1] * 2 + there[2]))
    return pairs


routes = {
    1: moves(lambda z, y, x: (z, y, 1 - x)),
    2: moves(lambda z, y, x: (z, 1 - y, x)),
    4: moves(lambda z, y, x: (z ^ 1, y, x)),
    8: moves(lambda z, y, x: (z ^ 2, y, x)),
}


def send(values, bit):
    return lax.ppermute(values, "dp", routes[bit])


def swap_cores(values):
    return lax.ppermute(values, "mp", [(0, 1), (1, 0)])


def widen(values):
    return values.astype(jnp.float32)


def pick(values, axis, index):
    return lax.dynamic_index_in_dim(values, index, axis, keepdims=False)


def bit_of(bit):
    return (lax.axis_index("dp") // bit) % 2


def after(values, *others):
    return lax.optimization_barrier((values,) + others)[0]


def assemble_kernel(places, spans, place_ref, *refs):
    pieces, wholes, sem = refs[: len(places)], refs[len(places) : -1], refs[-1]
    chip, core = place_ref[0], place_ref[1]
    rows, columns = pieces[0].shape[2], pieces[0].shape[3]
    copies = []
    for piece, (offsets, other) in zip(pieces, places):
        for number, offset in enumerate(offsets):
            row = pl.ds(pl.multiple_of((chip ^ offset) * rows, 16), rows)
            column = pl.ds(pl.multiple_of((core ^ other) * columns, 128), columns)
            for whole, (start, count) in zip(wholes, spans):
                copies.append(
                    pltpu.make_async_copy(
                        piece.at[number, pl.ds(start, count)], whole.at[:, row, column], sem
                    )
                )
    for copy in copies:
        copy.start()
    for copy in copies:
        copy.wait()


def assemble(pieces, places, spans):
    _, _, rows, columns = pieces[0].shape
    place = jnp.stack([lax.axis_index("dp"), lax.axis_index("mp")]).astype(jnp.int32)
    return pl.pallas_call(
        functools.partial(assemble_kernel, places, spans),
        out_shape=[shape_of((count, rows * CHIPS, columns * 2), low) for _, count in spans],
        in_specs=[pl.BlockSpec(memory_space=pltpu.SMEM)]
        + [pl.BlockSpec(memory_space=pl.ANY)] * len(pieces),
        out_specs=vmem(len(spans)),
        scratch_shapes=[pltpu.SemaphoreType.DMA],
        compiler_params=params_of(24),
        cost_estimate=cost_of(3),
        name="assemble",
    )(place, *pieces)


def gather_mats(own, order, spans):
    if lax.axis_size("dp") != CHIPS:
        whole = lax.all_gather(own, "dp", axis=1, tiled=True)
        whole = lax.all_gather(whole, "mp", axis=2, tiled=True)
        return [whole[start : start + count] for start, count in spans]
    values, offsets = own[None], [0]
    for bit in order[:-1]:
        values = jnp.concatenate([values, send(values, bit)])
        offsets = offsets + [offset ^ bit for offset in offsets]
    last = send(values, order[-1])
    far = [offset ^ order[-1] for offset in offsets]
    pieces = [values, swap_cores(values), last, swap_cores(last)]
    places = [(offsets, 0), (offsets, 1), (far, 0), (far, 1)]
    return assemble(pieces, places, spans)


class Scatter:
    def __init__(self, mine, other, order):
        self.staged = lax.axis_size("dp") == CHIPS
        self.parts = widen(mine) + widen(swap_cores(other))
        self.order = list(order)
        self.left = [8, 4, 2, 1]
        if self.staged:
            count, width, columns = self.parts.shape
            self.parts = self.parts.astype(low)
            self.parts = self.parts.reshape(count, 2, 2, 2, 2, width // CHIPS, columns)

    def step(self, times=1):
        for _ in range(times if self.staged else 0):
            bit = self.order.pop(0)
            axis = 1 + self.left.index(bit)
            self.left.remove(bit)
            kept = pick(self.parts, axis, bit_of(bit))
            arrived = send(pick(self.parts, axis, 1 - bit_of(bit)), bit)
            self.parts = widen(kept) + widen(arrived)
            if self.left:
                self.parts = self.parts.astype(low)
        return self.parts

    def finish(self):
        if self.staged:
            return self.step(len(self.order))
        return lax.psum_scatter(self.parts, "dp", scatter_dimension=1, tiled=True)


def gather_small(values):
    if lax.axis_size("dp") != CHIPS:
        return lax.all_gather(values, "dp", axis=0, tiled=False)
    values = values[None]
    for bit in (1, 2, 4, 8):
        there = send(values, bit)
        at_zero = bit_of(bit) == 0
        values = jnp.concatenate(
            [jnp.where(at_zero, values, there), jnp.where(at_zero, there, values)]
        )
    return values


def scatter_small(values):
    values = values + swap_cores(values)
    if lax.axis_size("dp") != CHIPS:
        return lax.psum_scatter(values, "dp", scatter_dimension=0, tiled=True)[0]
    for bit in (8, 4, 2, 1):
        half = values.shape[0] // 2
        at_zero = bit_of(bit) == 0
        kept = jnp.where(at_zero, values[:half], values[half:])
        sent = jnp.where(at_zero, values[half:], values[:half])
        values = kept + send(sent, bit)
    return values[0]


def sum_all(value):
    if lax.axis_size("dp") != CHIPS:
        return lax.psum(value, ("dp", "mp"))
    value = value.reshape(1, 1)
    value = value + swap_cores(value)
    for bit in (1, 2, 4, 8):
        value = value + send(value, bit)
    return value[0, 0]


def dot_nn(left, right):
    return lax.dot_general(left, right, (((1,), (0,)), ((), ())), preferred_element_type=jnp.float32)


def dot_nt(left, right):
    return lax.dot_general(left, right, (((1,), (1,)), ((), ())), preferred_element_type=jnp.float32)


def dot_tn(left, right):
    return lax.dot_general(left, right, (((0,), (0,)), ((), ())), preferred_element_type=jnp.float32)


def fold_rows(values):
    return jnp.sum(values.reshape(values.shape[0] // 8, 8, values.shape[1]), axis=0)


def close_rows(values):
    return jnp.sum(values, axis=0, keepdims=True)


def norm_rows(summed, gain, shift):
    average = jnp.mean(summed, axis=-1, keepdims=True)
    centered = summed - average
    inverse = lax.rsqrt(jnp.mean(centered * centered, axis=-1, keepdims=True) + norm_eps)
    normed = centered * inverse
    return normed * gain + shift, normed, inverse


def norm_rows_back(grad_out, normed, inverse, gain):
    scaled = grad_out * gain
    return inverse * (
        scaled
        - jnp.mean(scaled, axis=-1, keepdims=True)
        - normed * jnp.mean(scaled * normed, axis=-1, keepdims=True)
    )


def stack_heads(block):
    first = lax.broadcasted_iota(jnp.int32, block.shape, 1) < HEAD_DIM
    nothing = jnp.zeros_like(block)
    return jnp.concatenate(
        [jnp.where(first, block, nothing), jnp.where(first, nothing, block)], axis=0
    )


def merge_heads(double):
    rows = double.shape[0] // 2
    first = lax.broadcasted_iota(jnp.int32, (rows, double.shape[1]), 1) < HEAD_DIM
    return jnp.where(first, double[:rows], double[rows:])


def pair_forward(queries, keys, values, bias):
    count = keys.shape[0]
    scores = dot_nt(stack_heads(keys), queries) * HEAD_DIM ** (-0.5)
    weights, totals = [], []
    for part in (scores[:count] + bias, scores[count:] + bias):
        top = jnp.max(part, axis=0, keepdims=True)
        powers = jnp.exp(part - top)
        total = jnp.sum(powers, axis=0, keepdims=True)
        weights.append((powers * (1.0 / total)).astype(low))
        totals.append(top + jnp.log(total))
    context = dot_tn(jnp.concatenate(weights, axis=0), stack_heads(values))
    return context.astype(low), totals


def pair_backward(queries, keys, values, grad, bias, totals):
    count = keys.shape[0]
    both_keys = stack_heads(keys)
    scores = dot_nt(both_keys, queries) * HEAD_DIM ** (-0.5)
    sensed = dot_nt(stack_heads(values), grad)
    weights, slopes = [], []
    for part, sense, total in (
        (scores[:count], sensed[:count], totals[0]),
        (scores[count:], sensed[count:], totals[1]),
    ):
        weight = jnp.exp(part + bias - total)
        inner = jnp.sum(sense * weight, axis=0, keepdims=True)
        weights.append(weight.astype(low))
        slopes.append((weight * (sense - inner)).astype(low))
    weights = jnp.concatenate(weights, axis=0)
    slopes = jnp.concatenate(slopes, axis=0)
    grad_queries = (dot_tn(slopes, both_keys) * HEAD_DIM ** (-0.5)).astype(low)
    grad_keys = (merge_heads(dot_nn(slopes, queries)) * HEAD_DIM ** (-0.5)).astype(low)
    grad_values = merge_heads(dot_nn(weights, grad)).astype(low)
    return grad_queries, grad_keys, grad_values


def tiles_of(width):
    return [(at, min(TILE, width - at)) for at in range(0, width, TILE)]


def row_block(start, size, step):
    return pl.ds(pl.multiple_of(start + step * size, 16), size)


def attend_front(plan, *refs):
    streams, relations, cross = plan["streams"], plan["relations"], plan["cross"]
    refs = list(refs)

    def take(count):
        taken = refs[:count]
        del refs[:count]
        return taken

    (x_ref,) = take(1)
    before = [] if cross else take(1)
    mats = take(plan["mats"])
    gain_ref, bias_ref, key_ref = take(3)
    same = take(len(relations))
    q_ref, k_ref, v_ref, ctx_ref = take(4)
    logs = take(len(relations))
    normed = take(len(streams))
    inverse = take(len(streams))
    lowered = take(len(streams))
    (acc_ref,) = take(1)
    width = x_ref.shape[1]
    weights = [mats[i // (4 // len(mats))].at[i % (4 // len(mats))] for i in range(4)]
    rows = x_ref[...]
    for target, weight, row in ((q_ref, 0, 0), (k_ref, 1, None), (v_ref, 2, 1)):
        for at, size in tiles_of(width):
            part = dot_nn(rows, weights[weight][:, at : at + size])
            if row is not None:
                line = plan["rows"][row]
                part = part + bias_ref[line : line + 1, at : at + size]
            target[:, at : at + size] = part.astype(low)
    pairs = width // PAIR
    groups = plan["groups"]

    def one_group(group, carry):
        for which, (asking, asked) in enumerate(relations):
            ask = row_block(*streams[asking], group)
            key = row_block(*streams[asked], group)
            bias = same[which][...] + key_ref[key, :]
            for pair in range(pairs):
                lanes = slice(pair * PAIR, (pair + 1) * PAIR)
                context, totals = pair_forward(
                    q_ref[ask, lanes], k_ref[key, lanes], v_ref[key, lanes], bias
                )
                ctx_ref[ask, lanes] = context
                for side in range(2):
                    logs[which][group * (2 * pairs) + 2 * pair + side] = totals[side]
        return carry

    lax.fori_loop(0, groups, one_group, 0)
    context = ctx_ref[...]
    for at, size in tiles_of(width):
        acc_ref[:, at : at + size] = dot_nt(context, weights[3][at : at + size, :])
    gain = gain_ref[plan["gain"] : plan["gain"] + 1, :]
    shift = bias_ref[plan["shift"] : plan["shift"] + 1, :]
    out_bias = bias_ref[plan["rows"][2] : plan["rows"][2] + 1, :]
    for index, (start, size) in enumerate(streams):

        def one_chunk(step, carry, start=start, index=index):
            here = row_block(start, CHUNK, step)
            there = row_block(0, CHUNK, step)
            if cross:
                base = widen(x_ref[here, :])
            else:
                last_gain, last_shift = plan["before"]
                base = (
                    before[0][here, :] * gain_ref[last_gain : last_gain + 1, :]
                    + bias_ref[last_shift : last_shift + 1, :]
                )
            value, unit, scale = norm_rows(base + acc_ref[here, :] + out_bias, gain, shift)
            normed[index][there, :] = unit
            inverse[index][there, :] = scale
            lowered[index][there, :] = value.astype(low)
            return carry

        lax.fori_loop(0, size * groups // CHUNK, one_chunk, 0)


def attend_back(plan, *refs):
    streams, relations = plan["streams"], plan["relations"]
    refs = list(refs)

    def take(count):
        taken = refs[:count]
        del refs[:count]
        return taken

    (core_ref,) = take(1)
    carried = [take(plan["carried"]) for _ in streams]
    normed = take(len(streams))
    inverse = take(len(streams))
    (x_ref,) = take(1)
    mats = take(plan["mats"])
    gain_ref, key_ref = take(2)
    same = take(len(relations))
    q_ref, k_ref, v_ref, ctx_ref = take(4)
    logs = take(len(relations))
    grad_in = take(len(streams))
    mine = take(plan["mats"])
    other = take(plan["mats"])
    (small_ref,) = take(1)
    do_ref, dctx_ref, dq_ref, dk_ref, dv_ref = take(5)
    width = x_ref.shape[1]
    half = width // 2
    each = 4 // plan["mats"]
    weights = [mats[i // each].at[i % each] for i in range(4)]
    gain = gain_ref[plan["gain"] : plan["gain"] + 1, :]
    groups = plan["groups"]
    nothing = jnp.zeros((8, width), jnp.float32)
    sums = (nothing, nothing, nothing)
    for index, (start, size) in enumerate(streams):

        def one_chunk(step, sums, start=start, index=index):
            here = row_block(start, CHUNK, step)
            there = row_block(0, CHUNK, step)
            grad = carried[index][0][there, :]
            for more in carried[index][1:]:
                grad = grad + more[there, :]
            unit = normed[index][there, :]
            down = norm_rows_back(grad, unit, inverse[index][there, :], gain)
            sent = down.astype(low)
            grad_in[index][there, :] = down
            do_ref[here, :] = sent
            return (
                sums[0] + fold_rows(grad * unit),
                sums[1] + fold_rows(grad),
                sums[2] + fold_rows(widen(sent)),
            )

        sums = lax.fori_loop(0, size * groups // CHUNK, one_chunk, sums)
    sent = do_ref[...]
    for at, size in tiles_of(width):
        dctx_ref[:, at : at + size] = dot_nn(sent, weights[3][:, at : at + size]).astype(low)
    pairs = width // PAIR

    def one_group(group, carry):
        for which, (asking, asked) in enumerate(relations):
            ask = row_block(*streams[asking], group)
            key = row_block(*streams[asked], group)
            bias = same[which][...] + key_ref[key, :]
            for pair in range(pairs):
                lanes = slice(pair * PAIR, (pair + 1) * PAIR)
                base = group * (2 * pairs) + 2 * pair
                grads = pair_backward(
                    q_ref[ask, lanes],
                    k_ref[key, lanes],
                    v_ref[key, lanes],
                    dctx_ref[ask, lanes],
                    bias,
                    [logs[which][base], logs[which][base + 1]],
                )
                dq_ref[ask, lanes], dk_ref[key, lanes], dv_ref[key, lanes] = grads
        return carry

    lax.fori_loop(0, groups, one_group, 0)
    at_zero = core_ref[0] == 0
    rows = x_ref[...]
    context = ctx_ref[...]
    for number, (left, right) in enumerate(
        ((rows, dq_ref), (rows, dk_ref), (rows, dv_ref), (sent, ctx_ref))
    ):
        wide = right[...]
        for at, size in tiles_of(width):
            whole = dot_tn(left[:, at : at + size], wide).astype(low)
            former, latter = whole[:, :half], whole[:, half:]
            mine[number // each][number % each, at : at + size, :] = jnp.where(
                at_zero, former, latter
            )
            other[number // each][number % each, at : at + size, :] = jnp.where(
                at_zero, latter, former
            )
    for index, (start, size) in enumerate(streams):
        span = slice(start, start + size * groups)
        for at, wide in tiles_of(width):
            grad_in[index][:, at : at + wide] += (
                dot_nt(dq_ref[span, :], weights[0][at : at + wide, :])
                + dot_nt(dk_ref[span, :], weights[1][at : at + wide, :])
                + dot_nt(dv_ref[span, :], weights[2][at : at + wide, :])
            )

    def add_chunk(step, sums):
        here = row_block(0, CHUNK, step)
        return (
            sums[0] + fold_rows(widen(dq_ref[here, :])),
            sums[1] + fold_rows(widen(dv_ref[here, :])),
        )

    more = lax.fori_loop(0, x_ref.shape[0] // CHUNK, add_chunk, (nothing, nothing))
    small_ref[...] = jnp.concatenate(
        [close_rows(part) for part in sums + more] + [jnp.zeros((3, width), jnp.float32)], axis=0
    )


def vmem(count):
    return [pl.BlockSpec(memory_space=pltpu.VMEM)] * count


def shape_of(shape, kind):
    return jax.ShapeDtypeStruct(tuple(shape), kind)


def cost_of(micros):
    return pl.CostEstimate(flops=int(micros * 1.15e9), bytes_accessed=1 << 20, transcendentals=0)


def params_of(mib):
    return pltpu.CompilerParams(vmem_limit_bytes=mib << 20)


def layer_plan(layer, sizes, groups, mats):
    if layer == 0:
        starts = (0, sizes[0] * groups)
        streams = [(starts[i], sizes[i]) for i in range(2)]
        relations, gain, shift = [(0, 1), (1, 0)], 0, 11
    else:
        streams, relations = [(0, sizes[0])], [(0, 0)]
        gain, shift = layer, 11 + layer
    return {
        "streams": streams,
        "relations": relations,
        "cross": layer == 0,
        "mats": mats,
        "groups": groups,
        "gain": gain,
        "shift": shift,
        "rows": [3 * layer, 3 * layer + 1, 3 * layer + 2],
        "before": (0, 11),
        "carried": 1 if layer == 0 else 2,
    }


def run_front(plan, x, before, mats, gains, biases, key_bias, same):
    rows, width = x.shape
    groups = plan["groups"]
    outs = [shape_of((rows, width), low)] * 4
    for asking, _ in plan["relations"]:
        outs.append(
            shape_of((groups * width // HEAD_DIM, 1, plan["streams"][asking][1]), jnp.float32)
        )
    counts = [size * groups for _, size in plan["streams"]]
    outs += [shape_of((count, width), jnp.float32) for count in counts]
    outs += [shape_of((count, 1), jnp.float32) for count in counts]
    outs += [shape_of((count, width), low) for count in counts]
    args = [x] + ([] if before is None else [before]) + list(mats) + [gains, biases, key_bias]
    args += list(same)
    results = pl.pallas_call(
        functools.partial(attend_front, plan),
        out_shape=outs,
        in_specs=vmem(len(args)),
        out_specs=vmem(len(outs)),
        scratch_shapes=[pltpu.VMEM((rows, width), jnp.float32)],
        compiler_params=params_of(48),
        cost_estimate=cost_of(0.028 * rows),
        name="attend_front",
    )(*args)
    related, many = len(plan["relations"]), len(counts)
    kept = results[: 4 + related]
    rest = results[4 + related :]
    return kept, rest[:many], rest[many : 2 * many], rest[2 * many :]


def run_back(plan, core, carried, normed, inverse, x, mats, gains, key_bias, same, kept):
    rows, width = x.shape
    counts = [size * plan["groups"] for _, size in plan["streams"]]
    grads = [shape_of(mat.shape[:2] + (width // 2,), low) for mat in mats]
    outs = [shape_of((count, width), jnp.float32) for count in counts] + grads + grads
    outs.append(shape_of((8, width), jnp.float32))
    args = [part for parts in carried for part in parts] + list(normed) + list(inverse) + [x]
    args += list(mats) + [gains, key_bias] + list(same) + list(kept)
    results = pl.pallas_call(
        functools.partial(attend_back, plan),
        out_shape=outs,
        in_specs=[pl.BlockSpec(memory_space=pltpu.SMEM)] + vmem(len(args)),
        out_specs=vmem(len(outs)),
        scratch_shapes=[pltpu.VMEM((rows, width), low)] * 5,
        compiler_params=params_of(56),
        name="attend_back",
    )(core, *args)
    many, count = len(counts), len(mats)
    return (
        results[:many],
        results[many : many + count],
        results[many + count : many + 2 * count],
        results[-1],
    )


def feed_up(line, x_ref, mat_ref, bias_ref, h_ref, slope_ref):
    bias = bias_ref[line : line + 1, :]
    weight = mat_ref[0]
    rows = x_ref.shape[0]
    block = min(FEED_ROWS, rows)

    def one_chunk(step, carry):
        here = row_block(0, block, step)
        hidden = dot_nn(x_ref[here, :], weight) + bias
        share = 0.5 + 0.5 * lax.erf(hidden * SQRT_HALF)
        h_ref[here, :] = (hidden * share).astype(low)
        slope_ref[here, :] = (share + hidden * (jnp.exp(hidden * hidden * -0.5) * BELL)).astype(low)
        return carry

    lax.fori_loop(0, rows // block, one_chunk, 0)


def feed_down(plan, h_ref, mat_ref, gain_ref, bias_ref, unit_ref, cot_ref, live_ref, *refs):
    out_ref, du_ref, do_ref, small_ref, acc_ref = refs
    step = pl.program_id(0)
    width = out_ref.shape[1]

    @pl.when(step == 0)
    def _():
        acc_ref[...] = jnp.zeros_like(acc_ref)

    rows = h_ref[...]
    for at, size in tiles_of(width):
        acc_ref[:, at : at + size] += dot_nt(rows, mat_ref[0, at : at + size, :])

    @pl.when(step == pl.num_programs(0) - 1)
    def _():
        def line(ref, row):
            return ref[row : row + 1, :]

        stream = plan
        last_gain, last_shift = line(gain_ref, 1 + stream), line(bias_ref, 12 + stream)
        gain, shift = line(gain_ref, 3 + stream), line(bias_ref, 14 + stream)
        out_bias = line(bias_ref, 9 + stream)
        nothing = jnp.zeros((8, width), jnp.float32)

        def one_chunk(chunk, sums):
            here = row_block(0, CHUNK, chunk)
            live = live_ref[here, :]
            base = unit_ref[here, :] * last_gain + last_shift
            value, unit, scale = norm_rows(base + acc_ref[here, :] + out_bias, gain, shift)
            out_ref[here, :] = value * live
            grad = widen(cot_ref[here, :]) * live
            down = norm_rows_back(grad, unit, scale, gain)
            sent = down.astype(low)
            du_ref[here, :] = down
            do_ref[here, :] = sent
            return (
                sums[0] + fold_rows(grad * unit),
                sums[1] + fold_rows(grad),
                sums[2] + fold_rows(widen(sent)),
            )

        sums = lax.fori_loop(0, out_ref.shape[0] // CHUNK, one_chunk, (nothing,) * 3)
        small_ref[...] = jnp.concatenate(
            [close_rows(part) for part in sums] + [jnp.zeros((5, width), jnp.float32)], axis=0
        )


def feed_back(core_ref, do_ref, x_ref, h_ref, slope_ref, up_ref, down_ref, *refs):
    dx_ref, mine, other, line_ref = refs
    step = pl.program_id(0)
    sent = do_ref[...]
    rows = x_ref[...]
    slope = (dot_nn(sent, down_ref[0]) * widen(slope_ref[...])).astype(low)
    line_ref[...] = jnp.broadcast_to(
        close_rows(fold_rows(widen(slope))), line_ref.shape
    )
    grad_up = dot_tn(rows, slope).astype(low)
    grad_down = dot_tn(sent, h_ref[...]).astype(low)
    part = dot_nt(slope, up_ref[0])

    @pl.when(step == 0)
    def _():
        dx_ref[...] = part

    @pl.when(step > 0)
    def _():
        dx_ref[...] += part

    @pl.when(step < pl.num_programs(0) // 2)
    def _():
        other[0] = grad_up
        other[1] = grad_down

    @pl.when(step >= pl.num_programs(0) // 2)
    def _():
        mine[0] = grad_up
        mine[1] = grad_down


def run_up(stream, x, mat, biases):
    rows, width = x.shape
    hidden = mat.shape[2]
    wide = lambda step: (0, step)
    return pl.pallas_call(
        functools.partial(feed_up, stream),
        grid=(hidden // FEED,),
        out_shape=[shape_of((rows, hidden), low)] * 2,
        in_specs=[
            pl.BlockSpec((rows, width), lambda step: (0, 0)),
            pl.BlockSpec((1, width, FEED), lambda step: (0, 0, step)),
            pl.BlockSpec((2, FEED), wide),
        ],
        out_specs=[pl.BlockSpec((rows, FEED), wide)] * 2,
        compiler_params=params_of(32),
        cost_estimate=cost_of(0.033 * rows),
        name="feed_up",
    )(x, mat, biases)


def run_down(stream, h, mat, gains, biases, unit, cot, live):
    rows, hidden = h.shape
    width = unit.shape[1]
    fixed = lambda step: (0, 0)

    def whole(array):
        return pl.BlockSpec(array.shape, fixed)

    outs = [
        shape_of((rows, width), jnp.float32),
        shape_of((rows, width), jnp.float32),
        shape_of((rows, width), low),
        shape_of((8, width), jnp.float32),
    ]
    return pl.pallas_call(
        functools.partial(feed_down, stream),
        grid=(hidden // FEED,),
        out_shape=outs,
        in_specs=[
            pl.BlockSpec((rows, FEED), lambda step: (0, step)),
            pl.BlockSpec((1, width, FEED), lambda step: (0, 0, step)),
            whole(gains),
            whole(biases),
            whole(unit),
            whole(cot),
            whole(live),
        ],
        out_specs=[whole(out) for out in outs],
        scratch_shapes=[pltpu.VMEM((rows, width), jnp.float32)],
        compiler_params=params_of(40),
        cost_estimate=cost_of(0.022 * rows),
        name="feed_down",
    )(h, mat, gains, biases, unit, cot, live)


def run_feed_back(core, sent, x, h, slope, up, down):
    rows, hidden = h.shape
    width = x.shape[1]
    steps = hidden // FEED
    half = steps // 2

    def chunk(step, core_ref):
        return (step + half * (1 - core_ref[0])) % steps

    def wide(step, core_ref):
        return (0, chunk(step, core_ref))

    def deep(step, core_ref):
        return (0, 0, chunk(step, core_ref))

    fixed = lambda step, core_ref: (0, 0)
    late = pl.BlockSpec((2, width, FEED), lambda step, core_ref: (0, 0, jnp.maximum(step - half, 0)))
    early = pl.BlockSpec((2, width, FEED), lambda step, core_ref: (0, 0, jnp.minimum(step, half - 1)))
    part = shape_of((2, width, hidden // 2), low)
    return pl.pallas_call(
        feed_back,
        grid_spec=pltpu.PrefetchScalarGridSpec(
            num_scalar_prefetch=1,
            grid=(steps,),
            in_specs=[
                pl.BlockSpec((rows, width), fixed),
                pl.BlockSpec((rows, width), fixed),
                pl.BlockSpec((rows, FEED), wide),
                pl.BlockSpec((rows, FEED), wide),
                pl.BlockSpec((1, width, FEED), deep),
                pl.BlockSpec((1, width, FEED), deep),
            ],
            out_specs=[
                pl.BlockSpec((rows, width), fixed),
                late,
                early,
                pl.BlockSpec((8, FEED), wide),
            ],
        ),
        out_shape=[
            shape_of((rows, width), jnp.float32),
            part,
            part,
            shape_of((8, hidden), jnp.float32),
        ],
        compiler_params=params_of(40),
        cost_estimate=cost_of(0.04 * rows),
        name="feed_back",
    )(core, sent, x, h, slope, up, down)


def adam_update(weight, moment_one, moment_two, average, grad, clip, rate):
    clipped = grad * clip
    new_one = beta_one * moment_one + (1.0 - beta_one) * clipped
    new_two = beta_two * moment_two + (1.0 - beta_two) * clipped * clipped
    direction = (
        new_one / (1.0 - beta_one**STEP) / (jnp.sqrt(new_two / (1.0 - beta_two**STEP)) + adam_eps)
    )
    new_weight = weight - rate * (direction + weight_decay * weight)
    new_average = ema_decay * average + (1.0 - ema_decay) * new_weight
    return (new_weight, new_one, new_two, new_average)


def local(
    lang,
    vis,
    word_mask,
    region_count,
    cot_lang,
    cot_vis,
    attn_w,
    attn_m,
    attn_v,
    attn_ema,
    ffn_w,
    ffn_m,
    ffn_v,
    ffn_ema,
    gains,
    gains_m,
    gains_v,
    gains_ema,
    biases,
    biases_m,
    biases_v,
    biases_ema,
    bias_up,
    bias_up_m,
    bias_up_v,
    bias_up_ema,
):
    core_index = lax.axis_index("mp")
    items, words, regions = lang.shape[0], lang.shape[1], vis.shape[1]
    width = lang.shape[2]
    model_share = gains.shape[1]
    hidden_share = bias_up.shape[1]
    small_own = jnp.concatenate([gains.reshape(-1), biases.reshape(-1), bias_up.reshape(-1)])
    small_size = small_own.shape[0]
    padded = -(-small_size // 1024) * 1024
    small_all = gather_small(jnp.pad(small_own, (0, padded - small_size)).reshape(-1, 128))
    small_all = small_all.reshape(small_all.shape[0], padded)
    cuts = (5 * model_share, 21 * model_share)

    def spread(columns, count):
        parts = columns.reshape(columns.shape[0], count, -1)
        return parts.transpose(1, 0, 2).reshape(count, -1)

    gain_all = spread(small_all[:, : cuts[0]], 5)
    bias_all = spread(small_all[:, cuts[0] : cuts[1]], 16)
    up_all = spread(small_all[:, cuts[1] : small_size], 2)
    attn_low = attn_w.astype(low)
    ffn_low = ffn_w.astype(low)
    forth, back = (4, 8, 1, 2), (4, 8, 2, 1)
    cross_mats = gather_mats(attn_low[0], forth, [(0, 4)])
    self_mats = gather_mats(attn_low[1:].reshape((-1,) + attn_low.shape[2:]), back, [(0, 4), (4, 4)])
    word_mats = gather_mats(ffn_low[0], forth, [(0, 1), (1, 1)])
    region_mats = gather_mats(ffn_low[1], back, [(0, 1), (1, 1)])
    up_mats, down_mats = zip(word_mats, region_mats)

    core = core_index.astype(jnp.int32).reshape(1)
    slots = (words, regions)
    groups = items // GROUP
    sizes = (words * GROUP, regions * GROUP)
    counts = (words * items, regions * items)
    word_live = word_mask.astype(jnp.float32)
    region_live = (jnp.arange(regions)[None, :] < region_count[:, None]).astype(jnp.float32)
    live = [word_live.reshape(-1, 1), region_live.reshape(-1, 1)]
    key_bias = [(part - 1.0) * -mask_fill for part in live]
    key_all = jnp.concatenate(key_bias)
    x_all = jnp.concatenate([lang.reshape(-1, width), vis.reshape(-1, width)])
    cots = [cot_lang.reshape(-1, width), cot_vis.reshape(-1, width)]

    def same_item(asked, asking):
        rows = jnp.arange(sizes[asked])[:, None] // slots[asked]
        columns = jnp.arange(sizes[asking])[None, :] // slots[asking]
        return jnp.where(rows == columns, 0.0, mask_fill).astype(jnp.float32)

    cross_plan = layer_plan(0, sizes, groups, 1)
    cross_same = [same_item(1, 0), same_item(0, 1)]
    cross_kept, unit_one, scale_one, low_one = run_front(
        cross_plan, x_all, None, cross_mats, gain_all, bias_all, key_all, cross_same
    )
    self_plans = [layer_plan(1 + stream, (sizes[stream],), groups, 1) for stream in range(2)]
    self_same = [[same_item(stream, stream)] for stream in range(2)]
    yx, xy = (2, 1, 8, 4), (1, 2, 8, 4)

    def go_up(stream):
        kept, unit, scale, lowered = run_front(
            self_plans[stream],
            low_one[stream],
            unit_one[stream],
            [self_mats[stream]],
            gain_all,
            bias_all,
            key_bias[stream],
            self_same[stream],
        )
        return kept, unit[0], scale[0], lowered[0]

    def go_feed(stream, made, gate):
        return run_up(stream, made[3], up_mats[stream], after(up_all, *gate))

    def go_down(stream, made, up):
        out, grad, sent, small = run_down(
            stream,
            up[0],
            down_mats[stream],
            gain_all,
            bias_all,
            made[1],
            cots[stream],
            live[stream],
        )
        return out.reshape(items, slots[stream], width), grad, sent, small

    def go_feed_back(stream, made, up, down):
        return run_feed_back(
            core, down[2], made[3], *up, up_mats[stream], down_mats[stream]
        )

    def go_back(stream, made, down, feed, gate):
        return run_back(
            self_plans[stream],
            after(core, *gate),
            [[down[1], feed[0]]],
            [made[1]],
            [made[2]],
            low_one[stream],
            [self_mats[stream]],
            gain_all,
            key_bias[stream],
            self_same[stream],
            made[0],
        )

    word_made = go_up(0)
    word_up = go_feed(0, word_made, ())
    word_down = go_down(0, word_made, word_up)
    word_feed = go_feed_back(0, word_made, word_up, word_down)
    word_ring = Scatter(word_feed[1], word_feed[2], yx)
    word_back = go_back(0, word_made, word_down, word_feed, ())
    word_self_ring = Scatter(word_back[1][0], word_back[2][0], xy)
    region_made = go_up(1)
    region_up = go_feed(1, region_made, (word_ring.parts,))
    word_ring.step()
    region_down = go_down(1, region_made, region_up)
    region_feed = go_feed_back(1, region_made, region_up, region_down)
    region_back = go_back(
        1, region_made, region_down, region_feed, (word_ring.parts, word_self_ring.parts)
    )
    region_rings = [
        Scatter(region_feed[1][part : part + 1], region_feed[2][part : part + 1], order)
        for part, order in enumerate((xy, yx))
    ]
    word_ring.step()
    word_self_ring.step()
    region_self_ring = Scatter(region_back[1][0], region_back[2][0], yx)
    grads_in, mine, other, cross_small = run_back(
        cross_plan,
        after(
            core, word_ring.parts, word_self_ring.parts, *[ring.parts for ring in region_rings]
        ),
        [[word_back[0][0]], [region_back[0][0]]],
        unit_one,
        scale_one,
        x_all,
        cross_mats,
        gain_all,
        key_all,
        cross_same,
        cross_kept,
    )
    outputs = [word_down[0], region_down[0]]
    downs = [word_down[1:], region_down[1:]]
    feeds = [word_feed, region_feed]
    self_small = [word_back[3], region_back[3]]
    grad_lang = grads_in[0].reshape(lang.shape)
    grad_vis = grads_in[1].reshape(vis.shape)
    cross_rings = [
        Scatter(mine[0][part : part + 2], other[0][part : part + 2], order)
        for part, order in ((0, xy), (2, yx))
    ]
    region_shard = jnp.concatenate([ring.finish() for ring in region_rings])
    cross_shard = jnp.concatenate([ring.finish() for ring in cross_rings])
    attn_shard = jnp.stack([cross_shard, word_self_ring.finish(), region_self_ring.finish()])
    ffn_shard = jnp.stack([word_ring.finish(), region_shard])

    layers = [cross_small, self_small[0], self_small[1]]
    gain_rows = [part[0:1] for part in layers] + [part[2][0:1] for part in downs]
    bias_rows = []
    for part in layers:
        bias_rows += [part[3:5], part[2:3]]
    bias_rows += [part[2][2:3] for part in downs]
    bias_rows += [part[1:2] for part in layers] + [part[2][1:2] for part in downs]
    up_rows = [part[3][0:1] for part in feeds]

    def split(rows, share):
        rows = jnp.concatenate(rows)
        count = rows.shape[0]
        return rows.reshape(count, -1, share).transpose(1, 0, 2).reshape(-1, count * share)

    small_grad = jnp.concatenate(
        [split(gain_rows, model_share), split(bias_rows, model_share), split(up_rows, hidden_share)],
        axis=1,
    )
    small_grad = jnp.pad(small_grad, ((0, 0), (0, padded - small_size)))
    small_sum = scatter_small(small_grad.reshape(small_grad.shape[0], -1, 128)).reshape(-1)
    gains_shard = small_sum[: cuts[0]].reshape(5, model_share)
    biases_shard = small_sum[cuts[0] : cuts[1]].reshape(16, model_share)
    up_shard = small_sum[cuts[1] : small_size].reshape(2, hidden_share)
    squares = jnp.sum(attn_shard * attn_shard) + jnp.sum(ffn_shard * ffn_shard)
    squares = squares + jnp.where(core_index == 0, jnp.sum(small_sum * small_sum), 0.0)
    grad_norm = jnp.sqrt(sum_all(squares))
    clip = jnp.minimum(1.0, clip_norm / (grad_norm + 1e-06))
    attn_new = adam_update(attn_w, attn_m, attn_v, attn_ema, attn_shard, clip, rate_mats)
    ffn_new = adam_update(ffn_w, ffn_m, ffn_v, ffn_ema, ffn_shard, clip, rate_mats)
    gains_new = adam_update(gains, gains_m, gains_v, gains_ema, gains_shard, clip, rate_small)
    biases_new = adam_update(biases, biases_m, biases_v, biases_ema, biases_shard, clip, rate_small)
    up_new = adam_update(bias_up, bias_up_m, bias_up_v, bias_up_ema, up_shard, clip, rate_small)
    return (
        outputs[0],
        outputs[1],
        grad_lang,
        grad_vis,
        grad_norm,
        attn_new[0],
        attn_new[1],
        attn_new[2],
        attn_new[3],
        ffn_new[0],
        ffn_new[1],
        ffn_new[2],
        ffn_new[3],
        gains_new[0],
        gains_new[1],
        gains_new[2],
        gains_new[3],
        biases_new[0],
        biases_new[1],
        biases_new[2],
        biases_new[3],
        up_new[0],
        up_new[1],
        up_new[2],
        up_new[3],
    )


def solution(mesh):
    return jax.shard_map(
        local,
        mesh=mesh,
        in_specs=(
            P(("dp", "mp"), None, None),
            P(("dp", "mp"), None, None),
            P(("dp", "mp"), None),
            P(("dp", "mp")),
            P(("dp", "mp"), None, None),
            P(("dp", "mp"), None, None),
            P(None, None, "dp", "mp"),
            P(None, None, "dp", "mp"),
            P(None, None, "dp", "mp"),
            P(None, None, "dp", "mp"),
            P(None, None, "dp", "mp"),
            P(None, None, "dp", "mp"),
            P(None, None, "dp", "mp"),
            P(None, None, "dp", "mp"),
            P(None, "dp"),
            P(None, "dp"),
            P(None, "dp"),
            P(None, "dp"),
            P(None, "dp"),
            P(None, "dp"),
            P(None, "dp"),
            P(None, "dp"),
            P(None, "dp"),
            P(None, "dp"),
            P(None, "dp"),
            P(None, "dp"),
        ),
        out_specs=(
            P(("dp", "mp"), None, None),
            P(("dp", "mp"), None, None),
            P(("dp", "mp"), None, None),
            P(("dp", "mp"), None, None),
            P(),
            P(None, None, "dp", "mp"),
            P(None, None, "dp", "mp"),
            P(None, None, "dp", "mp"),
            P(None, None, "dp", "mp"),
            P(None, None, "dp", "mp"),
            P(None, None, "dp", "mp"),
            P(None, None, "dp", "mp"),
            P(None, None, "dp", "mp"),
            P(None, "dp"),
            P(None, "dp"),
            P(None, "dp"),
            P(None, "dp"),
            P(None, "dp"),
            P(None, "dp"),
            P(None, "dp"),
            P(None, "dp"),
            P(None, "dp"),
            P(None, "dp"),
            P(None, "dp"),
            P(None, "dp"),
        ),
        check_vma=False,
    )
```

time: 1650 us -> 836 us (0.51)
  waiting for transfers between devices: 807 us -> 348 us
  matrix products: 268 us -> 0 us
  Pallas kernels: 0 us -> 237 us
  blocking collectives: 180 us -> 0 us
  other arithmetic: 166 us -> 63.2 us
  local copies, waits for them, and re-layouts: 188 us -> 101 us
  starting transfers between devices: 3.14 us -> 73.1 us
    unnamed x24 -> x0, waiting for transfers between devices: 399 us -> none
    ppermute x0 -> x73, waiting for transfers between devices: none -> 348 us  [the longest x56 347 us: send(): return lax.ppermute(values, 'dp', routes[bit])]
    reduce_scatter x13 -> x0, waiting for transfers between devices: 301 us -> none  [the longest x1 287 us: local(): lax.psum_scatter(ffn_grad, 'dp', scatter_dimension=2, tiled=True)]
    dot_general x84 -> x0, matrix products: 268 us -> none  [the longest x2 20.2 us: feed_backward(): jnp.einsum('gnd,df->gnf', grad_out, matrices[1], preferred_element_type=j...]
    pallas_call x0 -> x16, Pallas kernels: none -> 237 us  [the longest x3 86 us: run_back(): pl.pallas_call(functools.partial(attend_back, plan), out_shape=outs, in_s...]
    all_gather x11 -> x0, blocking collectives: 141 us -> none  [the longest x1 43.5 us: local(): lax.all_gather(biases, 'dp', axis=1, tiled=True)]
    all_gather x8 -> x0, waiting for transfers between devices: 107 us -> none  [the longest x1 55.5 us: local(): lax.all_gather(attn_w.astype(jnp.bfloat16), 'dp', axis=2, tiled=True)]
    convert_element_type x38 -> x1, local copies, waits for them, and re-layouts: 77 us -> 0.13 us  [local(): (jnp.arange(regions)[None, :] < region_count[:, None]).astype(jnp.float32)]
  transfers between devices with their start and end apart: 23 -> 73, of which waited for: 8 -> 32; matrix products, arithmetic and copies ran while one was open for 30% -> 15% of each run, Pallas kernels for 0% -> 29%
where the time goes in v1:
time: 836 us; the launch traced here: 831 us
  waiting for transfers between devices  348 us (42%)
  Pallas kernels  237 us (28%)
  local copies, waits for them, and re-layouts  101 us (12%)
  starting transfers between devices  73.1 us (9%)
  other arithmetic  63.2 us (8%)
  between operations  8.8 us (1%)
    ppermute x56, waiting for transfers between devices, send(): return lax.ppermute(values, 'dp', routes[bit])  347 us
    pallas_call x3, Pallas kernels, run_back(): pl.pallas_call(functools.partial(attend_back, plan), out_shape=outs, in_s...  86 us
    ppermute x56, starting transfers between devices, send(): return lax.ppermute(values, 'dp', routes[bit])  69.1 us
    pallas_call x3, Pallas kernels, run_front(): pl.pallas_call(functools.partial(attend_front, plan), out_shape=outs, in_...  50.9 us
    unnamed x224, local copies, waits for them, and re-layouts  42.6 us
    pallas_call x2, Pallas kernels, run_feed_back(): pl.pallas_call(feed_back, grid_spec=pltpu.PrefetchScalarGridSpec(num_scal...  35.2 us
    pallas_call x2, Pallas kernels, run_up(): pl.pallas_call(functools.partial(feed_up, stream), grid=(hidden // FEED,)...  29.2 us
    pallas_call x2, Pallas kernels, run_down(): pl.pallas_call(functools.partial(feed_down, stream), grid=(hidden // FEED...  19.4 us
  transfers between devices with their start and end apart: 73, of which 32 were waited for; matrix products, arithmetic and copies ran while one was open for 15% of the time, Pallas kernels for 29%

profile of v1, /device:TPU:0, one launch (start us, length us, event | category | flops | bytes accessed | tf_op | source)
XLA Modules:
  0.0 830.8 jit_solution(18092818595913824302)
XLA Ops:
  17.0 14.2 %collective-permute-done.10 = bf16[1,8,48,384]{3,2,1,0:T(8,128)(2,1)S(1)} collective-permute-done((bf16[1,8,48,384]{3,2,1,0:T(8,128)(2,1)S(1)}, bf16[1,8,48,384]{3,2,1,0:T(8,128)(2,1)S(1)}, u32[]{:S(2)}, u32[]{:S(2)}) %collective-permute-start.10) | collective-permute-done | bytes 294944 | tf_op jit(solution)/shard_map/ppermute | solution.py:57
  35.7 27.1 %collective-permute-done.17 = bf16[2,2,48,1536]{3,2,1,0:T(8,128)(2,1)S(1)} collective-permute-done((bf16[2,2,48,1536]{3,2,1,0:T(8,128)(2,1)S(1)}, bf16[2,2,48,1536]{3,2,1,0:T(8,128)(2,1)S(1)}, u32[]{:S(2)}, u32[]{:S(2)}) %collective-permute-start.17) | collective-permute-done | bytes 589856 | tf_op jit(solution)/shard_map/ppermute | solution.py:57
  65.8 9.6 %collective-permute-done.11 = bf16[2,8,48,384]{3,2,1,0:T(8,128)(2,1)S(1)} collective-permute-done((bf16[2,8,48,384]{3,2,1,0:T(8,128)(2,1)S(1)}, bf16[2,8,48,384]{3,2,1,0:T(8,128)(2,1)S(1)}, u32[]{:S(2)}, u32[]{:S(2)}) %collective-permute-start.11) | collective-permute-done | bytes 589856 | tf_op jit(solution)/shard_map/ppermute | solution.py:57
  83.4 16.1 %collective-permute-done.2 = bf16[4,4,48,384]{3,2,1,0:T(8,128)(2,1)S(1)} collective-permute-done((bf16[4,4,48,384]{3,2,1,0:T(8,128)(2,1)S(1)}, bf16[4,4,48,384]{3,2,1,0:T(8,128)(2,1)S(1)}, u32[]{:S(2)}, u32[]{:S(2)}) %collective-permute-start.2) | collective-permute-done | bytes 589856 | tf_op jit(solution)/shard_map/ppermute | solution.py:57
  118.3 57.3 %collective-permute-done.7 = f32[2,16,128]{2,1,0:T(8,128)S(1)} collective-permute-done((f32[2,16,128]{2,1,0:T(8,128)S(1)}, f32[2,16,128]{2,1,0:T(8,128)S(1)}, u32[]{:S(2)}, u32[]{:S(2)}) %collective-permute-start.7) | collective-permute-done | bytes 16416 | tf_op jit(solution)/shard_map/ppermute | solution.py:57
  213.6 25.6 %attend_front.3 = (bf16[896,768]{1,0:T(8,128)(2,1)S(1)}, bf16[896,768]{1,0:T(8,128)(2,1)}, bf16[896,768]{1,0:T(8,128)(2,1)}, bf16[896,768]{1,0:T(8,128)(2,1)}, f...) custom-call(bf16[896,768]{1,0:T(8,128)(2,1)} %constant_dynamic-updat, ...), custom_call_target="tpu_custom_call" | custom-call | flops 28851200000 | bytes 1048576 | tf_op jit(solution)/shard_map/attend_front/pallas_call | solution.py:537
  239.3 4.6 assemble.5
  248.2 8.5 %attend_front.4 = (bf16[320,768]{1,0:T(8,128)(2,1)S(1)}, bf16[320,768]{1,0:T(8,128)(2,1)S(1)}, bf16[320,768]{1,0:T(8,128)(2,1)S(1)}, bf16[320,768]{1,0:T(8,128)(...) custom-call(bf16[320,768]{1,0:T(8,128)(2,1)S(1)} %get-tuple-element., ...), custom_call_target="tpu_custom_call" | custom-call | flops 10304000000 | bytes 1048576 | tf_op jit(solution)/shard_map/attend_front/pallas_call | solution.py:537
  263.1 10.6 %feed_up.2 = (bf16[320,3072]{1,0:T(8,128)(2,1)S(1)}, bf16[320,3072]{1,0:T(8,128)(2,1)S(1)}) custom-call(bf16[320,768]{1,0:T(8,128)(2,1)S(1)} %get-tuple-element.98.x_ref, bf16[1,768,3072]{2,1,0:T(8,128)(2,1)S(1)} %get-tuple-element.99.mat_ref.up_ref, f32[2,3072]{1,0:T(2,128)S(1)} %copy-done.48), custom_call_target="tpu_custom_call" | custom-call | flops 12144000000 | bytes 1048576 | tf_op jit(solution)/shard_map/feed_up/pallas_call | solution.py:679
  276.2 6.8 feed_down.2
  285.4 15.0 %feed_back.2 = (f32[320,768]{1,0:T(8,128)S(1)}, bf16[2,768,1536]{2,1,0:T(8,128)(2,1)S(1)}, bf16[2,768,1536]{2,1,0:T(8,128)(2,1)}, f32[8,3072]{1,0:T(8,128)S(1)}) custom-call(s32[1]{0:T(128)} %bitcast.1.core_ref.refs_0_, bf16[320,768]{1,0:T(8,128)(2,1)S(1)} %get-tuple-element.109.do_ref, bf16[320,768]{1,0:T(8,128)(2,1)S(1)} %get-tuple-element.98.x_ref, ...), custom_call_target="tpu_custom_call" | custom-call | flops 14720000000 | bytes 1048576 | tf_op jit(solution)/shard_map/feed_back/pallas_call | solution.py:749
  304.2 19.1 %attend_back.3 = (f32[320,768]{1,0:T(8,128)}, bf16[4,768,384]{2,1,0:T(8,128)(2,1)}, bf16[4,768,384]{2,1,0:T(8,128)(2,1)}, f32[8,768]{1,0:T(8,128)}) custom-call(s32[1]{0:T(128)} %bitcast.1.core_ref.refs_0_, f32[320,768]{1,0:T(8,128)} %copy-done.17, f32[320,768]{1,0:T(8,128)} %copy-done.18, f32[320,768]{1,0:T(8,128)} %copy-done.16, f32[320,1]{1,0:T(8,128)} %copy-done.41, ...), custom_call_target="tpu_custom_call" | custom-call | tf_op jit(solution)/shard_map/attend_back/pallas_call | solution.py:561
  326.2 26.8 %collective-permute-done.24 = bf16[4,2,48,1536]{3,2,1,0:T(8,128)(2,1)S(1)} collective-permute-done((bf16[4,2,48,1536]{3,2,1,0:T(8,128)(2,1)S(1)}, bf16[4,2,48,1536]{3,2,1,0:T(8,128)(2,1)S(1)}, u32[]{:S(2)}, u32[]{:S(2)}) %collective-permute-start.24) | collective-permute-done | bytes 1179680 | tf_op jit(solution)/shard_map/ppermute | solution.py:57
  366.5 42.2 %collective-permute-done.26.refs_2_ = bf16[8,2,48,1536]{3,2,1,0:T(8,128)(2,1)} collective-permute-done((bf16[8,2,48,1536]{3,2,1,0:T(8,128)(2,1)S(1)}, bf16[8,2,48,1536]{3,2,1,0:T(8,128)(2,1)}, u32[]{:S(2)}, u32[]{:S(2)}) %collective-permute-start.26) | collective-permute-done | bytes 2359328 | tf_op jit(solution)/shard_map/ppermute | solution.py:57
  408.8 23.8 %collective-permute-done.32 = bf16[4,2,2,2,48,384]{5,4,0,2,1,3:T(8,128)(2,1)} collective-permute-done((bf16[4,2,2,2,48,384]{5,4,0,2,1,3:T(8,128)(2,1)}, bf16[4,2,2,2,48,384]{5,4,0,2,1,3:T(8,128)(2,1)}, u32[]{:S(2)}, u32[]{:S(2)}) %collective-permute-start.32) | collective-permute-done | bytes 1179680 | tf_op jit(solution)/shard_map/ppermute | solution.py:57
  437.1 16.8 %attend_front.5 = (bf16[576,768]{1,0:T(8,128)(2,1)S(1)}, bf16[576,768]{1,0:T(8,128)(2,1)S(1)}, bf16[576,768]{1,0:T(8,128)(2,1)S(1)}, bf16[576,768]{1,0:T(8,128)(...) custom-call(bf16[576,768]{1,0:T(8,128)(2,1)S(1)} %copy-done.21, ...), custom_call_target="tpu_custom_call" | custom-call | flops 18547200000 | bytes 1048576 | tf_op jit(solution)/shard_map/attend_front/pallas_call | solution.py:537
  453.9 4.8 assemble.7
  473.4 18.6 %feed_up.3 = (bf16[576,3072]{1,0:T(8,128)(2,1)S(1)}, bf16[576,3072]{1,0:T(8,128)(2,1)S(1)}) custom-call(bf16[576,768]{1,0:T(8,128)(2,1)S(1)} %get-tuple-element.107.x_ref, bf16[1,768,3072]{2,1,0:T(8,128)(2,1)S(1)} %bitcast.213, f32[2,3072]{1,0:T(2,128)S(1)} %copy-done.49), custom_call_target="tpu_custom_call" | custom-call | flops 21859201024 | bytes 1048576 | tf_op jit(solution)/shard_map/feed_up/pallas_call | solution.py:679
  492.0 12.7 %feed_down.3 = (f32[576,768]{1,0:T(8,128)S(1)}, f32[576,768]{1,0:T(8,128)S(1)}, bf16[576,768]{1,0:T(8,128)(2,1)S(1)}, f32[8,768]{1,0:T(8,128)S(1)}) custom-call(bf16[576,3072]{1,0:T(8,128)(2,1)S(1)} %get-tuple-element.114.h_ref, bf16[1,768,3072]{2,1,0:T(8,128)(2,1)} %copy-done.54, f32[5,768]{1,0:T(8,128)S(1)} %copy-done.34, f32[16,768]{1,0:T(8,128)S(1)} %copy-done.44, ...), custom_call_target="tpu_custom_call" | custom-call | flops 14572800000 | bytes 1048576 | tf_op jit(solution)/shard_map/feed_down/pallas_call | solution.py:709
  506.5 20.2 %feed_back.3 = (f32[576,768]{1,0:T(8,128)S(1)}, bf16[2,768,1536]{2,1,0:T(8,128)(2,1)}, bf16[2,768,1536]{2,1,0:T(8,128)(2,1)}, f32[8,3072]{1,0:T(8,128)S(1)}) custom-call(s32[1]{0:T(128)} %bitcast.1.core_ref.refs_0_, bf16[576,768]{1,0:T(8,128)(2,1)S(1)} %get-tuple-element.128.do_ref, bf16[576,768]{1,0:T(8,128)(2,1)S(1)} %get-tuple-element.107.x_ref, ...), custom_call_target="tpu_custom_call" | custom-call | flops 26496000000 | bytes 1048576 | tf_op jit(solution)/shard_map/feed_back/pallas_call | solution.py:749
  526.8 5.5 fusion.35
  554.3 28.1 %attend_back.4 = (f32[576,768]{1,0:T(8,128)}, bf16[4,768,384]{2,1,0:T(8,128)(2,1)}, bf16[4,768,384]{2,1,0:T(8,128)(2,1)}, f32[8,768]{1,0:T(8,128)}) custom-call(s32[1]{0:T(128)} %bitcast.1.core_ref.refs_0_, f32[576,768]{1,0:T(8,128)} %copy-done.7, f32[576,768]{1,0:T(8,128)} %copy-done.8, f32[576,768]{1,0:T(8,128)} %get-tuple-element.116.unit_ref.refs_3_, ...), custom_call_target="tpu_custom_call" | custom-call | tf_op jit(solution)/shard_map/attend_back/pallas_call | solution.py:561
  598.4 38.7 %attend_back.5 = (f32[320,768]{1,0:T(8,128)}, f32[576,768]{1,0:T(8,128)}, bf16[4,768,384]{2,1,0:T(8,128)(2,1)}, bf16[4,768,384]{2,1,0:T(8,128)(2,1)}, f32[8,768]{1,0:T(8,128)}) custom-call(s32[1]{0:T(128)} %bitcast.1.core_ref.refs_0_, f32[320,768]{1,0:T(8,128)} %get-tuple-element.133.refs_1_, f32[576,768]{1,0:T(8,128)} %get-tuple-element.143.refs_2_, ...), custom_call_target="tpu_custom_call" | custom-call | tf_op jit(solution)/shard_map/attend_back/pallas_call | solution.py:561
  651.0 4.6 collective-permute-done.64
  672.2 7.6 collective-permute-done.56
  683.0 14.6 %collective-permute-done.57 = bf16[1,2,48,1536]{3,2,1,0:T(8,128)(2,1)S(1)} collective-permute-done((bf16[1,2,48,1536]{3,2,1,0:T(8,128)(2,1)S(1)}, bf16[1,2,48,1536]{3,2,1,0:T(8,128)(2,1)S(1)}, u32[]{:S(2)}, u32[]{:S(2)}) %collective-permute-start.57) | collective-permute-done | bytes 294944 | tf_op jit(solution)/shard_map/ppermute | solution.py:57
  697.7 10.0 %collective-permute-done.61 = bf16[1,2,48,1536]{3,2,1,0:T(8,128)(2,1)S(1)} collective-permute-done((bf16[1,2,48,1536]{3,2,1,0:T(8,128)(2,1)S(1)}, bf16[1,2,48,1536]{3,2,1,0:T(8,128)(2,1)S(1)}, u32[]{:S(2)}, u32[]{:S(2)}) %collective-permute-start.61) | collective-permute-done | bytes 294944 | tf_op jit(solution)/shard_map/ppermute | solution.py:57
  726.6 9.8 %collective-permute-done.41 = bf16[2,2,2,2,48,384]{5,4,0,2,1,3:T(8,128)(2,1)S(1)} collective-permute-done((bf16[2,2,2,2,48,384]{5,4,0,2,1,3:T(8,128)(2,1)S(1)}, bf16[2,2,2,2,48,384]{5,4,0,2,1,3:T(8,128)(2,1)S(1)}, u32[]{:S(2)}, u32[]{:S(2)}) %collective-permute-start.41) | collective-permute-done | bytes 589856 | tf_op jit(solution)/shard_map/ppermute | solution.py:57
  743.6 21.8 %collective-permute-done.37 = bf16[2,2,2,48,384]{4,3,0,2,1:T(8,128)(2,1)S(1)} collective-permute-done((bf16[2,2,2,48,384]{4,3,0,2,1:T(8,128)(2,1)S(1)}, bf16[2,2,2,48,384]{4,3,0,2,1:T(8,128)(2,1)S(1)}, u32[]{:S(2)}, u32[]{:S(2)}) %collective-permute-start.37) | collective-permute-done | bytes 294944 | tf_op jit(solution)/shard_map/ppermute | solution.py:57
  768.2 6.9 collective-permute-done.38
  780.0 11.7 %collective-permute-done.51 = bf16[4,2,48,384]{3,2,0,1:T(8,128)(2,1)S(1)} collective-permute-done((bf16[4,2,48,384]{3,2,0,1:T(8,128)(2,1)S(1)}, bf16[4,2,48,384]{3,2,0,1:T(8,128)(2,1)S(1)}, u32[]{:S(2)}, u32[]{:S(2)}) %collective-permute-start.51) | collective-permute-done | bytes 294944 | tf_op jit(solution)/shard_map/ppermute | solution.py:57
  792.0 5.1 collective-permute-done.52
  (538 shorter events, 277.4 us)
Async XLA Ops:
  6.2 108.3 %collective-permute-start.6 = (f32[1,16,128]{2,1,0:T(8,128)S(1)}, f32[1,16,128]{2,1,0:T(8,128)S(1)}, u32[]{:S(2)}, u32[]{:S(2)}) collective-permute-start(f32[1,16,128]{2,1,0:T(8,128)S(1)} %pad_bitcast_fusion.1), channel_id=1, source_target_pairs={{0,2},{2,0},{4,6},{6,4},{8,10},{10,8},{12,14},{14,12},{16,18},{18,... | collective-permute-start | bytes 24584 | tf_op jit(solution)/shard_map/ppermute | solution.py:57
  13.8 49.0 %collective-permute-start.17 = (bf16[2,2,48,1536]{3,2,1,0:T(8,128)(2,1)S(1)}, bf16[2,2,48,1536]{3,2,1,0:T(8,128)(2,1)S(1)}, u32[]{:S(2)}, u32[]{:S(2)}) collective-permute-start(bf16[2,2,48,1536]{3,2,1,0:T(8,128)(2,1)S(1)} %pad_maximum_fusion.11), channel_id=1, source_target_pairs={{0,16},{2,18},{4,20},{6,22},{8,24},{10,26},{12,28},{14,30},{16,0},... | collective-permute-start | bytes 1769480 | tf_op jit(solution)/shard_map/ppermute | solution.py:57
  31.3 44.1 %collective-permute-start.11 = (bf16[2,8,48,384]{3,2,1,0:T(8,128)(2,1)S(1)}, bf16[2,8,48,384]{3,2,1,0:T(8,128)(2,1)S(1)}, u32[]{:S(2)}, u32[]{:S(2)}) collective-permute-start(bf16[2,8,48,384]{3,2,1,0:T(8,128)(2,1)S(1)} %pad_maximum_fusion.10), channel_id=1, source_target_pairs={{0,16},{2,18},{4,20},{6,22},{8,24},{10,26},{12,28},{14,30},{16,0},... | collective-permute-start | bytes 1769480 | tf_op jit(solution)/shard_map/ppermute | solution.py:57
  32.8 48.1 %collective-permute-start.1 = (bf16[2,4,48,384]{3,2,1,0:T(8,128)(2,1)}, bf16[2,4,48,384]{3,2,1,0:T(8,128)(2,1)S(1)}, u32[]{:S(2)}, u32[]{:S(2)}) collective-permute-start(bf16[2,4,48,384]{3,2,1,0:T(8,128)(2,1)} %pad_maximum_fusion.14), channel_id=1, source_target_pairs={{0,16},{2,18},{4,20},{6,22},{8,24},{10,26},{12,28},{14,30},{16,0},... | collective-permute-start | bytes 884744 | tf_op jit(solution)/shard_map/ppermute | solution.py:57
  64.0 43.0 %collective-permute-start.18 = (bf16[4,2,48,1536]{3,2,1,0:T(8,128)(2,1)}, bf16[4,2,48,1536]{3,2,1,0:T(8,128)(2,1)}, u32[]{:S(2)}, u32[]{:S(2)}) collective-permute-start(bf16[4,2,48,1536]{3,2,1,0:T(8,128)(2,1)} %pad_maximum_fusion.5), channel_id=1, source_target_pairs={{0,2},{2,0},{4,6},{6,4},{8,10},{10,8},{12,14},{14,12},{16,18},{18,... | collective-permute-start | bytes 3538952 | tf_op jit(solution)/shard_map/ppermute | solution.py:57
  101.6 74.1 %collective-permute-start.4 = (bf16[8,4,48,384]{3,2,1,0:T(8,128)(2,1)}, bf16[8,4,48,384]{3,2,1,0:T(8,128)(2,1)}, u32[]{:S(2)}, u32[]{:S(2)}) collective-permute-start(bf16[8,4,48,384]{3,2,1,0:T(8,128)(2,1)} %pad_maximum_fusion.3.refs_0_), channel_id=1, source_target_pairs={{0,4},{2,6},{4,0},{6,2},{8,12},{10,14},{12,8},{14,10},{16,20},{18,... | collective-permute-start | bytes 3538952 | tf_op jit(solution)/shard_map/ppermute | solution.py:57
  105.5 107.6 %collective-permute-start.14 = (bf16[8,8,48,384]{3,2,1,0:T(8,128)(2,1)}, bf16[8,8,48,384]{3,2,1,0:T(8,128)(2,1)}, u32[]{:S(2)}, u32[]{:S(2)}) collective-permute-start(bf16[8,8,48,384]{3,2,1,0:T(8,128)(2,1)} %pad_maximum_fusion.refs_0_), channel_id=1, source_target_pairs={{0,2},{2,0},{4,6},{6,4},{8,10},{10,8},{12,14},{14,12},{16,18},{18,... | collective-permute-start | bytes 7077896 | tf_op jit(solution)/shard_map/ppermute | solution.py:57
  108.5 104.6 %collective-permute-start.20 = (bf16[8,2,48,1536]{3,2,1,0:T(8,128)(2,1)S(1)}, bf16[8,2,48,1536]{3,2,1,0:T(8,128)(2,1)}, u32[]{:S(2)}, u32[]{:S(2)}) collective-permute-start(bf16[8,2,48,1536]{3,2,1,0:T(8,128)(2,1)S(1)} %pad_maximum_fusion.1.refs_0_), channel_id=1, source_target_pairs={{0,4},{2,6},{4,0},{6,2},{8,12},{10,14},{12,8},{14,10},{16,20},{18,... | collective-permute-start | bytes 7077896 | tf_op jit(solution)/shard_map/ppermute | solution.py:57
  114.6 61.0 %collective-permute-start.7 = (f32[2,16,128]{2,1,0:T(8,128)S(1)}, f32[2,16,128]{2,1,0:T(8,128)S(1)}, u32[]{:S(2)}, u32[]{:S(2)}) collective-permute-start(f32[2,16,128]{2,1,0:T(8,128)S(1)} %pad_maximum_fusion.19), channel_id=1, source_target_pairs={{0,4},{2,6},{4,0},{6,2},{8,12},{10,14},{12,8},{14,10},{16,20},{18,... | collective-permute-start | bytes 49160 | tf_op jit(solution)/shard_map/ppermute | solution.py:57
  175.6 31.9 %collective-permute-start.3 = (bf16[8,4,48,384]{3,2,1,0:T(8,128)(2,1)}, bf16[8,4,48,384]{3,2,1,0:T(8,128)(2,1)}, u32[]{:S(2)}, u32[]{:S(2)}) collective-permute-start(bf16[8,4,48,384]{3,2,1,0:T(8,128)(2,1)} %pad_maximum_fusion.3.refs_0_), channel_id=1, source_target_pairs={{0,1},{1,0},{2,3},{3,2},{4,5},{5,4},{6,7},{7,6},{8,9},{9,8},{10,11... | collective-permute-start | bytes 3538952 | tf_op jit(solution)/shard_map/ppermute | solution.py:61
  204.5 118.9 %collective-permute-start.23 = (bf16[2,2,48,1536]{3,2,1,0:T(8,128)(2,1)}, bf16[2,2,48,1536]{3,2,1,0:T(8,128)(2,1)}, u32[]{:S(2)}, u32[]{:S(2)}) collective-permute-start(bf16[2,2,48,1536]{3,2,1,0:T(8,128)(2,1)} %pad_maximum_fusion.12), channel_id=1, source_target_pairs={{0,16},{2,18},{4,20},{6,22},{8,24},{10,26},{12,28},{14,30},{16,0},... | collective-permute-start | bytes 1769480 | tf_op jit(solution)/shard_map/ppermute | solution.py:57
  207.5 31.8 %collective-permute-start.13 = (bf16[8,8,48,384]{3,2,1,0:T(8,128)(2,1)}, bf16[8,8,48,384]{3,2,1,0:T(8,128)(2,1)S(1)}, u32[]{:S(2)}, u32[]{:S(2)}) collective-permute-start(bf16[8,8,48,384]{3,2,1,0:T(8,128)(2,1)} %pad_maximum_fusion.refs_0_), channel_id=1, source_target_pairs={{0,1},{1,0},{2,3},{3,2},{4,5},{5,4},{6,7},{7,6},{8,9},{9,8},{10,11... | collective-permute-start | bytes 7077896 | tf_op jit(solution)/shard_map/ppermute | solution.py:61
  207.5 49.4 %collective-permute-start.19 = (bf16[8,2,48,1536]{3,2,1,0:T(8,128)(2,1)S(1)}, bf16[8,2,48,1536]{3,2,1,0:T(8,128)(2,1)S(1)}, u32[]{:S(2)}, u32[]{:S(2)}) collective-permute-start(bf16[8,2,48,1536]{3,2,1,0:T(8,128)(2,1)S(1)} %pad_maximum_fusion.1.refs_0_), channel_id=1, source_target_pairs={{0,1},{1,0},{2,3},{3,2},{4,5},{5,4},{6,7},{7,6},{8,9},{9,8},{10,11... | collective-permute-start | bytes 7077896 | tf_op jit(solution)/shard_map/ppermute | solution.py:61
  213.2 43.7 %collective-permute-start.21 = (bf16[8,2,48,1536]{3,2,1,0:T(8,128)(2,1)}, bf16[8,2,48,1536]{3,2,1,0:T(8,128)(2,1)}, u32[]{:S(2)}, u32[]{:S(2)}) collective-permute-start(bf16[8,2,48,1536]{3,2,1,0:T(8,128)(2,1)} %collective-permute-done.20.refs_2_), channel_id=1, source_target_pairs={{0,1},{1,0},{2,3},{3,2},{4,5},{5,4},{6,7},{7,6},{8,9},{9,8},{10,11... | collective-permute-start | bytes 7077896 | tf_op jit(solution)/shard_map/ppermute | solution.py:61
  323.3 32.6 %collective-permute-start.31 = (bf16[4,768,384]{2,1,0:T(8,128)(2,1)}, bf16[4,768,384]{2,1,0:T(8,128)(2,1)}, u32[]{:S(2)}, u32[]{:S(2)}) collective-permute-start(bf16[4,768,384]{2,1,0:T(8,128)(2,1)} %get-tuple-element.127), channel_id=1, source_target_pairs={{0,1},{1,0},{2,3},{3,2},{4,5},{5,4},{6,7},{7,6},{8,9},{9,8},{10,11... | collective-permute-start | bytes 7077896 | tf_op jit(solution)/shard_map/ppermute | solution.py:61
  354.4 54.3 %collective-permute-start.26 = (bf16[8,2,48,1536]{3,2,1,0:T(8,128)(2,1)S(1)}, bf16[8,2,48,1536]{3,2,1,0:T(8,128)(2,1)}, u32[]{:S(2)}, u32[]{:S(2)}) collective-permute-start(bf16[8,2,48,1536]{3,2,1,0:T(8,128)(2,1)S(1)} %pad_maximum_fusion.2.refs_0_), channel_id=1, source_target_pairs={{0,2},{2,0},{4,6},{6,4},{8,10},{10,8},{12,14},{14,12},{16,18},{18,... | collective-permute-start | bytes 7077896 | tf_op jit(solution)/shard_map/ppermute | solution.py:57
  355.9 109.3 %collective-permute-start.28 = (bf16[2,768,1536]{2,1,0:T(8,128)(2,1)}, bf16[2,768,1536]{2,1,0:T(8,128)(2,1)}, u32[]{:S(2)}, u32[]{:S(2)}) collective-permute-start(bf16[2,768,1536]{2,1,0:T(8,128)(2,1)} %get-tuple-element.112), channel_id=1, source_target_pairs={{0,1},{1,0},{2,3},{3,2},{4,5},{5,4},{6,7},{7,6},{8,9},{9,8},{10,11... | collective-permute-start | bytes 14155784 | tf_op jit(solution)/shard_map/ppermute | solution.py:61
  361.3 71.3 %collective-permute-start.32 = (bf16[4,2,2,2,48,384]{5,4,0,2,1,3:T(8,128)(2,1)}, bf16[4,2,2,2,48,384]{5,4,0,2,1,3:T(8,128)(2,1)}, u32[]{:S(2)}, u32[]{:S(2)}) collective-permute-start(bf16[4,2,2,2,48,384]{5,4,0,2,1,3:T(8,128)(2,1)} %bitcast.203), channel_id=1, source_target_pairs={{0,2},{2,0},{4,6},{6,4},{8,10},{10,8},{12,14},{14,12},{16,18},{18,... | collective-permute-start | bytes 3538952 | tf_op jit(solution)/shard_map/ppermute | solution.py:57
  366.3 87.6 %collective-permute-start.25 = (bf16[8,2,48,1536]{3,2,1,0:T(8,128)(2,1)S(1)}, bf16[8,2,48,1536]{3,2,1,0:T(8,128)(2,1)}, u32[]{:S(2)}, u32[]{:S(2)}) collective-permute-start(bf16[8,2,48,1536]{3,2,1,0:T(8,128)(2,1)S(1)} %pad_maximum_fusion.2.refs_0_), channel_id=1, source_target_pairs={{0,1},{1,0},{2,3},{3,2},{4,5},{5,4},{6,7},{7,6},{8,9},{9,8},{10,11... | collective-permute-start | bytes 7077896 | tf_op jit(solution)/shard_map/ppermute | solution.py:61
  408.7 45.2 %collective-permute-start.27 = (bf16[8,2,48,1536]{3,2,1,0:T(8,128)(2,1)}, bf16[8,2,48,1536]{3,2,1,0:T(8,128)(2,1)}, u32[]{:S(2)}, u32[]{:S(2)}) collective-permute-start(bf16[8,2,48,1536]{3,2,1,0:T(8,128)(2,1)} %collective-permute-done.26.refs_2_), channel_id=1, source_target_pairs={{0,1},{1,0},{2,3},{3,2},{4,5},{5,4},{6,7},{7,6},{8,9},{9,8},{10,11... | collective-permute-start | bytes 7077896 | tf_op jit(solution)/shard_map/ppermute | solution.py:61
  465.1 72.2 %collective-permute-start.46 = (bf16[4,2,48,384]{3,2,0,1:T(8,128)(2,1)}, bf16[4,2,48,384]{3,2,0,1:T(8,128)(2,1)}, u32[]{:S(2)}, u32[]{:S(2)}) collective-permute-start(bf16[4,2,48,384]{3,2,0,1:T(8,128)(2,1)} %dynamic-slice_bitcast_fusion.10), channel_id=1, source_target_pairs={{0,16},{2,18},{4,20},{6,22},{8,24},{10,26},{12,28},{14,30},{16,0},... | collective-permute-start | bytes 884744 | tf_op jit(solution)/shard_map/ppermute | solution.py:57
  472.5 77.8 %collective-permute-start.29 = (bf16[2,2,2,2,48,1536]{5,4,0,2,1,3:T(8,128)(2,1)}, bf16[2,2,2,2,48,1536]{5,4,0,2,1,3:T(8,128)(2,1)}, u32[]{:S(2)}, u32[]{:S(2)}) collective-permute-start(bf16[2,2,2,2,48,1536]{5,4,0,2,1,3:T(8,128)(2,1)} %bitcast.199), channel_id=1, source_target_pairs={{0,4},{2,6},{4,0},{6,2},{8,12},{10,14},{12,8},{14,10},{16,20},{18,... | collective-permute-start | bytes 7077896 | tf_op jit(solution)/shard_map/ppermute | solution.py:57
  532.3 50.9 %collective-permute-start.34 = (bf16[1,768,1536]{2,1,0:T(8,128)(2,1)}, bf16[1,768,1536]{2,1,0:T(8,128)(2,1)}, u32[]{:S(2)}, u32[]{:S(2)}) collective-permute-start(bf16[1,768,1536]{2,1,0:T(8,128)(2,1)} %get-tuple-element.284), channel_id=1, source_target_pairs={{0,1},{1,0},{2,3},{3,2},{4,5},{5,4},{6,7},{7,6},{8,9},{9,8},{10,11... | collective-permute-start | bytes 7077896 | tf_op jit(solution)/shard_map/ppermute | solution.py:61
  532.3 50.9 %collective-permute-start.33 = (bf16[1,768,1536]{2,1,0:T(8,128)(2,1)}, bf16[1,768,1536]{2,1,0:T(8,128)(2,1)}, u32[]{:S(2)}, u32[]{:S(2)}) collective-permute-start(bf16[1,768,1536]{2,1,0:T(8,128)(2,1)} %get-tuple-element.285), channel_id=1, source_target_pairs={{0,1},{1,0},{2,3},{3,2},{4,5},{5,4},{6,7},{7,6},{8,9},{9,8},{10,11... | collective-permute-start | bytes 7077896 | tf_op jit(solution)/shard_map/ppermute | solution.py:61
  552.7 40.3 %collective-permute-start.30 = (bf16[2,2,2,48,1536]{4,3,0,2,1:T(8,128)(2,1)S(1)}, bf16[2,2,2,48,1536]{4,3,0,2,1:T(8,128)(2,1)}, u32[]{:S(2)}, u32[]{:S(2)}) collective-permute-start(bf16[2,2,2,48,1536]{4,3,0,2,1:T(8,128)(2,1)S(1)} %dynamic-slice_bitcast_fusion), channel_id=1, source_target_pairs={{0,2},{2,0},{4,6},{6,4},{8,10},{10,8},{12,14},{14,12},{16,18},{18,... | collective-permute-start | bytes 3538952 | tf_op jit(solution)/shard_map/ppermute | solution.py:57
  583.2 139.5 %collective-permute-start.48 = (bf16[4,768,384]{2,1,0:T(8,128)(2,1)}, bf16[4,768,384]{2,1,0:T(8,128)(2,1)}, u32[]{:S(2)}, u32[]{:S(2)}) collective-permute-start(bf16[4,768,384]{2,1,0:T(8,128)(2,1)} %get-tuple-element.157), channel_id=1, source_target_pairs={{0,1},{1,0},{2,3},{3,2},{4,5},{5,4},{6,7},{7,6},{8,9},{9,8},{10,11... | collective-permute-start | bytes 7077896 | tf_op jit(solution)/shard_map/ppermute | solution.py:61
  590.4 58.8 %collective-permute-start.55 = (bf16[1,2,2,2,48,1536]{5,4,2,1,3,0:T(8,128)(2,1)}, bf16[1,2,2,2,48,1536]{5,4,2,1,3,0:T(8,128)(2,1)}, u32[]{:S(2)}, u32[]{:S(2)}) collective-permute-start(bf16[1,2,2,2,48,1536]{5,4,2,1,3,0:T(8,128)(2,1)} %bitcast.201), channel_id=1, source_target_pairs={{0,2},{2,0},{4,6},{6,4},{8,10},{10,8},{12,14},{14,12},{16,18},{18,... | collective-permute-start | bytes 3538952 | tf_op jit(solution)/shard_map/ppermute | solution.py:57
  590.9 64.7 %collective-permute-start.59 = (bf16[1,2,2,2,48,1536]{5,4,2,1,3,0:T(8,128)(2,1)}, bf16[1,2,2,2,48,1536]{5,4,2,1,3,0:T(8,128)(2,1)}, u32[]{:S(2)}, u32[]{:S(2)}) collective-permute-start(bf16[1,2,2,2,48,1536]{5,4,2,1,3,0:T(8,128)(2,1)} %bitcast.200), channel_id=1, source_target_pairs={{0,4},{2,6},{4,0},{6,2},{8,12},{10,14},{12,8},{14,10},{16,20},{18,... | collective-permute-start | bytes 3538952 | tf_op jit(solution)/shard_map/ppermute | solution.py:57
  595.5 73.8 %collective-permute-start.53 = (bf16[2,2,48,1536]{3,2,0,1:T(8,128)(2,1)}, bf16[2,2,48,1536]{3,2,0,1:T(8,128)(2,1)}, u32[]{:S(2)}, u32[]{:S(2)}) collective-permute-start(bf16[2,2,48,1536]{3,2,0,1:T(8,128)(2,1)} %dynamic-slice_bitcast_fusion.3), channel_id=1, source_target_pairs={{0,16},{2,18},{4,20},{6,22},{8,24},{10,26},{12,28},{14,30},{16,0},... | collective-permute-start | bytes 1769480 | tf_op jit(solution)/shard_map/ppermute | solution.py:57
  647.8 69.1 %collective-permute-start.35 = (bf16[2,768,384]{2,1,0:T(8,128)(2,1)}, bf16[2,768,384]{2,1,0:T(8,128)(2,1)}, u32[]{:S(2)}, u32[]{:S(2)}) collective-permute-start(bf16[2,768,384]{2,1,0:T(8,128)(2,1)} %get-tuple-element.295), channel_id=1, source_target_pairs={{0,1},{1,0},{2,3},{3,2},{4,5},{5,4},{6,7},{7,6},{8,9},{9,8},{10,11... | collective-permute-start | bytes 3538952 | tf_op jit(solution)/shard_map/ppermute | solution.py:61
  655.6 61.4 %collective-permute-start.40 = (bf16[2,768,384]{2,1,0:T(8,128)(2,1)}, bf16[2,768,384]{2,1,0:T(8,128)(2,1)}, u32[]{:S(2)}, u32[]{:S(2)}) collective-permute-start(bf16[2,768,384]{2,1,0:T(8,128)(2,1)} %get-tuple-element.296), channel_id=1, source_target_pairs={{0,1},{1,0},{2,3},{3,2},{4,5},{5,4},{6,7},{7,6},{8,9},{9,8},{10,11... | collective-permute-start | bytes 3538952 | tf_op jit(solution)/shard_map/ppermute | solution.py:61
  725.3 40.1 %collective-permute-start.49 = (bf16[4,2,2,2,48,384]{5,4,0,2,1,3:T(8,128)(2,1)S(1)}, bf16[4,2,2,2,48,384]{5,4,0,2,1,3:T(8,128)(2,1)S(1)}, u32[]{:S(2)}, u32[]{:S(2)}) collective-permute-start(bf16[4,2,2,2,48,384]{5,4,0,2,1,3:T(8,128)(2,1)S(1)} %bitcast.227), channel_id=1, source_target_pairs={{0,4},{2,6},{4,0},{6,2},{8,12},{10,14},{12,8},{14,10},{16,20},{18,... | collective-permute-start | bytes 3538952 | tf_op jit(solution)/shard_map/ppermute | solution.py:57
  (147 other events, 2148.4 us)

commit v2 on v1

--- a/solution.py
+++ b/solution.py
@@ -29,10 +29,12 @@
 PAIR = 2 * HEAD_DIM
 TILE = 256
 CHUNK = 32
-FEED = 512
+FEED = 1536
 FEED_ROWS = 64
+BELL = (2.0 * math.pi) ** -0.5
+COST_SCALE = 0.05
+HEAD_SCALE = HEAD_DIM ** (-0.5)
 SQRT_HALF = 0.5**0.5
-BELL = (2.0 * math.pi) ** -0.5
 
 
 def moves(target):
@@ -41,7 +43,8 @@
         for y in range(2):
             for x in range(2):
                 there = target(z, y, x)
-                pairs.append((z * 4 + y * 2 + x, there[0] * 4 + there[1] * 2 + there[2]))
+                if there is not None:
+                    pairs.append((z * 4 + y * 2 + x, there[0] * 4 + there[1] * 2 + there[2]))
     return pairs
 
 
@@ -51,6 +54,9 @@
     4: moves(lambda z, y, x: (z ^ 1, y, x)),
     8: moves(lambda z, y, x: (z ^ 2, y, x)),
 }
+middle = moves(lambda z, y, x: (3 - z, y, x) if z in (1, 2) else None)
+inwards = moves(lambda z, y, x: (z ^ 1, y, x) if z in (0, 3) else None)
+outwards = moves(lambda z, y, x: (z ^ 1, y, x) if z in (1, 2) else None)
 
 
 def send(values, bit):
@@ -77,19 +83,29 @@
     return lax.optimization_barrier((values,) + others)[0]
 
 
-def assemble_kernel(places, spans, place_ref, *refs):
+def assemble_kernel(places, spans, rows, place_ref, *refs):
     pieces, wholes, sem = refs[: len(places)], refs[len(places) : -1], refs[-1]
-    chip, core = place_ref[0], place_ref[1]
-    rows, columns = pieces[0].shape[2], pieces[0].shape[3]
+    columns = pieces[0].shape[3]
+    below = wholes[len(spans)] if len(wholes) > len(spans) else None
     copies = []
-    for piece, (offsets, other) in zip(pieces, places):
-        for number, offset in enumerate(offsets):
-            row = pl.ds(pl.multiple_of((chip ^ offset) * rows, 16), rows)
-            column = pl.ds(pl.multiple_of((core ^ other) * columns, 128), columns)
+    for piece, (first, other) in zip(pieces, places):
+        for number in range(piece.shape[0]):
+            row = pl.ds(pl.multiple_of(place_ref[first + number] * rows, 16), rows)
+            column = pl.ds(pl.multiple_of((place_ref[CHIPS] ^ other) * columns, 128), columns)
             for whole, (start, count) in zip(wholes, spans):
+                if piece.shape[2] == rows:
+                    pairs = [(piece.at[number, pl.ds(start, count)], whole.at[:, row, column])]
+                else:
+                    pairs = [
+                        (piece.at[number, 0, pl.ds(at * rows, rows)], whole.at[at, row, column])
+                        for at in range(start, start + count)
+                    ]
+                copies += [pltpu.make_async_copy(here, there, sem) for here, there in pairs]
+            if below is not None and not other:
+                rest = pl.ds(piece.shape[2] - below.shape[1], below.shape[1])
                 copies.append(
                     pltpu.make_async_copy(
-                        piece.at[number, pl.ds(start, count)], whole.at[:, row, column], sem
+                        piece.at[number, 0, rest], below.at[place_ref[first + number]], sem
                     )
                 )
     for copy in copies:
@@ -98,15 +114,18 @@
         copy.wait()
 
 
-def assemble(pieces, places, spans):
-    _, _, rows, columns = pieces[0].shape
-    place = jnp.stack([lax.axis_index("dp"), lax.axis_index("mp")]).astype(jnp.int32)
+def assemble(pieces, places, spans, rows, place):
+    columns = pieces[0].shape[3]
+    outs = [shape_of((count, rows * CHIPS, columns * 2), low) for _, count in spans]
+    below = pieces[0].shape[2] - rows * sum(count for _, count in spans)
+    if pieces[0].shape[2] != rows:
+        outs.append(shape_of((CHIPS, below, columns), low))
     return pl.pallas_call(
-        functools.partial(assemble_kernel, places, spans),
-        out_shape=[shape_of((count, rows * CHIPS, columns * 2), low) for _, count in spans],
+        functools.partial(assemble_kernel, places, spans, rows),
+        out_shape=outs,
         in_specs=[pl.BlockSpec(memory_space=pltpu.SMEM)]
         + [pl.BlockSpec(memory_space=pl.ANY)] * len(pieces),
-        out_specs=vmem(len(spans)),
+        out_specs=vmem(len(outs)),
         scratch_shapes=[pltpu.SemaphoreType.DMA],
         compiler_params=params_of(24),
         cost_estimate=cost_of(3),
@@ -114,62 +133,141 @@
     )(place, *pieces)
 
 
-def gather_mats(own, order, spans):
-    if lax.axis_size("dp") != CHIPS:
-        whole = lax.all_gather(own, "dp", axis=1, tiled=True)
-        whole = lax.all_gather(whole, "mp", axis=2, tiled=True)
-        return [whole[start : start + count] for start, count in spans]
-    values, offsets = own[None], [0]
-    for bit in order[:-1]:
-        values = jnp.concatenate([values, send(values, bit)])
-        offsets = offsets + [offset ^ bit for offset in offsets]
-    last = send(values, order[-1])
-    far = [offset ^ order[-1] for offset in offsets]
-    pieces = [values, swap_cores(values), last, swap_cores(last)]
-    places = [(offsets, 0), (offsets, 1), (far, 0), (far, 1)]
-    return assemble(pieces, places, spans)
+class Gather:
+    def __init__(self, own):
+        self.staged = lax.axis_size("dp") == CHIPS
+        self.own = own[None]
+        self.last = self.pair = self.mid = self.four = self.own
+
+    def near(self, *gate):
+        if self.staged:
+            own = after(self.own, *gate) if gate else self.own
+            self.pair = self.last = jnp.concatenate([self.own, send(own, 4)])
+
+    def inner(self, *gate):
+        if self.staged:
+            self.mid = self.last = lax.ppermute(after(self.pair, *gate), "dp", middle)
+
+    def outer(self, *gate):
+        if self.staged:
+            out = lax.ppermute(after(self.mid, *gate), "dp", outwards)
+            self.four = self.last = jnp.concatenate([self.pair, self.mid + out])
+
+    def sides(self, *gate):
+        if self.staged:
+            four = after(self.four, *gate)
+            self.by_x, self.by_y = send(four, 1), send(four, 2)
+            self.last = (self.by_x, self.by_y)
+
+    def corner(self, *gate):
+        if self.staged:
+            by_x, by_y = after((self.by_x[:2], self.by_y[2:]), *gate)
+            self.corners = send(by_x, 2), send(by_y, 1)
+            self.last = self.corners
+
+    def most(self, *gate):
+        if self.staged:
+            parts = jnp.concatenate([self.four, self.by_x, self.by_y])
+            self.major = (parts, swap_cores(after(parts, *gate)))
+            self.last = self.major[1]
+
+    def rest(self, *gate):
+        if self.staged:
+            parts = jnp.concatenate(self.corners)
+            self.minor = (parts, swap_cores(after(parts, *gate)))
+            self.last = self.minor[1]
+
+    def place(self):
+        chip = lax.axis_index("dp")
+        z = chip // 4
+        far = jnp.where((z == 1) | (z == 2), 12, 8)
+        four = jnp.stack([chip, chip ^ 4, chip ^ far, chip ^ far ^ 4])
+        return jnp.concatenate(
+            [four, four ^ 1, four ^ 2, four ^ 3, lax.axis_index("mp").reshape(1)]
+        ).astype(jnp.int32)
+
+    def finish(self, spans, rows):
+        if not self.staged:
+            whole = lax.all_gather(self.own[0], "dp", axis=1, tiled=True)
+            whole = lax.all_gather(whole, "mp", axis=2, tiled=True)
+            return [whole[start : start + count] for start, count in spans]
+        pieces, places = [], []
+        for pair, first in zip((self.major, self.minor), (0, 12)):
+            pieces += pair
+            places += [(first, 0), (first, 1)]
+        made = assemble(pieces, places, spans, rows, self.place())
+        self.below = made[-1]
+        return made[: len(spans)]
 
 
 class Scatter:
-    def __init__(self, mine, other, order):
+    def __init__(self, other, gate=()):
         self.staged = lax.axis_size("dp") == CHIPS
-        self.parts = widen(mine) + widen(swap_cores(other))
-        self.order = list(order)
-        self.left = [8, 4, 2, 1]
+        self.raw = []
+        self.arrived = self.last = swap_cores(after(other, *gate))
+
+    def add(self, mine, split):
+        self.total = widen(mine) + widen(self.arrived)
         if self.staged:
-            count, width, columns = self.parts.shape
-            self.parts = self.parts.astype(low)
-            self.parts = self.parts.reshape(count, 2, 2, 2, 2, width // CHIPS, columns)
-
-    def step(self, times=1):
-        for _ in range(times if self.staged else 0):
-            bit = self.order.pop(0)
-            axis = 1 + self.left.index(bit)
-            self.left.remove(bit)
-            kept = pick(self.parts, axis, bit_of(bit))
-            arrived = send(pick(self.parts, axis, 1 - bit_of(bit)), bit)
-            self.parts = widen(kept) + widen(arrived)
-            if self.left:
-                self.parts = self.parts.astype(low)
-        return self.parts
-
-    def finish(self):
+            total = self.total.astype(low)
+            total = total.reshape((-1, 4, 2, 2, total.shape[1] // CHIPS, total.shape[2]))
+            count = total.shape[0]
+            self.parts = [total[: count // 2], total[count // 2 :]] if split else [total]
+            self.last = self.parts
+
+    def side(self, bit, *gate):
+        if not self.staged:
+            return
+        parts, self.raw = [], []
+        for part, way in zip(self.parts, (bit, 3 - bit)):
+            axis = 2 if way == 2 or part.ndim == 5 else 3
+            kept = pick(part, axis, bit_of(way))
+            arrived = send(after(pick(part, axis, 1 - bit_of(way)), *gate), way)
+            self.raw.append(arrived)
+            parts.append((widen(kept) + widen(arrived)).astype(low))
+        if parts[0].ndim == 4:
+            whole = parts[0] if len(parts) == 1 else jnp.concatenate(parts)
+            whole = whole.reshape((whole.shape[0], 2, 2) + whole.shape[2:])
+            self.own = pick(whole, 1, bit_of(8))
+            self.far = pick(whole, 1, 1 - bit_of(8))
+            self.last = (self.own, self.far)
+        else:
+            self.parts = self.last = parts
+
+    def join(self, narrow):
         if self.staged:
-            return self.step(len(self.order))
-        return lax.psum_scatter(self.parts, "dp", scatter_dimension=1, tiled=True)
-
-
-def gather_small(values):
-    if lax.axis_size("dp") != CHIPS:
-        return lax.all_gather(values, "dp", axis=0, tiled=False)
-    values = values[None]
-    for bit in (1, 2, 4, 8):
-        there = send(values, bit)
-        at_zero = bit_of(bit) == 0
-        values = jnp.concatenate(
-            [jnp.where(at_zero, values, there), jnp.where(at_zero, there, values)]
-        )
-    return values
+            columns = narrow.own.shape[-1]
+
+            def cut(values):
+                return [values[..., at : at + columns] for at in range(0, values.shape[-1], columns)]
+
+            self.own = jnp.concatenate(cut(self.own) + [narrow.own])
+            self.far = jnp.concatenate(cut(self.far) + [narrow.far])
+            self.last = (self.own, self.far)
+
+    def outer(self, *gate):
+        if self.staged:
+            arrived = lax.ppermute(after(self.far, *gate), "dp", inwards)
+            self.far = self.last = (widen(self.far) + widen(arrived)).astype(low)
+
+    def inner(self, *gate):
+        if self.staged:
+            arrived = lax.ppermute(after(self.far, *gate), "dp", middle)
+            self.own = self.last = (widen(self.own) + widen(arrived)).astype(low)
+
+    def near(self, *gate):
+        if not self.staged:
+            return lax.psum_scatter(self.total, "dp", scatter_dimension=1, tiled=True)
+        arrived = send(after(pick(self.own, 1, 1 - bit_of(4)), *gate), 4)
+        return widen(pick(self.own, 1, bit_of(4))) + widen(arrived)
+
+
+def three_terms(values):
+    terms = []
+    for _ in range(3):
+        terms.append(values.astype(low))
+        values = values - lax.reduce_precision(values, 8, 7)
+    return jnp.stack(terms)
 
 
 def scatter_small(values):
@@ -248,7 +346,7 @@
 
 def pair_forward(queries, keys, values, bias):
     count = keys.shape[0]
-    scores = dot_nt(stack_heads(keys), queries) * HEAD_DIM ** (-0.5)
+    scores = dot_nt(stack_heads(keys), queries * HEAD_SCALE)
     weights, totals = [], []
     for part in (scores[:count] + bias, scores[count:] + bias):
         top = jnp.max(part, axis=0, keepdims=True)
@@ -263,7 +361,8 @@
 def pair_backward(queries, keys, values, grad, bias, totals):
     count = keys.shape[0]
     both_keys = stack_heads(keys)
-    scores = dot_nt(both_keys, queries) * HEAD_DIM ** (-0.5)
+    queries = queries * HEAD_SCALE
+    scores = dot_nt(both_keys, queries)
     sensed = dot_nt(stack_heads(values), grad)
     weights, slopes = [], []
     for part, sense, total in (
@@ -277,7 +376,7 @@
     weights = jnp.concatenate(weights, axis=0)
     slopes = jnp.concatenate(slopes, axis=0)
     grad_queries = (dot_tn(slopes, both_keys) * HEAD_DIM ** (-0.5)).astype(low)
-    grad_keys = (merge_heads(dot_nn(slopes, queries)) * HEAD_DIM ** (-0.5)).astype(low)
+    grad_keys = merge_heads(dot_nn(slopes, queries)).astype(low)
     grad_values = merge_heads(dot_nn(weights, grad)).astype(low)
     return grad_queries, grad_keys, grad_values
 
@@ -367,6 +466,27 @@
         lax.fori_loop(0, size * groups // CHUNK, one_chunk, 0)
 
 
+def add_inputs(streams, groups, weights, grads, grad_in):
+    dq_ref, dk_ref, dv_ref = grads
+    for index, (start, size) in enumerate(streams):
+        span = slice(start, start + size * groups)
+        for at, wide in tiles_of(dq_ref.shape[1]):
+            grad_in[index][:, at : at + wide] += (
+                dot_nt(dq_ref[span, :], weights[0][at : at + wide, :])
+                + dot_nt(dk_ref[span, :], weights[1][at : at + wide, :])
+                + dot_nt(dv_ref[span, :], weights[2][at : at + wide, :])
+            )
+
+
+def cross_inputs(plan, dq_ref, dk_ref, dv_ref, mat_ref, *refs):
+    streams = plan["streams"]
+    grads, outs = refs[: len(streams)], refs[len(streams) :]
+    for grad, out in zip(grads, outs):
+        out[...] = grad[...]
+    weights = [mat_ref.at[i] for i in range(3)]
+    add_inputs(streams, plan["groups"], weights, (dq_ref, dk_ref, dv_ref), outs)
+
+
 def attend_back(plan, *refs):
     streams, relations = plan["streams"], plan["relations"]
     refs = list(refs)
@@ -390,7 +510,8 @@
     mine = take(plan["mats"])
     other = take(plan["mats"])
     (small_ref,) = take(1)
-    do_ref, dctx_ref, dq_ref, dk_ref, dv_ref = take(5)
+    dq_ref, dk_ref, dv_ref = take(3)
+    do_ref, dctx_ref = take(2)
     width = x_ref.shape[1]
     half = width // 2
     each = 4 // plan["mats"]
@@ -446,13 +567,15 @@
     lax.fori_loop(0, groups, one_group, 0)
     at_zero = core_ref[0] == 0
     rows = x_ref[...]
-    context = ctx_ref[...]
+    last = None
     for number, (left, right) in enumerate(
         ((rows, dq_ref), (rows, dk_ref), (rows, dv_ref), (sent, ctx_ref))
     ):
         wide = right[...]
+        if left is not last:
+            flipped, last = left.T, left
         for at, size in tiles_of(width):
-            whole = dot_tn(left[:, at : at + size], wide).astype(low)
+            whole = dot_nn(flipped[at : at + size, :], wide).astype(low)
             former, latter = whole[:, :half], whole[:, half:]
             mine[number // each][number % each, at : at + size, :] = jnp.where(
                 at_zero, former, latter
@@ -460,14 +583,8 @@
             other[number // each][number % each, at : at + size, :] = jnp.where(
                 at_zero, latter, former
             )
-    for index, (start, size) in enumerate(streams):
-        span = slice(start, start + size * groups)
-        for at, wide in tiles_of(width):
-            grad_in[index][:, at : at + wide] += (
-                dot_nt(dq_ref[span, :], weights[0][at : at + wide, :])
-                + dot_nt(dk_ref[span, :], weights[1][at : at + wide, :])
-                + dot_nt(dv_ref[span, :], weights[2][at : at + wide, :])
-            )
+    if not plan["cross"]:
+        add_inputs(streams, groups, weights, (dq_ref, dk_ref, dv_ref), grad_in)
 
     def add_chunk(step, sums):
         here = row_block(0, CHUNK, step)
@@ -491,7 +608,7 @@
 
 
 def cost_of(micros):
-    return pl.CostEstimate(flops=int(micros * 1.15e9), bytes_accessed=1 << 20, transcendentals=0)
+    return pl.CostEstimate(flops=int(micros * COST_SCALE * 1.15e9), bytes_accessed=1 << 20, transcendentals=0)
 
 
 def params_of(mib):
@@ -516,7 +633,7 @@
         "shift": shift,
         "rows": [3 * layer, 3 * layer + 1, 3 * layer + 2],
         "before": (0, 11),
-        "carried": 1 if layer == 0 else 2,
+        "carried": 1 if layer == 0 else 3,
     }
 
 
@@ -556,14 +673,16 @@
     grads = [shape_of(mat.shape[:2] + (width // 2,), low) for mat in mats]
     outs = [shape_of((count, width), jnp.float32) for count in counts] + grads + grads
     outs.append(shape_of((8, width), jnp.float32))
+    pieces = [shape_of((rows, width), low)] * 3
+    cross = plan["cross"]
     args = [part for parts in carried for part in parts] + list(normed) + list(inverse) + [x]
     args += list(mats) + [gains, key_bias] + list(same) + list(kept)
     results = pl.pallas_call(
         functools.partial(attend_back, plan),
-        out_shape=outs,
+        out_shape=outs + (pieces if cross else []),
         in_specs=[pl.BlockSpec(memory_space=pltpu.SMEM)] + vmem(len(args)),
-        out_specs=vmem(len(outs)),
-        scratch_shapes=[pltpu.VMEM((rows, width), low)] * 5,
+        out_specs=vmem(len(outs) + (3 if cross else 0)),
+        scratch_shapes=[pltpu.VMEM((rows, width), low)] * (2 if cross else 5),
         compiler_params=params_of(56),
         name="attend_back",
     )(core, *args)
@@ -572,25 +691,37 @@
         results[:many],
         results[many : many + count],
         results[many + count : many + 2 * count],
-        results[-1],
+        results[len(outs) - 1],
+        results[len(outs) :],
     )
 
 
-def feed_up(line, x_ref, mat_ref, bias_ref, h_ref, slope_ref):
+def run_cross_inputs(plan, pieces, mat, grads):
+    outs = [shape_of(grad.shape, jnp.float32) for grad in grads]
+    return pl.pallas_call(
+        functools.partial(cross_inputs, plan),
+        out_shape=outs,
+        in_specs=vmem(4 + len(grads)),
+        out_specs=vmem(len(grads)),
+        compiler_params=params_of(48),
+        cost_estimate=cost_of(10),
+        name="cross_inputs",
+    )(*pieces, mat, *grads)
+
+
+def feed_up(line, x_ref, mat_ref, bias_ref, h_ref, slope_ref, hidden_ref):
     bias = bias_ref[line : line + 1, :]
-    weight = mat_ref[0]
-    rows = x_ref.shape[0]
-    block = min(FEED_ROWS, rows)
+    hidden_ref[...] = dot_nn(x_ref[...], mat_ref[0])
 
     def one_chunk(step, carry):
-        here = row_block(0, block, step)
-        hidden = dot_nn(x_ref[here, :], weight) + bias
+        here = row_block(0, FEED_ROWS, step)
+        hidden = hidden_ref[here, :] + bias
         share = 0.5 + 0.5 * lax.erf(hidden * SQRT_HALF)
         h_ref[here, :] = (hidden * share).astype(low)
         slope_ref[here, :] = (share + hidden * (jnp.exp(hidden * hidden * -0.5) * BELL)).astype(low)
         return carry
 
-    lax.fori_loop(0, rows // block, one_chunk, 0)
+    lax.fori_loop(0, x_ref.shape[0] // FEED_ROWS, one_chunk, 0)
 
 
 def feed_down(plan, h_ref, mat_ref, gain_ref, bias_ref, unit_ref, cot_ref, live_ref, *refs):
@@ -641,16 +772,19 @@
 
 
 def feed_back(core_ref, do_ref, x_ref, h_ref, slope_ref, up_ref, down_ref, *refs):
-    dx_ref, mine, other, line_ref = refs
+    dx_ref, grad_ref, line_ref, sent_flip, rows_flip = refs
     step = pl.program_id(0)
     sent = do_ref[...]
-    rows = x_ref[...]
+
+    @pl.when(step == 0)
+    def _():
+        sent_flip[...] = sent.T
+        rows_flip[...] = x_ref[...].T
+
     slope = (dot_nn(sent, down_ref[0]) * widen(slope_ref[...])).astype(low)
-    line_ref[...] = jnp.broadcast_to(
-        close_rows(fold_rows(widen(slope))), line_ref.shape
-    )
-    grad_up = dot_tn(rows, slope).astype(low)
-    grad_down = dot_tn(sent, h_ref[...]).astype(low)
+    line_ref[...] = jnp.broadcast_to(close_rows(fold_rows(widen(slope))), line_ref.shape)
+    grad_ref[0] = dot_nn(rows_flip[...], slope).astype(low)
+    grad_ref[1] = dot_nn(sent_flip[...], h_ref[...]).astype(low)
     part = dot_nt(slope, up_ref[0])
 
     @pl.when(step == 0)
@@ -660,16 +794,6 @@
     @pl.when(step > 0)
     def _():
         dx_ref[...] += part
-
-    @pl.when(step < pl.num_programs(0) // 2)
-    def _():
-        other[0] = grad_up
-        other[1] = grad_down
-
-    @pl.when(step >= pl.num_programs(0) // 2)
-    def _():
-        mine[0] = grad_up
-        mine[1] = grad_down
 
 
 def run_up(stream, x, mat, biases):
@@ -686,6 +810,7 @@
             pl.BlockSpec((2, FEED), wide),
         ],
         out_specs=[pl.BlockSpec((rows, FEED), wide)] * 2,
+        scratch_shapes=[pltpu.VMEM((rows, FEED), jnp.float32)],
         compiler_params=params_of(32),
         cost_estimate=cost_of(0.033 * rows),
         name="feed_up",
@@ -727,14 +852,14 @@
     )(h, mat, gains, biases, unit, cot, live)
 
 
-def run_feed_back(core, sent, x, h, slope, up, down):
+def run_feed_back(core, flip, sent, x, h, slope, up, down):
     rows, hidden = h.shape
     width = x.shape[1]
-    steps = hidden // FEED
-    half = steps // 2
+    steps = hidden // FEED // 2
 
     def chunk(step, core_ref):
-        return (step + half * (1 - core_ref[0])) % steps
+        side = core_ref[0]
+        return step + steps * (1 - side if flip else side)
 
     def wide(step, core_ref):
         return (0, chunk(step, core_ref))
@@ -743,9 +868,6 @@
         return (0, 0, chunk(step, core_ref))
 
     fixed = lambda step, core_ref: (0, 0)
-    late = pl.BlockSpec((2, width, FEED), lambda step, core_ref: (0, 0, jnp.maximum(step - half, 0)))
-    early = pl.BlockSpec((2, width, FEED), lambda step, core_ref: (0, 0, jnp.minimum(step, half - 1)))
-    part = shape_of((2, width, hidden // 2), low)
     return pl.pallas_call(
         feed_back,
         grid_spec=pltpu.PrefetchScalarGridSpec(
@@ -761,19 +883,18 @@
             ],
             out_specs=[
                 pl.BlockSpec((rows, width), fixed),
-                late,
-                early,
-                pl.BlockSpec((8, FEED), wide),
+                pl.BlockSpec((2, width, FEED), lambda step, core_ref: (0, 0, step)),
+                pl.BlockSpec((8, FEED), lambda step, core_ref: (0, step)),
             ],
+            scratch_shapes=[pltpu.VMEM((width, rows), low)] * 2,
         ),
         out_shape=[
             shape_of((rows, width), jnp.float32),
-            part,
-            part,
-            shape_of((8, hidden), jnp.float32),
+            shape_of((2, width, hidden // 2), low),
+            shape_of((8, hidden // 2), jnp.float32),
         ],
         compiler_params=params_of(40),
-        cost_estimate=cost_of(0.04 * rows),
+        cost_estimate=cost_of(0.02 * rows),
         name="feed_back",
     )(core, sent, x, h, slope, up, down)
 
@@ -826,25 +947,55 @@
     small_own = jnp.concatenate([gains.reshape(-1), biases.reshape(-1), bias_up.reshape(-1)])
     small_size = small_own.shape[0]
     padded = -(-small_size // 1024) * 1024
-    small_all = gather_small(jnp.pad(small_own, (0, padded - small_size)).reshape(-1, 128))
-    small_all = small_all.reshape(small_all.shape[0], padded)
+    staged = lax.axis_size("dp") == CHIPS
     cuts = (5 * model_share, 21 * model_share)
 
     def spread(columns, count):
         parts = columns.reshape(columns.shape[0], count, -1)
         return parts.transpose(1, 0, 2).reshape(count, -1)
 
+    attn_low = attn_w.astype(low)
+    ffn_low = ffn_w.astype(low)
+    share, columns = attn_w.shape[2:]
+    if staged:
+        terms = three_terms(small_own).reshape(-1)
+        tall = -(-terms.shape[0] // (16 * columns)) * 16
+        terms = jnp.pad(terms, (0, tall * columns - terms.shape[0])).reshape(tall, columns)
+        own = jnp.concatenate([attn_low[0].reshape(-1, columns), terms])[None]
+    else:
+        own = attn_low[0]
+    first, second, third, fourth = [
+        Gather(own),
+        Gather(attn_low[1:].reshape((-1,) + attn_low.shape[2:])),
+        Gather(ffn_low[0]),
+        Gather(ffn_low[1]),
+    ]
+    first.near()
+    second.near(first.last)
+    first.inner()
+    third.near(first.last)
+    second.inner(first.last)
+    first.outer()
+    fourth.near(first.last)
+    first.sides()
+    second.outer(first.four)
+    third.inner(second.last)
+    third.outer(second.last)
+    fourth.inner(third.mid)
+    first.corner()
+    second.sides(first.last)
+    first.most()
+    first.rest()
+    cross_mats = first.finish([(0, 4)], share)
+    if staged:
+        arrived = widen(first.below).reshape(CHIPS, -1)
+        arrived = arrived[:, : 3 * small_size].reshape(CHIPS, 3, small_size)
+        small_all = arrived[:, 0] + arrived[:, 1] + arrived[:, 2]
+    else:
+        small_all = lax.all_gather(small_own, "dp", axis=0, tiled=False)
     gain_all = spread(small_all[:, : cuts[0]], 5)
     bias_all = spread(small_all[:, cuts[0] : cuts[1]], 16)
     up_all = spread(small_all[:, cuts[1] : small_size], 2)
-    attn_low = attn_w.astype(low)
-    ffn_low = ffn_w.astype(low)
-    forth, back = (4, 8, 1, 2), (4, 8, 2, 1)
-    cross_mats = gather_mats(attn_low[0], forth, [(0, 4)])
-    self_mats = gather_mats(attn_low[1:].reshape((-1,) + attn_low.shape[2:]), back, [(0, 4), (4, 4)])
-    word_mats = gather_mats(ffn_low[0], forth, [(0, 1), (1, 1)])
-    region_mats = gather_mats(ffn_low[1], back, [(0, 1), (1, 1)])
-    up_mats, down_mats = zip(word_mats, region_mats)
 
     core = core_index.astype(jnp.int32).reshape(1)
     slots = (words, regions)
@@ -866,9 +1017,20 @@
 
     cross_plan = layer_plan(0, sizes, groups, 1)
     cross_same = [same_item(1, 0), same_item(0, 1)]
+    gains_first = after(gain_all, second.last, third.four, fourth.mid)
     cross_kept, unit_one, scale_one, low_one = run_front(
-        cross_plan, x_all, None, cross_mats, gain_all, bias_all, key_all, cross_same
+        cross_plan, x_all, None, cross_mats, gains_first, bias_all, key_all, cross_same
     )
+    second.corner()
+    third.sides(second.by_x if staged else second.last)
+    fourth.outer()
+    window = (scale_one, second.last, third.last, fourth.last)
+    second.most(*window)
+    second.rest(*window)
+    self_mats = second.finish([(0, 4), (4, 4)], share)
+    third.corner(*window)
+    fourth.sides(*window)
+    fronts_gate = (fourth.four,) if staged else ()
     self_plans = [layer_plan(1 + stream, (sizes[stream],), groups, 1) for stream in range(2)]
     self_same = [[same_item(stream, stream)] for stream in range(2)]
     yx, xy = (2, 1, 8, 4), (1, 2, 8, 4)
@@ -879,7 +1041,7 @@
             low_one[stream],
             unit_one[stream],
             [self_mats[stream]],
-            gain_all,
+            after(gain_all, *fronts_gate),
             bias_all,
             key_bias[stream],
             self_same[stream],
@@ -887,13 +1049,13 @@
         return kept, unit[0], scale[0], lowered[0]
 
     def go_feed(stream, made, gate):
-        return run_up(stream, made[3], up_mats[stream], after(up_all, *gate))
+        return run_up(stream, made[3], mats_of[stream][0], after(up_all, *gate))
 
     def go_down(stream, made, up):
         out, grad, sent, small = run_down(
             stream,
             up[0],
-            down_mats[stream],
+            mats_of[stream][1],
             gain_all,
             bias_all,
             made[1],
@@ -902,16 +1064,16 @@
         )
         return out.reshape(items, slots[stream], width), grad, sent, small
 
-    def go_feed_back(stream, made, up, down):
+    def go_feed_back(flip, stream, made, up, down, gate):
         return run_feed_back(
-            core, down[2], made[3], *up, up_mats[stream], down_mats[stream]
+            after(core, *gate), flip, down[2], made[3], *up, *mats_of[stream]
         )
 
     def go_back(stream, made, down, feed, gate):
         return run_back(
             self_plans[stream],
             after(core, *gate),
-            [[down[1], feed[0]]],
+            [[down[1], feed[0], feed[1]]],
             [made[1]],
             [made[2]],
             low_one[stream],
@@ -922,33 +1084,55 @@
             made[0],
         )
 
+    region_made = go_up(1)
     word_made = go_up(0)
+    window = (word_made[2], region_made[2], third.last, fourth.last)
+    third.most(*window)
+    third.rest(*window)
+    fourth.corner(*window)
+    word_mats = third.finish([(0, 1), (1, 1)], share)
+    mats_of = [word_mats]
     word_up = go_feed(0, word_made, ())
     word_down = go_down(0, word_made, word_up)
-    word_feed = go_feed_back(0, word_made, word_up, word_down)
-    word_ring = Scatter(word_feed[1], word_feed[2], yx)
-    word_back = go_back(0, word_made, word_down, word_feed, ())
-    word_self_ring = Scatter(word_back[1][0], word_back[2][0], xy)
-    region_made = go_up(1)
-    region_up = go_feed(1, region_made, (word_ring.parts,))
-    word_ring.step()
+    corners = fourth.last
+    word_far = go_feed_back(True, 0, word_made, word_up, word_down, (corners,))
+    word_ring = Scatter(word_far[1])
+    word_own = go_feed_back(False, 0, word_made, word_up, word_down, (word_far[2],))
+    word_ring.add(word_own[1], True)
+    fourth.most(word_own[2])
+    fourth.rest(word_own[2])
+    mats_of.append(fourth.finish([(0, 1), (1, 1)], share))
+    word_back = go_back(
+        0, word_made, word_down, (word_far[0], word_own[0]), (word_ring.last, corners)
+    )
+    word_ring.side(1)
+    word_self_ring = Scatter(word_back[2][0])
+    region_up = go_feed(1, region_made, (word_self_ring.last,))
+    word_self_ring.add(word_back[1][0], True)
     region_down = go_down(1, region_made, region_up)
-    region_feed = go_feed_back(1, region_made, region_up, region_down)
+    window = (region_down[3], word_ring.raw)
+    region_far = go_feed_back(True, 1, region_made, region_up, region_down, (word_ring.raw,))
+    word_ring.side(2, *window)
+    word_self_ring.side(1, *window)
+    region_ring = Scatter(region_far[1])
+    region_own = go_feed_back(
+        False, 1, region_made, region_up, region_down, (region_far[2],)
+    )
+    region_ring.add(region_own[1], True)
     region_back = go_back(
-        1, region_made, region_down, region_feed, (word_ring.parts, word_self_ring.parts)
+        1, region_made, region_down, (region_far[0], region_own[0]), (region_ring.last,)
     )
-    region_rings = [
-        Scatter(region_feed[1][part : part + 1], region_feed[2][part : part + 1], order)
-        for part, order in enumerate((xy, yx))
-    ]
-    word_ring.step()
-    word_self_ring.step()
-    region_self_ring = Scatter(region_back[1][0], region_back[2][0], yx)
-    grads_in, mine, other, cross_small = run_back(
+    window = (region_own[2], word_ring.raw, word_self_ring.raw)
+    region_ring.side(1, *window)
+    word_self_ring.side(2, *window)
+    word_ring.join(word_self_ring)
+    word_ring.outer(region_back[3])
+    region_self_ring = Scatter(region_back[2][0], region_ring.raw + word_self_ring.raw)
+    swapped = region_self_ring.arrived
+    region_self_ring.add(region_back[1][0], True)
+    units, mine, other, cross_small, pieces = run_back(
         cross_plan,
-        after(
-            core, word_ring.parts, word_self_ring.parts, *[ring.parts for ring in region_rings]
-        ),
+        after(core, region_self_ring.last),
         [[word_back[0][0]], [region_back[0][0]]],
         unit_one,
         scale_one,
@@ -959,29 +1143,57 @@
         cross_same,
         cross_kept,
     )
+    region_ring.side(2, swapped)
+    region_self_ring.side(1)
+    cross_ring = Scatter(other[0], region_ring.raw + region_self_ring.raw)
+    region_self_ring.side(2, cross_small)
+    region_ring.outer(cross_small)
+    word_ring.inner(cross_small)
+    cross_ring.add(mine[0], True)
+    grads_in = run_cross_inputs(
+        cross_plan, pieces, cross_mats[0], after(units, cross_ring.last)
+    )
+    cross_ring.side(1)
+    small_gate = (cross_ring.raw, grads_in[0])
+    word_shard = word_ring.near(*small_gate)
+    region_ring.inner(*small_gate)
+    region_self_ring.outer(*small_gate)
+    cross_ring.side(2, *small_gate)
+    region_self_ring.inner()
+    cross_ring.outer()
+    cross_ring.inner()
+    if staged:
+        wide = ffn_w.shape[3] // columns * 2
+        parts = [word_shard[at : at + 2] for at in range(0, wide, 2)]
+        word_shard, word_self_shard = jnp.concatenate(parts, axis=-1), word_shard[wide:]
+    else:
+        word_self_shard = word_self_ring.near()
+    attn_shard = jnp.stack([cross_ring.near(), word_self_shard, region_self_ring.near()])
+    ffn_shard = jnp.stack([word_shard, region_ring.near()])
     outputs = [word_down[0], region_down[0]]
     downs = [word_down[1:], region_down[1:]]
-    feeds = [word_feed, region_feed]
+    feeds = [(word_far, word_own), (region_far, region_own)]
     self_small = [word_back[3], region_back[3]]
     grad_lang = grads_in[0].reshape(lang.shape)
     grad_vis = grads_in[1].reshape(vis.shape)
-    cross_rings = [
-        Scatter(mine[0][part : part + 2], other[0][part : part + 2], order)
-        for part, order in ((0, xy), (2, yx))
-    ]
-    region_shard = jnp.concatenate([ring.finish() for ring in region_rings])
-    cross_shard = jnp.concatenate([ring.finish() for ring in cross_rings])
-    attn_shard = jnp.stack([cross_shard, word_self_ring.finish(), region_self_ring.finish()])
-    ffn_shard = jnp.stack([word_ring.finish(), region_shard])
-
-    layers = [cross_small, self_small[0], self_small[1]]
+
+    layers = [after(part, small_gate) for part in (cross_small, self_small[0], self_small[1])]
     gain_rows = [part[0:1] for part in layers] + [part[2][0:1] for part in downs]
     bias_rows = []
     for part in layers:
         bias_rows += [part[3:5], part[2:3]]
     bias_rows += [part[2][2:3] for part in downs]
     bias_rows += [part[1:2] for part in layers] + [part[2][1:2] for part in downs]
-    up_rows = [part[3][0:1] for part in feeds]
+    up_rows = []
+    for far, own in feeds:
+        lines = far[2][0:1], own[2][0:1]
+        up_rows.append(
+            jnp.where(
+                core_index == 0,
+                jnp.concatenate([lines[1], lines[0]], axis=1),
+                jnp.concatenate([lines[0], lines[1]], axis=1),
+            )
+        )
 
     def split(rows, share):
         rows = jnp.concatenate(rows)

time: 836 us -> 653 us (0.78)
  waiting for transfers between devices: 348 us -> 82.1 us
  starting transfers between devices: 73.1 us -> 124 us
  local copies, waits for them, and re-layouts: 101 us -> 136 us
  Pallas kernels: 237 us -> 224 us
    ppermute x56 -> x52, waiting for transfers between devices: 347 us -> 56.7 us  [send(): return lax.ppermute(values, 'dp', routes[bit])]
    ppermute x0 -> x16, starting transfers between devices: none -> 39.4 us  [the longest x4 24.4 us: outer(): arrived = lax.ppermute(after(self.far, *gate), 'dp', inwards)]
    unnamed x224 -> x331, local copies, waits for them, and re-layouts: 42.6 us -> 68.6 us
    ppermute x0 -> x16, waiting for transfers between devices: none -> 25 us  [the longest x4 15.5 us: outer(): out = lax.ppermute(after(self.mid, *gate), 'dp', outwards)]
    pallas_call x2, Pallas kernels: 29.2 us -> 11.7 us  [run_up(): pl.pallas_call(functools.partial(feed_up, stream), grid=(hidden // FEED,)...]
    ppermute x56 -> x52, starting transfers between devices: 69.1 us -> 82 us  [send(): return lax.ppermute(values, 'dp', routes[bit])]
    concatenate x0 -> x18, local copies, waits for them, and re-layouts: none -> 11.5 us  [the longest x4 4.93 us: most(): parts = jnp.concatenate([self.four, self.by_x, self.by_y])]
    unnamed x3 -> x6, other arithmetic: 0.01 us -> 8.47 us
  transfers between devices with their start and end apart: 73 -> 83, of which waited for: 32 -> 26; matrix products, arithmetic and copies ran while one was open for 15% -> 23% of each run, Pallas kernels for 29% -> 26%
where the time goes in v2:
time: 653 us; the launch traced here: 645 us
  Pallas kernels  224 us (34%)
  local copies, waits for them, and re-layouts  136 us (21%)
  starting transfers between devices  124 us (19%)
  waiting for transfers between devices  82.1 us (13%)
  other arithmetic  69.5 us (11%)
  between operations  9.87 us (2%)
    pallas_call x3, Pallas kernels, run_back(): pl.pallas_call(functools.partial(attend_back, plan), out_shape=outs + (pi...  85.6 us
    ppermute x52, starting transfers between devices, send(): return lax.ppermute(values, 'dp', routes[bit])  82 us
    unnamed x331, local copies, waits for them, and re-layouts  68.6 us
    ppermute x52, waiting for transfers between devices, send(): return lax.ppermute(values, 'dp', routes[bit])  56.7 us
    pallas_call x3, Pallas kernels, run_front(): pl.pallas_call(functools.partial(attend_front, plan), out_shape=outs, in_...  50.2 us
    pallas_call x4, Pallas kernels, run_feed_back(): pl.pallas_call(feed_back, grid_spec=pltpu.PrefetchScalarGridSpec(num_scal...  38.4 us
    ppermute x4, starting transfers between devices, outer(): arrived = lax.ppermute(after(self.far, *gate), 'dp', inwards)  24.4 us
    convert_element_type x20, other arithmetic, side(): parts.append((widen(kept) + widen(arrived)).astype(low))  18.8 us
  transfers between devices with their start and end apart: 83, of which 26 were waited for; matrix products, arithmetic and copies ran while one was open for 23% of the time, Pallas kernels for 26%

profile of v2, /device:TPU:0, one launch (start us, length us, event | category | flops | bytes accessed | tf_op | source)
XLA Modules:
  0.0 644.9 jit_solution(16745320146007134381)
XLA Ops:
  22.6 8.5 %collective-permute-start.14 = (bf16[1,2,48,1536]{3,2,1,0:T(8,128)(2,1)}, bf16[1,2,48,1536]{3,2,1,0:T(8,128)(2,1)S(1)}, u32[]{:S(2)}, u32[]{:S(2)}) collective-permute-start(bf16[1,2,48,1536]{3,2,1,0:T(8,128)(2,1)} %get-tuple-element.173), channel_id=1, source_target_pairs={{0,8},{2,10},{4,12},{6,14},{8,0},{10,2},{12,4},{14,6},{16,24},{18,... | collective-permute-start | bytes 884744 | tf_op jit(solution)/shard_map/ppermute | solution.py:63
  31.1 3.9 collective-permute-done.2
  50.4 6.3 collective-permute-start.17
  79.0 11.6 %collective-permute-done.16 = bf16[2,2,48,1536]{3,2,1,0:T(8,128)(2,1)S(1)} collective-permute-done((bf16[2,2,48,1536]{3,2,1,0:T(8,128)(2,1)}, bf16[2,2,48,1536]{3,2,1,0:T(8,128)(2,1)S(1)}, u32[]{:S(2)}, u32[]{:S(2)}) %collective-permute-start.16) | collective-permute-done | bytes 589856 | tf_op jit(solution)/shard_map/ppermute | solution.py:153
  96.2 6.9 %collective-permute-done.12 = bf16[4,8,48,384]{3,2,1,0:T(8,128)(2,1)S(1)} collective-permute-done((bf16[4,8,48,384]{3,2,1,0:T(8,128)(2,1)S(1)}, bf16[4,8,48,384]{3,2,1,0:T(8,128)(2,1)S(1)}, u32[]{:S(2)}, u32[]{:S(2)}) %collective-permute-start.12) | collective-permute-done | bytes 1179680 | tf_op jit(solution)/shard_map/ppermute | solution.py:63
  116.6 25.4 %attend_front.3 = (bf16[896,768]{1,0:T(8,128)(2,1)S(1)}, bf16[896,768]{1,0:T(8,128)(2,1)}, bf16[896,768]{1,0:T(8,128)(2,1)}, bf16[896,768]{1,0:T(8,128)(2,1)}, f...) custom-call(bf16[896,768]{1,0:T(8,128)(2,1)} %constant_dynamic-updat, ...), custom_call_target="tpu_custom_call" | custom-call | flops 1442560000 | bytes 1048576 | tf_op jit(solution)/shard_map/attend_front/pallas_call | solution.py:654
  172.9 8.6 %attend_front.4 = (bf16[320,768]{1,0:T(8,128)(2,1)S(1)}, bf16[320,768]{1,0:T(8,128)(2,1)S(1)}, bf16[320,768]{1,0:T(8,128)(2,1)S(1)}, bf16[320,768]{1,0:T(8,128)(...) custom-call(bf16[320,768]{1,0:T(8,128)(2,1)S(1)} %get-tuple-element., ...), custom_call_target="tpu_custom_call" | custom-call | flops 515200000 | bytes 1048576 | tf_op jit(solution)/shard_map/attend_front/pallas_call | solution.py:654
  186.9 16.2 %attend_front.5 = (bf16[576,768]{1,0:T(8,128)(2,1)S(1)}, bf16[576,768]{1,0:T(8,128)(2,1)S(1)}, bf16[576,768]{1,0:T(8,128)(2,1)S(1)}, bf16[576,768]{1,0:T(8,128)(...) custom-call(bf16[576,768]{1,0:T(8,128)(2,1)S(1)} %get-tuple-element., ...), custom_call_target="tpu_custom_call" | custom-call | flops 927360000 | bytes 1048576 | tf_op jit(solution)/shard_map/attend_front/pallas_call | solution.py:654
  213.4 12.2 %collective-permute-done.32 = bf16[2,2,48,1536]{3,2,1,0:T(8,128)(2,1)} collective-permute-done((bf16[2,2,48,1536]{3,2,1,0:T(8,128)(2,1)}, bf16[2,2,48,1536]{3,2,1,0:T(8,128)(2,1)}, u32[]{:S(2)}, u32[]{:S(2)}) %collective-permute-start.32) | collective-permute-done | bytes 589856 | tf_op jit(solution)/shard_map/ppermute | solution.py:63
  229.4 4.4 feed_up.2
  233.9 6.1 feed_down.2
  242.3 9.0 %feed_back.4 = (f32[320,768]{1,0:T(8,128)S(1)}, bf16[2,768,1536]{2,1,0:T(8,128)(2,1)}, f32[8,1536]{1,0:T(8,128)S(1)}) custom-call(s32[1]{0:T(128)} %bitcast.4.core_ref.refs_0_, bf16[320,768]{1,0:T(8,128)(2,1)S(1)} %get-tuple-element.210.do_ref, bf16[320,768]{1,0:T(8,128)(2,1)S(1)} %get-tuple-element.190.x_ref, ...), custom_call_target="tpu_custom_call" | custom-call | flops 368000000 | bytes 1048576 | tf_op jit(solution)/shard_map/feed_back/pallas_call | solution.py:871
  257.7 6.7 %feed_back.5 = (f32[320,768]{1,0:T(8,128)S(1)}, bf16[2,768,1536]{2,1,0:T(8,128)(2,1)S(1)}, f32[8,1536]{1,0:T(8,128)S(1)}) custom-call(s32[1]{0:T(128)} %bitcast.4.core_ref.refs_0_, bf16[320,768]{1,0:T(8,128)(2,1)S(1)} %get-tuple-element.210.do_ref, bf16[320,768]{1,0:T(8,128)(2,1)S(1)} %get-tuple-element.190.x_ref, ...), custom_call_target="tpu_custom_call" | custom-call | flops 368000000 | bytes 1048576 | tf_op jit(solution)/shard_map/feed_back/pallas_call | solution.py:871
  278.4 20.0 %attend_back.3 = (f32[320,768]{1,0:T(8,128)}, bf16[4,768,384]{2,1,0:T(8,128)(2,1)}, bf16[4,768,384]{2,1,0:T(8,128)(2,1)}, f32[8,768]{1,0:T(8,128)}) custom-call(s32[1]{0:T(128)} %bitcast.4.core_ref.refs_0_, f32[320,768]{1,0:T(8,128)} %copy-done.48, f32[320,768]{1,0:T(8,128)} %copy-done.49, f32[320,768]{1,0:T(8,128)} %copy-done.51, f32[320,768]{1,0:T(8,128)} %copy-done.21, ...), custom_call_target="tpu_custom_call" | custom-call | tf_op jit(solution)/shard_map/attend_back/pallas_call | solution.py:680
  324.5 7.3 %feed_up.3 = (bf16[576,3072]{1,0:T(8,128)(2,1)S(1)}, bf16[576,3072]{1,0:T(8,128)(2,1)S(1)}) custom-call(bf16[576,768]{1,0:T(8,128)(2,1)S(1)} %copy-done.10, bf16[1,768,3072]{2,1,0:T(8,128)(2,1)S(1)} %get-tuple-element.217.mat_ref.up_ref, f32[2,3072]{1,0:T(2,128)S(1)} %copy-done.66), custom_call_target="tpu_custom_call" | custom-call | flops 1092960000 | bytes 1048576 | tf_op jit(solution)/shard_map/feed_up/pallas_call | solution.py:803
  331.9 12.3 %feed_down.3 = (f32[576,768]{1,0:T(8,128)S(1)}, f32[576,768]{1,0:T(8,128)S(1)}, bf16[576,768]{1,0:T(8,128)(2,1)S(1)}, f32[8,768]{1,0:T(8,128)S(1)}) custom-call(bf16[576,3072]{1,0:T(8,128)(2,1)S(1)} %get-tuple-element.231.h_ref, bf16[1,768,3072]{2,1,0:T(8,128)(2,1)} %copy-done.4, f32[5,768]{1,0:T(8,128)S(1)} %copy-done.31, f32[16,768]{1,0:T(8,128)S(1)} %copy-done.35, ...), custom_call_target="tpu_custom_call" | custom-call | flops 728640000 | bytes 1048576 | tf_op jit(solution)/shard_map/feed_down/pallas_call | solution.py:834
  344.3 12.1 %feed_back.6 = (f32[576,768]{1,0:T(8,128)S(1)}, bf16[2,768,1536]{2,1,0:T(8,128)(2,1)}, f32[8,1536]{1,0:T(8,128)S(1)}) custom-call(s32[1]{0:T(128)} %bitcast.4.core_ref.refs_0_, bf16[576,768]{1,0:T(8,128)(2,1)S(1)} %get-tuple-element.236.do_ref, bf16[576,768]{1,0:T(8,128)(2,1)S(1)} %copy-done.10, bf16[576,3072]{1,0:T(8,128)(2,1)S(1)} %get-tuple-element.231.h_ref, ...), custom_call_target="tpu_custom_call" | custom-call | flops 662400000 | bytes 1048576 | tf_op jit(solution)/shard_map/feed_back/pallas_call | solution.py:871
  375.1 10.6 %feed_back.7 = (f32[576,768]{1,0:T(8,128)S(1)}, bf16[2,768,1536]{2,1,0:T(8,128)(2,1)}, f32[8,1536]{1,0:T(8,128)S(1)}) custom-call(s32[1]{0:T(128)} %bitcast.4.core_ref.refs_0_, bf16[576,768]{1,0:T(8,128)(2,1)S(1)} %copy-done.26, bf16[576,768]{1,0:T(8,128)(2,1)S(1)} %copy-done.11, bf16[576,3072]{1,0:T(8,128)(2,1)S(1)} %get-tuple-element.231.h_ref, ...), custom_call_target="tpu_custom_call" | custom-call | flops 662400000 | bytes 1048576 | tf_op jit(solution)/shard_map/feed_back/pallas_call | solution.py:871
  392.3 5.2 collective-permute-done.43
  412.2 28.7 %attend_back.4 = (f32[576,768]{1,0:T(8,128)}, bf16[4,768,384]{2,1,0:T(8,128)(2,1)}, bf16[4,768,384]{2,1,0:T(8,128)(2,1)}, f32[8,768]{1,0:T(8,128)}) custom-call(s32[1]{0:T(128)} %bitcast.4.core_ref.refs_0_, f32[576,768]{1,0:T(8,128)} %copy-done.37, f32[576,768]{1,0:T(8,128)} %copy-done.38, f32[576,768]{1,0:T(8,128)} %copy-done.39, ...), custom_call_target="tpu_custom_call" | custom-call | tf_op jit(solution)/shard_map/attend_back/pallas_call | solution.py:680
  444.8 8.6 %collective-permute-start.62 = (bf16[12,2,48,384]{3,2,0,1:T(8,128)(2,1)S(1)}, bf16[12,2,48,384]{3,2,0,1:T(8,128)(2,1)S(1)}, u32[]{:S(2)}, u32[]{:S(2)}) collective-permute-start(bf16[12,2,48,384]{3,2,0,1:T(8,128)(2,1)S(1)} %fusion.26), channel_id=1, source_target_pairs={{0,8},{2,10},{4,12},{6,14},{24,16},{26,18},{28,20},{30,22},{1,9},{... | collective-permute-start | bytes 2654216 | tf_op jit(solution)/shard_map/ppermute | solution.py:250
  464.3 8.5 %collective-permute-done.62 = bf16[12,2,48,384]{3,2,0,1:T(8,128)(2,1)S(1)} collective-permute-done((bf16[12,2,48,384]{3,2,0,1:T(8,128)(2,1)S(1)}, bf16[12,2,48,384]{3,2,0,1:T(8,128)(2,1)S(1)}, u32[]{:S(2)}, u32[]{:S(2)}) %collective-permute-start.62) | collective-permute-done | bytes 884768 | tf_op jit(solution)/shard_map/ppermute | solution.py:250
  474.0 36.9 %attend_back.5 = (f32[320,768]{1,0:T(8,128)}, f32[576,768]{1,0:T(8,128)}, bf16[4,768,384]{2,1,0:T(8,128)(2,1)}, bf16[4,768,384]{2,1,0:T(8,128)(2,1)}, f32[8,768]...) custom-call(s32[1]{0:T(128)} %bitcast.4.core_ref.refs_0_, ...), custom_call_target="tpu_custom_call" | custom-call | tf_op jit(solution)/shard_map/attend_back/pallas_call | solution.py:680
  517.9 7.5 %collective-permute-start.70 = (bf16[2,2,48,1536]{3,2,0,1:T(8,128)(2,1)}, bf16[2,2,48,1536]{3,2,0,1:T(8,128)(2,1)}, u32[]{:S(2)}, u32[]{:S(2)}) collective-permute-start(bf16[2,2,48,1536]{3,2,0,1:T(8,128)(2,1)} %dynamic-slice_bitcast_fusion.2), channel_id=1, source_target_pairs={{0,8},{2,10},{4,12},{6,14},{24,16},{26,18},{28,20},{30,22},{1,9},{... | collective-permute-start | bytes 1769480 | tf_op jit(solution)/shard_map/ppermute | solution.py:250
  534.5 7.5 %cross_inputs.1 = (f32[320,768]{1,0:T(8,128)S(1)}, f32[576,768]{1,0:T(8,128)}) custom-call(bf16[896,768]{1,0:T(8,128)(2,1)S(1)} %copy-done.43, bf16[896,768]{1,0:T(8,128)(2,1)S(1)} %copy-done.44, bf16[896,768]{1,0:T(8,128)(2,1)S(1)} %copy-done.45, bf16[4,768,768]{2,1,0:T(8,128)(2,1)} %copy-done, f32[320,768]{1,0:T(8,128)S(1)} %copy-done.50, ...), custom_call_target="tpu_custom_call" | custom-call | flops 575000000 | bytes 1048576 | tf_op jit(solution)/shard_map/cross_inputs/pallas_call | solution.py:701
  563.5 6.6 %collective-permute-done.76 = f32[2,16,128]{2,1,0:T(8,128)S(1)} collective-permute-done((f32[2,16,128]{2,1,0:T(8,128)S(1)}, f32[2,16,128]{2,1,0:T(8,128)S(1)}, u32[]{:S(2)}, u32[]{:S(2)}) %collective-permute-start.76) | collective-permute-done | bytes 16416 | tf_op jit(solution)/shard_map/ppermute | solution.py:63
  579.5 5.3 collective-permute-start.59
  586.5 5.2 collective-permute-done.64
  596.3 4.6 collective-permute-start.69
  601.1 4.6 collective-permute-done.69
  628.1 3.7 collective-permute-start.82
  633.7 4.5 add_multiply_fusion.1
  (706 shorter events, 309.1 us)
Async XLA Ops:
  22.6 24.3 %collective-permute-start.14 = (bf16[1,2,48,1536]{3,2,1,0:T(8,128)(2,1)}, bf16[1,2,48,1536]{3,2,1,0:T(8,128)(2,1)S(1)}, u32[]{:S(2)}, u32[]{:S(2)}) collective-permute-start(bf16[1,2,48,1536]{3,2,1,0:T(8,128)(2,1)} %get-tuple-element.173), channel_id=1, source_target_pairs={{0,8},{2,10},{4,12},{6,14},{8,0},{10,2},{12,4},{14,6},{16,24},{18,... | collective-permute-start | bytes 884744 | tf_op jit(solution)/shard_map/ppermute | solution.py:63
  70.0 37.7 %collective-permute-start.5 = (bf16[12,1,208,384]{3,2,1,0:T(8,128)(2,1)S(1)}, bf16[12,1,208,384]{3,2,1,0:T(8,128)(2,1)S(1)}, u32[]{:S(2)}, u32[]{:S(2)}) collective-permute-start(bf16[12,1,208,384]{3,2,1,0:T(8,128)(2,1)S(1)} %constant_dynamic-update-slice_fusion.2.refs_0_), channel_id=1, source_target_pairs={{0,1},{1,0},{2,3},{3,2},{4,5},{5,4},{6,7},{7,6},{8,9},{9,8},{10,11... | collective-permute-start | bytes 5750792 | tf_op jit(solution)/shard_map/ppermute | solution.py:67
  75.0 30.7 %collective-permute-start.13 = (bf16[4,8,48,384]{3,2,1,0:T(8,128)(2,1)S(1)}, bf16[4,8,48,384]{3,2,1,0:T(8,128)(2,1)S(1)}, u32[]{:S(2)}, u32[]{:S(2)}) collective-permute-start(bf16[4,8,48,384]{3,2,1,0:T(8,128)(2,1)S(1)} %copy-done.117), channel_id=1, source_target_pairs={{0,4},{2,6},{4,0},{6,2},{8,12},{10,14},{12,8},{14,10},{16,20},{18,... | collective-permute-start | bytes 3538952 | tf_op jit(solution)/shard_map/ppermute | solution.py:63
  75.4 27.7 %collective-permute-start.12 = (bf16[4,8,48,384]{3,2,1,0:T(8,128)(2,1)S(1)}, bf16[4,8,48,384]{3,2,1,0:T(8,128)(2,1)S(1)}, u32[]{:S(2)}, u32[]{:S(2)}) collective-permute-start(bf16[4,8,48,384]{3,2,1,0:T(8,128)(2,1)S(1)} %copy-done.117), channel_id=1, source_target_pairs={{0,2},{2,0},{4,6},{6,4},{8,10},{10,8},{12,14},{14,12},{16,18},{18,... | collective-permute-start | bytes 3538952 | tf_op jit(solution)/shard_map/ppermute | solution.py:63
  78.9 28.4 %collective-permute-start.8 = (bf16[4,1,208,384]{3,2,1,0:T(8,128)(2,1)S(1)}, bf16[4,1,208,384]{3,2,1,0:T(8,128)(2,1)S(1)}, u32[]{:S(2)}, u32[]{:S(2)}) collective-permute-start(bf16[4,1,208,384]{3,2,1,0:T(8,128)(2,1)S(1)} %constant_dynamic-update-slice_fusion.7.refs_2_), channel_id=1, source_target_pairs={{0,1},{1,0},{2,3},{3,2},{4,5},{5,4},{6,7},{7,6},{8,9},{9,8},{10,11... | collective-permute-start | bytes 1916936 | tf_op jit(solution)/shard_map/ppermute | solution.py:67
  90.6 55.1 %collective-permute-start.23 = (bf16[2,2,48,1536]{3,2,1,0:T(8,128)(2,1)}, bf16[2,2,48,1536]{3,2,1,0:T(8,128)(2,1)}, u32[]{:S(2)}, u32[]{:S(2)}) collective-permute-start(bf16[2,2,48,1536]{3,2,1,0:T(8,128)(2,1)} %collective-permute-done.18), channel_id=1, source_target_pairs={{8,0},{10,2},{12,4},{14,6},{16,24},{18,26},{20,28},{22,30},{9,1},{... | collective-permute-start | bytes 1769480 | tf_op jit(solution)/shard_map/ppermute | solution.py:153
  103.1 47.8 %collective-permute-start.22 = (bf16[4,2,48,1536]{3,2,1,0:T(8,128)(2,1)}, bf16[4,2,48,1536]{3,2,1,0:T(8,128)(2,1)}, u32[]{:S(2)}, u32[]{:S(2)}) collective-permute-start(bf16[4,2,48,1536]{3,2,1,0:T(8,128)(2,1)} %pad_maximum_fusion.1), channel_id=1, source_target_pairs={{0,4},{2,6},{4,0},{6,2},{8,12},{10,14},{12,8},{14,10},{16,20},{18,... | collective-permute-start | bytes 3538952 | tf_op jit(solution)/shard_map/ppermute | solution.py:63
  105.7 45.3 %collective-permute-start.21 = (bf16[4,2,48,1536]{3,2,1,0:T(8,128)(2,1)}, bf16[4,2,48,1536]{3,2,1,0:T(8,128)(2,1)}, u32[]{:S(2)}, u32[]{:S(2)}) collective-permute-start(bf16[4,2,48,1536]{3,2,1,0:T(8,128)(2,1)} %pad_maximum_fusion.1), channel_id=1, source_target_pairs={{0,2},{2,0},{4,6},{6,4},{8,10},{10,8},{12,14},{14,12},{16,18},{18,... | collective-permute-start | bytes 3538952 | tf_op jit(solution)/shard_map/ppermute | solution.py:63
  107.3 43.6 %collective-permute-start.19 = (bf16[2,8,48,384]{3,2,1,0:T(8,128)(2,1)}, bf16[2,8,48,384]{3,2,1,0:T(8,128)(2,1)}, u32[]{:S(2)}, u32[]{:S(2)}) collective-permute-start(bf16[2,8,48,384]{3,2,1,0:T(8,128)(2,1)} %slice.361), channel_id=1, source_target_pairs={{0,4},{2,6},{4,0},{6,2},{8,12},{10,14},{12,8},{14,10},{16,20},{18,... | collective-permute-start | bytes 1769480 | tf_op jit(solution)/shard_map/ppermute | solution.py:63
  109.1 41.9 %collective-permute-start.20 = (bf16[2,8,48,384]{3,2,1,0:T(8,128)(2,1)}, bf16[2,8,48,384]{3,2,1,0:T(8,128)(2,1)}, u32[]{:S(2)}, u32[]{:S(2)}) collective-permute-start(bf16[2,8,48,384]{3,2,1,0:T(8,128)(2,1)} %slice.362), channel_id=1, source_target_pairs={{0,2},{2,0},{4,6},{6,4},{8,10},{10,8},{12,14},{14,12},{16,18},{18,... | collective-permute-start | bytes 1769480 | tf_op jit(solution)/shard_map/ppermute | solution.py:63
  153.9 52.1 %collective-permute-start.29 = (bf16[4,2,48,1536]{3,2,1,0:T(8,128)(2,1)}, bf16[4,2,48,1536]{3,2,1,0:T(8,128)(2,1)S(1)}, u32[]{:S(2)}, u32[]{:S(2)}) collective-permute-start(bf16[4,2,48,1536]{3,2,1,0:T(8,128)(2,1)} %pad_maximum_fusion.2), channel_id=1, source_target_pairs={{0,4},{2,6},{4,0},{6,2},{8,12},{10,14},{12,8},{14,10},{16,20},{18,... | collective-permute-start | bytes 3538952 | tf_op jit(solution)/shard_map/ppermute | solution.py:63
  154.3 51.7 %collective-permute-start.28 = (bf16[4,2,48,1536]{3,2,1,0:T(8,128)(2,1)}, bf16[4,2,48,1536]{3,2,1,0:T(8,128)(2,1)S(1)}, u32[]{:S(2)}, u32[]{:S(2)}) collective-permute-start(bf16[4,2,48,1536]{3,2,1,0:T(8,128)(2,1)} %pad_maximum_fusion.2), channel_id=1, source_target_pairs={{0,2},{2,0},{4,6},{6,4},{8,10},{10,8},{12,14},{14,12},{16,18},{18,... | collective-permute-start | bytes 3538952 | tf_op jit(solution)/shard_map/ppermute | solution.py:63
  158.7 47.3 %collective-permute-start.26 = (bf16[2,2,48,1536]{3,2,1,0:T(8,128)(2,1)}, bf16[2,2,48,1536]{3,2,1,0:T(8,128)(2,1)S(1)}, u32[]{:S(2)}, u32[]{:S(2)}) collective-permute-start(bf16[2,2,48,1536]{3,2,1,0:T(8,128)(2,1)} %slice.363), channel_id=1, source_target_pairs={{0,4},{2,6},{4,0},{6,2},{8,12},{10,14},{12,8},{14,10},{16,20},{18,... | collective-permute-start | bytes 1769480 | tf_op jit(solution)/shard_map/ppermute | solution.py:63
  160.3 45.6 %collective-permute-start.27 = (bf16[2,2,48,1536]{3,2,1,0:T(8,128)(2,1)}, bf16[2,2,48,1536]{3,2,1,0:T(8,128)(2,1)}, u32[]{:S(2)}, u32[]{:S(2)}) collective-permute-start(bf16[2,2,48,1536]{3,2,1,0:T(8,128)(2,1)} %slice.364), channel_id=1, source_target_pairs={{0,2},{2,0},{4,6},{6,4},{8,10},{10,8},{12,14},{14,12},{16,18},{18,... | collective-permute-start | bytes 1769480 | tf_op jit(solution)/shard_map/ppermute | solution.py:63
  266.0 44.8 %collective-permute-start.34 = (bf16[12,2,48,1536]{3,2,1,0:T(8,128)(2,1)}, bf16[12,2,48,1536]{3,2,1,0:T(8,128)(2,1)S(1)}, u32[]{:S(2)}, u32[]{:S(2)}) collective-permute-start(bf16[12,2,48,1536]{3,2,1,0:T(8,128)(2,1)} %constant_dynamic-update-slice_fusion.23.refs_0_), channel_id=1, source_target_pairs={{0,1},{1,0},{2,3},{3,2},{4,5},{5,4},{6,7},{7,6},{8,9},{9,8},{10,11... | collective-permute-start | bytes 10616840 | tf_op jit(solution)/shard_map/ppermute | solution.py:67
  268.4 42.4 %collective-permute-start.35 = (bf16[4,2,48,1536]{3,2,1,0:T(8,128)(2,1)}, bf16[4,2,48,1536]{3,2,1,0:T(8,128)(2,1)}, u32[]{:S(2)}, u32[]{:S(2)}) collective-permute-start(bf16[4,2,48,1536]{3,2,1,0:T(8,128)(2,1)} %constant_dynamic-update-slice_fusion.28.refs_2_), channel_id=1, source_target_pairs={{0,1},{1,0},{2,3},{3,2},{4,5},{5,4},{6,7},{7,6},{8,9},{9,8},{10,11... | collective-permute-start | bytes 3538952 | tf_op jit(solution)/shard_map/ppermute | solution.py:67
  274.1 42.5 %collective-permute-start.39 = (bf16[1,4,2,48,1536]{4,3,2,1,0:T(8,128)(2,1)}, bf16[1,4,2,48,1536]{4,3,2,1,0:T(8,128)(2,1)}, u32[]{:S(2)}, u32[]{:S(2)}) collective-permute-start(bf16[1,4,2,48,1536]{4,3,2,1,0:T(8,128)(2,1)} %dynamic-slice_bitcast_fusion.1), channel_id=1, source_target_pairs={{0,4},{2,6},{4,0},{6,2},{8,12},{10,14},{12,8},{14,10},{16,20},{18,... | collective-permute-start | bytes 3538952 | tf_op jit(solution)/shard_map/ppermute | solution.py:63
  278.1 38.5 %collective-permute-start.38 = (bf16[1,4,2,48,1536]{4,3,1,2,0:T(8,128)(2,1)}, bf16[1,4,2,48,1536]{4,3,1,2,0:T(8,128)(2,1)}, u32[]{:S(2)}, u32[]{:S(2)}) collective-permute-start(bf16[1,4,2,48,1536]{4,3,1,2,0:T(8,128)(2,1)} %bitcast.221), channel_id=1, source_target_pairs={{0,2},{2,0},{4,6},{6,4},{8,10},{10,8},{12,14},{14,12},{16,18},{18,... | collective-permute-start | bytes 3538952 | tf_op jit(solution)/shard_map/ppermute | solution.py:63
  298.4 25.2 %collective-permute-start.37 = (bf16[4,768,384]{2,1,0:T(8,128)(2,1)}, bf16[4,768,384]{2,1,0:T(8,128)(2,1)}, u32[]{:S(2)}, u32[]{:S(2)}) collective-permute-start(bf16[4,768,384]{2,1,0:T(8,128)(2,1)} %get-tuple-element.229), channel_id=1, source_target_pairs={{0,1},{1,0},{2,3},{3,2},{4,5},{5,4},{6,7},{7,6},{8,9},{9,8},{10,11... | collective-permute-start | bytes 7077896 | tf_op jit(solution)/shard_map/ppermute | solution.py:67
  356.4 44.4 %collective-permute-start.40 = (bf16[2,768,1536]{2,1,0:T(8,128)(2,1)}, bf16[2,768,1536]{2,1,0:T(8,128)(2,1)}, u32[]{:S(2)}, u32[]{:S(2)}) collective-permute-start(bf16[2,768,1536]{2,1,0:T(8,128)(2,1)} %get-tuple-element.241), channel_id=1, source_target_pairs={{0,1},{1,0},{2,3},{3,2},{4,5},{5,4},{6,7},{7,6},{8,9},{9,8},{10,11... | collective-permute-start | bytes 14155784 | tf_op jit(solution)/shard_map/ppermute | solution.py:67
  370.8 26.6 %collective-permute-start.43 = (bf16[2,4,2,48,384]{4,3,1,0,2:T(8,128)(2,1)}, bf16[2,4,2,48,384]{4,3,1,0,2:T(8,128)(2,1)}, u32[]{:S(2)}, u32[]{:S(2)}) collective-permute-start(bf16[2,4,2,48,384]{4,3,1,0,2:T(8,128)(2,1)} %bitcast.264), channel_id=1, source_target_pairs={{0,2},{2,0},{4,6},{6,4},{8,10},{10,8},{12,14},{14,12},{16,18},{18,... | collective-permute-start | bytes 1769480 | tf_op jit(solution)/shard_map/ppermute | solution.py:63
  371.1 28.5 %collective-permute-start.44 = (bf16[2,4,2,48,384]{4,3,2,1,0:T(8,128)(2,1)}, bf16[2,4,2,48,384]{4,3,2,1,0:T(8,128)(2,1)}, u32[]{:S(2)}, u32[]{:S(2)}) collective-permute-start(bf16[2,4,2,48,384]{4,3,2,1,0:T(8,128)(2,1)} %dynamic-slice_bitcast_fusion.7), channel_id=1, source_target_pairs={{0,4},{2,6},{4,0},{6,2},{8,12},{10,14},{12,8},{14,10},{16,20},{18,... | collective-permute-start | bytes 1769480 | tf_op jit(solution)/shard_map/ppermute | solution.py:63
  405.9 36.5 %collective-permute-start.46 = (bf16[1,4,2,48,1536]{4,3,2,1,0:T(8,128)(2,1)}, bf16[1,4,2,48,1536]{4,3,2,1,0:T(8,128)(2,1)}, u32[]{:S(2)}, u32[]{:S(2)}) collective-permute-start(bf16[1,4,2,48,1536]{4,3,2,1,0:T(8,128)(2,1)} %dynamic-slice_bitcast_fusion), channel_id=1, source_target_pairs={{0,4},{2,6},{4,0},{6,2},{8,12},{10,14},{12,8},{14,10},{16,20},{18,... | collective-permute-start | bytes 3538952 | tf_op jit(solution)/shard_map/ppermute | solution.py:63
  408.9 33.6 %collective-permute-start.45 = (bf16[1,4,2,48,1536]{4,3,1,2,0:T(8,128)(2,1)}, bf16[1,4,2,48,1536]{4,3,1,2,0:T(8,128)(2,1)S(1)}, u32[]{:S(2)}, u32[]{:S(2)}) collective-permute-start(bf16[1,4,2,48,1536]{4,3,1,2,0:T(8,128)(2,1)} %bitcast.220), channel_id=1, source_target_pairs={{0,2},{2,0},{4,6},{6,4},{8,10},{10,8},{12,14},{14,12},{16,18},{18,... | collective-permute-start | bytes 3538952 | tf_op jit(solution)/shard_map/ppermute | solution.py:63
  411.4 29.5 %collective-permute-start.47 = (bf16[2,4,48,384]{3,2,1,0:T(8,128)(2,1)}, bf16[2,4,48,384]{3,2,1,0:T(8,128)(2,1)}, u32[]{:S(2)}, u32[]{:S(2)}) collective-permute-start(bf16[2,4,48,384]{3,2,1,0:T(8,128)(2,1)} %dynamic-slice_bitcast_fusion.19), channel_id=1, source_target_pairs={{0,4},{2,6},{4,0},{6,2},{8,12},{10,14},{12,8},{14,10},{16,20},{18,... | collective-permute-start | bytes 884744 | tf_op jit(solution)/shard_map/ppermute | solution.py:63
  411.7 30.7 %collective-permute-start.48 = (bf16[2,4,48,384]{3,2,1,0:T(8,128)(2,1)}, bf16[2,4,48,384]{3,2,1,0:T(8,128)(2,1)}, u32[]{:S(2)}, u32[]{:S(2)}) collective-permute-start(bf16[2,4,48,384]{3,2,1,0:T(8,128)(2,1)} %dynamic-slice_bitcast_fusion.18), channel_id=1, source_target_pairs={{0,2},{2,0},{4,6},{6,4},{8,10},{10,8},{12,14},{14,12},{16,18},{18,... | collective-permute-start | bytes 884744 | tf_op jit(solution)/shard_map/ppermute | solution.py:63
  444.8 28.1 %collective-permute-start.62 = (bf16[12,2,48,384]{3,2,0,1:T(8,128)(2,1)S(1)}, bf16[12,2,48,384]{3,2,0,1:T(8,128)(2,1)S(1)}, u32[]{:S(2)}, u32[]{:S(2)}) collective-permute-start(bf16[12,2,48,384]{3,2,0,1:T(8,128)(2,1)S(1)} %fusion.26), channel_id=1, source_target_pairs={{0,8},{2,10},{4,12},{6,14},{24,16},{26,18},{28,20},{30,22},{1,9},{... | collective-permute-start | bytes 2654216 | tf_op jit(solution)/shard_map/ppermute | solution.py:250
  459.2 52.4 %collective-permute-start.53 = (bf16[2,4,2,48,384]{4,3,2,1,0:T(8,128)(2,1)}, bf16[2,4,2,48,384]{4,3,2,1,0:T(8,128)(2,1)}, u32[]{:S(2)}, u32[]{:S(2)}) collective-permute-start(bf16[2,4,2,48,384]{4,3,2,1,0:T(8,128)(2,1)} %dynamic-slice_bitcast_fusion.4), channel_id=1, source_target_pairs={{0,4},{2,6},{4,0},{6,2},{8,12},{10,14},{12,8},{14,10},{16,20},{18,... | collective-permute-start | bytes 1769480 | tf_op jit(solution)/shard_map/ppermute | solution.py:63
  460.7 51.0 %collective-permute-start.52 = (bf16[2,4,2,48,384]{4,3,1,0,2:T(8,128)(2,1)}, bf16[2,4,2,48,384]{4,3,1,0,2:T(8,128)(2,1)S(1)}, u32[]{:S(2)}, u32[]{:S(2)}) collective-permute-start(bf16[2,4,2,48,384]{4,3,1,0,2:T(8,128)(2,1)} %bitcast.223), channel_id=1, source_target_pairs={{0,2},{2,0},{4,6},{6,4},{8,10},{10,8},{12,14},{14,12},{16,18},{18,... | collective-permute-start | bytes 1769480 | tf_op jit(solution)/shard_map/ppermute | solution.py:63
  461.2 50.4 %collective-permute-start.50 = (bf16[1,4,48,1536]{3,2,1,0:T(8,128)(2,1)S(1)}, bf16[1,4,48,1536]{3,2,1,0:T(8,128)(2,1)S(1)}, u32[]{:S(2)}, u32[]{:S(2)}) collective-permute-start(bf16[1,4,48,1536]{3,2,1,0:T(8,128)(2,1)S(1)} %dynamic-slice_bitcast_fusion.6), channel_id=1, source_target_pairs={{0,4},{2,6},{4,0},{6,2},{8,12},{10,14},{12,8},{14,10},{16,20},{18,... | collective-permute-start | bytes 1769480 | tf_op jit(solution)/shard_map/ppermute | solution.py:63
  462.8 48.9 %collective-permute-start.51 = (bf16[1,4,48,1536]{3,2,1,0:T(8,128)(2,1)}, bf16[1,4,48,1536]{3,2,1,0:T(8,128)(2,1)}, u32[]{:S(2)}, u32[]{:S(2)}) collective-permute-start(bf16[1,4,48,1536]{3,2,1,0:T(8,128)(2,1)} %dynamic-slice_bitcast_fusion.5), channel_id=1, source_target_pairs={{0,2},{2,0},{4,6},{6,4},{8,10},{10,8},{12,14},{14,12},{16,18},{18,... | collective-permute-start | bytes 1769480 | tf_op jit(solution)/shard_map/ppermute | solution.py:63
  517.9 26.7 %collective-permute-start.70 = (bf16[2,2,48,1536]{3,2,0,1:T(8,128)(2,1)}, bf16[2,2,48,1536]{3,2,0,1:T(8,128)(2,1)}, u32[]{:S(2)}, u32[]{:S(2)}) collective-permute-start(bf16[2,2,48,1536]{3,2,0,1:T(8,128)(2,1)} %dynamic-slice_bitcast_fusion.2), channel_id=1, source_target_pairs={{0,8},{2,10},{4,12},{6,14},{24,16},{26,18},{28,20},{30,22},{1,9},{... | collective-permute-start | bytes 1769480 | tf_op jit(solution)/shard_map/ppermute | solution.py:250
  (199 other events, 2256.8 us)

commit v3 on v2

--- a/solution.py
+++ b/solution.py
@@ -28,7 +28,7 @@
 CHIPS = 16
 PAIR = 2 * HEAD_DIM
 TILE = 256
-CHUNK = 32
+CHUNK = 64
 FEED = 1536
 FEED_ROWS = 64
 BELL = (2.0 * math.pi) ** -0.5
@@ -512,6 +512,18 @@
     (small_ref,) = take(1)
     dq_ref, dk_ref, dv_ref = take(3)
     do_ref, dctx_ref = take(2)
+    fetched = take(5 + plan["mats"])
+    sems = refs[0]
+    copies = [
+        pltpu.make_async_copy(source, target, sems.at[number])
+        for number, (source, target) in enumerate(
+            zip(mats + [q_ref, k_ref, v_ref, ctx_ref, x_ref], fetched)
+        )
+    ]
+    for copy in copies:
+        copy.start()
+    mats = fetched[: plan["mats"]]
+    q_ref, k_ref, v_ref, ctx_ref, x_ref = fetched[plan["mats"] :]
     width = x_ref.shape[1]
     half = width // 2
     each = 4 // plan["mats"]
@@ -540,6 +552,8 @@
             )
 
         sums = lax.fori_loop(0, size * groups // CHUNK, one_chunk, sums)
+    for copy in copies:
+        copy.wait()
     sent = do_ref[...]
     for at, size in tiles_of(width):
         dctx_ref[:, at : at + size] = dot_nn(sent, weights[3][:, at : at + size]).astype(low)
@@ -677,13 +691,21 @@
     cross = plan["cross"]
     args = [part for parts in carried for part in parts] + list(normed) + list(inverse) + [x]
     args += list(mats) + [gains, key_bias] + list(same) + list(kept)
+    far = [x] + list(mats) + list(kept[:4])
+    specs = [pl.BlockSpec(memory_space=pltpu.SMEM)] + [
+        pl.BlockSpec(memory_space=pl.ANY if any(arg is part for part in far) else pltpu.VMEM)
+        for arg in args
+    ]
     results = pl.pallas_call(
         functools.partial(attend_back, plan),
         out_shape=outs + (pieces if cross else []),
-        in_specs=[pl.BlockSpec(memory_space=pltpu.SMEM)] + vmem(len(args)),
+        in_specs=specs,
         out_specs=vmem(len(outs) + (3 if cross else 0)),
-        scratch_shapes=[pltpu.VMEM((rows, width), low)] * (2 if cross else 5),
-        compiler_params=params_of(56),
+        scratch_shapes=[pltpu.VMEM((rows, width), low)] * (2 if cross else 5)
+        + [pltpu.VMEM(mat.shape, low) for mat in mats]
+        + [pltpu.VMEM((rows, width), low)] * 5
+        + [pltpu.SemaphoreType.DMA((5 + len(mats),))],
+        compiler_params=params_of(58),
         name="attend_back",
     )(core, *args)
     many, count = len(counts), len(mats)
@@ -725,13 +747,15 @@
 
 
 def feed_down(plan, h_ref, mat_ref, gain_ref, bias_ref, unit_ref, cot_ref, live_ref, *refs):
-    out_ref, du_ref, do_ref, small_ref, acc_ref = refs
+    out_ref, du_ref, do_ref, small_ref, acc_ref, cots_ref = refs
     step = pl.program_id(0)
-    width = out_ref.shape[1]
+    items, slots, width = out_ref.shape
 
     @pl.when(step == 0)
     def _():
         acc_ref[...] = jnp.zeros_like(acc_ref)
+        for item in range(items):
+            cots_ref[item * slots : (item + 1) * slots, :] = widen(cot_ref[item])
 
     rows = h_ref[...]
     for at, size in tiles_of(width):
@@ -753,8 +777,8 @@
             live = live_ref[here, :]
             base = unit_ref[here, :] * last_gain + last_shift
             value, unit, scale = norm_rows(base + acc_ref[here, :] + out_bias, gain, shift)
-            out_ref[here, :] = value * live
-            grad = widen(cot_ref[here, :]) * live
+            grad = cots_ref[here, :] * live
+            cots_ref[here, :] = value * live
             down = norm_rows_back(grad, unit, scale, gain)
             sent = down.astype(low)
             du_ref[here, :] = down
@@ -765,7 +789,9 @@
                 sums[2] + fold_rows(widen(sent)),
             )
 
-        sums = lax.fori_loop(0, out_ref.shape[0] // CHUNK, one_chunk, (nothing,) * 3)
+        sums = lax.fori_loop(0, items * slots // CHUNK, one_chunk, (nothing,) * 3)
+        for item in range(items):
+            out_ref[item] = cots_ref[item * slots : (item + 1) * slots, :]
         small_ref[...] = jnp.concatenate(
             [close_rows(part) for part in sums] + [jnp.zeros((5, width), jnp.float32)], axis=0
         )
@@ -820,13 +846,11 @@
 def run_down(stream, h, mat, gains, biases, unit, cot, live):
     rows, hidden = h.shape
     width = unit.shape[1]
-    fixed = lambda step: (0, 0)
-
     def whole(array):
-        return pl.BlockSpec(array.shape, fixed)
+        return pl.BlockSpec(array.shape, lambda step: (0,) * len(array.shape))
 
     outs = [
-        shape_of((rows, width), jnp.float32),
+        shape_of(cot.shape, jnp.float32),
         shape_of((rows, width), jnp.float32),
         shape_of((rows, width), low),
         shape_of((8, width), jnp.float32),
@@ -845,7 +869,7 @@
             whole(live),
         ],
         out_specs=[whole(out) for out in outs],
-        scratch_shapes=[pltpu.VMEM((rows, width), jnp.float32)],
+        scratch_shapes=[pltpu.VMEM((rows, width), jnp.float32)] * 2,
         compiler_params=params_of(40),
         cost_estimate=cost_of(0.022 * rows),
         name="feed_down",
@@ -1008,7 +1032,7 @@
     key_bias = [(part - 1.0) * -mask_fill for part in live]
     key_all = jnp.concatenate(key_bias)
     x_all = jnp.concatenate([lang.reshape(-1, width), vis.reshape(-1, width)])
-    cots = [cot_lang.reshape(-1, width), cot_vis.reshape(-1, width)]
+    cots = [cot_lang, cot_vis]
 
     def same_item(asked, asking):
         rows = jnp.arange(sizes[asked])[:, None] // slots[asked]
@@ -1062,7 +1086,7 @@
             cots[stream],
             live[stream],
         )
-        return out.reshape(items, slots[stream], width), grad, sent, small
+        return out, grad, sent, small
 
     def go_feed_back(flip, stream, made, up, down, gate):
         return run_feed_back(

time: 653 us -> 624 us (0.956)
  local copies, waits for them, and re-layouts: 136 us -> 115 us
  Pallas kernels: 224 us -> 208 us
    reshape x4 -> x0, local copies, waits for them, and re-layouts: 9.18 us -> none  [the longest x2 5.15 us: go_down(): return (out.reshape(items, slots[stream], width), grad, sent, small)]
    unnamed x331 -> x317, local copies, waits for them, and re-layouts: 68.6 us -> 63.1 us
  transfers between devices with their start and end apart: 83 -> 83, of which waited for: 26 -> 25; matrix products, arithmetic and copies ran while one was open for 23% -> 22% of each run, Pallas kernels for 26% -> 26%
where the time goes in v3:
time: 624 us; the launch traced here: 616 us
  Pallas kernels  208 us (33%)
  starting transfers between devices  126 us (20%)
  local copies, waits for them, and re-layouts  115 us (18%)
  waiting for transfers between devices  82.3 us (13%)
  other arithmetic  74.2 us (12%)
  between operations  9.8 us (2%)
    ppermute x52, starting transfers between devices, send(): return lax.ppermute(values, 'dp', routes[bit])  83.7 us
    pallas_call x3, Pallas kernels, run_back(): pl.pallas_call(functools.partial(attend_back, plan), out_shape=outs + (pi...  79.8 us
    unnamed x317, local copies, waits for them, and re-layouts  63.1 us
    ppermute x52, waiting for transfers between devices, send(): return lax.ppermute(values, 'dp', routes[bit])  60.7 us
    pallas_call x3, Pallas kernels, run_front(): pl.pallas_call(functools.partial(attend_front, plan), out_shape=outs, in_...  46.1 us
    pallas_call x4, Pallas kernels, run_feed_back(): pl.pallas_call(feed_back, grid_spec=pltpu.PrefetchScalarGridSpec(num_scal...  36.7 us
    ppermute x4, starting transfers between devices, outer(): arrived = lax.ppermute(after(self.far, *gate), 'dp', inwards)  24.4 us
    convert_element_type x20, other arithmetic, side(): parts.append((widen(kept) + widen(arrived)).astype(low))  21.2 us
  transfers between devices with their start and end apart: 83, of which 25 were waited for; matrix products, arithmetic and copies ran while one was open for 22% of the time, Pallas kernels for 26%

profile of v3, /device:TPU:0, one launch (start us, length us, event | category | flops | bytes accessed | tf_op | source)
XLA Modules:
  0.0 616.2 jit_solution(17220127351473945855)
XLA Ops:
  24.5 8.6 %collective-permute-start.14 = (bf16[1,2,48,1536]{3,2,1,0:T(8,128)(2,1)}, bf16[1,2,48,1536]{3,2,1,0:T(8,128)(2,1)S(1)}, u32[]{:S(2)}, u32[]{:S(2)}) collective-permute-start(bf16[1,2,48,1536]{3,2,1,0:T(8,128)(2,1)} %get-tuple-element.173), channel_id=1, source_target_pairs={{0,8},{2,10},{4,12},{6,14},{8,0},{10,2},{12,4},{14,6},{16,24},{18,... | collective-permute-start | bytes 884744 | tf_op jit(solution)/shard_map/ppermute | solution.py:63
  51.5 6.3 %collective-permute-start.17 = (bf16[1,2,48,1536]{3,2,1,0:T(8,128)(2,1)S(1)}, bf16[1,2,48,1536]{3,2,1,0:T(8,128)(2,1)}, u32[]{:S(2)}, u32[]{:S(2)}) collective-permute-start(bf16[1,2,48,1536]{3,2,1,0:T(8,128)(2,1)S(1)} %get-tuple-element.176), channel_id=1, source_target_pairs={{0,8},{2,10},{4,12},{6,14},{8,0},{10,2},{12,4},{14,6},{16,24},{18,... | collective-permute-start | bytes 884744 | tf_op jit(solution)/shard_map/ppermute | solution.py:63
  80.0 11.7 %collective-permute-done.16 = bf16[2,2,48,1536]{3,2,1,0:T(8,128)(2,1)S(1)} collective-permute-done((bf16[2,2,48,1536]{3,2,1,0:T(8,128)(2,1)}, bf16[2,2,48,1536]{3,2,1,0:T(8,128)(2,1)S(1)}, u32[]{:S(2)}, u32[]{:S(2)}) %collective-permute-start.16) | collective-permute-done | bytes 589856 | tf_op jit(solution)/shard_map/ppermute | solution.py:153
  97.3 6.9 %collective-permute-done.12 = bf16[4,8,48,384]{3,2,1,0:T(8,128)(2,1)S(1)} collective-permute-done((bf16[4,8,48,384]{3,2,1,0:T(8,128)(2,1)S(1)}, bf16[4,8,48,384]{3,2,1,0:T(8,128)(2,1)S(1)}, u32[]{:S(2)}, u32[]{:S(2)}) %collective-permute-start.12) | collective-permute-done | bytes 1179680 | tf_op jit(solution)/shard_map/ppermute | solution.py:63
  117.6 22.9 %attend_front.3 = (bf16[896,768]{1,0:T(8,128)(2,1)S(1)}, bf16[896,768]{1,0:T(8,128)(2,1)}, bf16[896,768]{1,0:T(8,128)(2,1)}, bf16[896,768]{1,0:T(8,128)(2,1)}, f...) custom-call(bf16[896,768]{1,0:T(8,128)(2,1)} %constant_dynamic-updat, ...), custom_call_target="tpu_custom_call" | custom-call | flops 1442560000 | bytes 1048576 | tf_op jit(solution)/shard_map/attend_front/pallas_call | solution.py:668
  168.8 8.0 %attend_front.4 = (bf16[320,768]{1,0:T(8,128)(2,1)S(1)}, bf16[320,768]{1,0:T(8,128)(2,1)S(1)}, bf16[320,768]{1,0:T(8,128)(2,1)S(1)}, bf16[320,768]{1,0:T(8,128)(...) custom-call(bf16[320,768]{1,0:T(8,128)(2,1)S(1)} %get-tuple-element., ...), custom_call_target="tpu_custom_call" | custom-call | flops 515200000 | bytes 1048576 | tf_op jit(solution)/shard_map/attend_front/pallas_call | solution.py:668
  179.9 15.2 %attend_front.5 = (bf16[576,768]{1,0:T(8,128)(2,1)S(1)}, bf16[576,768]{1,0:T(8,128)(2,1)S(1)}, bf16[576,768]{1,0:T(8,128)(2,1)S(1)}, bf16[576,768]{1,0:T(8,128)(...) custom-call(bf16[576,768]{1,0:T(8,128)(2,1)S(1)} %get-tuple-element., ...), custom_call_target="tpu_custom_call" | custom-call | flops 927360000 | bytes 1048576 | tf_op jit(solution)/shard_map/attend_front/pallas_call | solution.py:668
  203.2 12.8 %collective-permute-done.32 = bf16[2,2,48,1536]{3,2,1,0:T(8,128)(2,1)} collective-permute-done((bf16[2,2,48,1536]{3,2,1,0:T(8,128)(2,1)}, bf16[2,2,48,1536]{3,2,1,0:T(8,128)(2,1)}, u32[]{:S(2)}, u32[]{:S(2)}) %collective-permute-start.32) | collective-permute-done | bytes 589856 | tf_op jit(solution)/shard_map/ppermute | solution.py:63
  216.0 4.1 assemble.6
  220.2 4.4 feed_up.2
  224.6 4.8 feed_down.2
  232.6 8.7 %feed_back.4 = (f32[320,768]{1,0:T(8,128)S(1)}, bf16[2,768,1536]{2,1,0:T(8,128)(2,1)}, f32[8,1536]{1,0:T(8,128)S(1)}) custom-call(s32[1]{0:T(128)} %bitcast.4.core_ref.refs_0_, bf16[320,768]{1,0:T(8,128)(2,1)S(1)} %get-tuple-element.210.do_ref, bf16[320,768]{1,0:T(8,128)(2,1)S(1)} %copy-done.12, bf16[320,3072]{1,0:T(8,128)(2,1)S(1)} %get-tuple-element.202.h_ref, ...), custom_call_target="tpu_custom_call" | custom-call | flops 368000000 | bytes 1048576 | tf_op jit(solution)/shard_map/feed_back/pallas_call | solution.py:895
  247.7 6.7 %feed_back.5 = (f32[320,768]{1,0:T(8,128)S(1)}, bf16[2,768,1536]{2,1,0:T(8,128)(2,1)S(1)}, f32[8,1536]{1,0:T(8,128)S(1)}) custom-call(s32[1]{0:T(128)} %bitcast.4.core_ref.refs_0_, bf16[320,768]{1,0:T(8,128)(2,1)S(1)} %copy-done.29, bf16[320,768]{1,0:T(8,128)(2,1)S(1)} %copy-done.12, bf16[320,3072]{1,0:T(8,128)(2,1)S(1)} %get-tuple-element.202.h_ref, ...), custom_call_target="tpu_custom_call" | custom-call | flops 368000000 | bytes 1048576 | tf_op jit(solution)/shard_map/feed_back/pallas_call | solution.py:895
  267.5 19.1 %attend_back.3 = (f32[320,768]{1,0:T(8,128)}, bf16[4,768,384]{2,1,0:T(8,128)(2,1)}, bf16[4,768,384]{2,1,0:T(8,128)(2,1)}, f32[8,768]{1,0:T(8,128)}) custom-call(s32[1]{0:T(128)} %bitcast.4.core_ref.refs_0_, f32[320,768]{1,0:T(8,128)} %copy-done.43, f32[320,768]{1,0:T(8,128)} %copy-done.44, f32[320,768]{1,0:T(8,128)} %copy-done.46, f32[320,768]{1,0:T(8,128)} %copy-done.18, ...), custom_call_target="tpu_custom_call" | custom-call | tf_op jit(solution)/shard_map/attend_back/pallas_call | solution.py:699
  291.9 4.1 assemble.7
  305.4 7.3 %feed_up.3 = (bf16[576,3072]{1,0:T(8,128)(2,1)S(1)}, bf16[576,3072]{1,0:T(8,128)(2,1)S(1)}) custom-call(bf16[576,768]{1,0:T(8,128)(2,1)S(1)} %get-tuple-element.206.x_ref, bf16[1,768,3072]{2,1,0:T(8,128)(2,1)S(1)} %get-tuple-element.217.mat_ref.up_ref, f32[2,3072]{1,0:T(2,128)S(1)} %reshape.822.bias_ref), custom_call_target="tpu_custom_call" | custom-call | flops 1092960000 | bytes 1048576 | tf_op jit(solution)/shard_map/feed_up/pallas_call | solution.py:829
  312.7 9.2 %feed_down.3 = (f32[16,36,768]{2,1,0:T(8,128)S(1)}, f32[576,768]{1,0:T(8,128)S(1)}, bf16[576,768]{1,0:T(8,128)(2,1)S(1)}, f32[8,768]{1,0:T(8,128)S(1)}) custom-call(bf16[576,3072]{1,0:T(8,128)(2,1)S(1)} %get-tuple-element.231.h_ref, bf16[1,768,3072]{2,1,0:T(8,128)(2,1)} %copy-done.4, f32[5,768]{1,0:T(8,128)S(1)} %copy-done.26, f32[16,768]{1,0:T(8,128)S(1)} %copy-done.31, ...), custom_call_target="tpu_custom_call" | custom-call | flops 728640000 | bytes 1048576 | tf_op jit(solution)/shard_map/feed_down/pallas_call | solution.py:858
  323.2 10.6 %feed_back.6 = (f32[576,768]{1,0:T(8,128)S(1)}, bf16[2,768,1536]{2,1,0:T(8,128)(2,1)}, f32[8,1536]{1,0:T(8,128)S(1)}) custom-call(s32[1]{0:T(128)} %bitcast.4.core_ref.refs_0_, bf16[576,768]{1,0:T(8,128)(2,1)S(1)} %get-tuple-element.236.do_ref, bf16[576,768]{1,0:T(8,128)(2,1)S(1)} %get-tuple-element.206.x_ref, ...), custom_call_target="tpu_custom_call" | custom-call | flops 662400000 | bytes 1048576 | tf_op jit(solution)/shard_map/feed_back/pallas_call | solution.py:895
  345.7 10.7 %feed_back.7 = (f32[576,768]{1,0:T(8,128)S(1)}, bf16[2,768,1536]{2,1,0:T(8,128)(2,1)}, f32[8,1536]{1,0:T(8,128)S(1)}) custom-call(s32[1]{0:T(128)} %bitcast.4.core_ref.refs_0_, bf16[576,768]{1,0:T(8,128)(2,1)S(1)} %get-tuple-element.236.do_ref, bf16[576,768]{1,0:T(8,128)(2,1)S(1)} %get-tuple-element.206.x_ref, ...), custom_call_target="tpu_custom_call" | custom-call | flops 662400000 | bytes 1048576 | tf_op jit(solution)/shard_map/feed_back/pallas_call | solution.py:895
  361.6 8.8 %collective-permute-done.43 = bf16[2,4,2,48,384]{4,3,1,0,2:T(8,128)(2,1)} collective-permute-done((bf16[2,4,2,48,384]{4,3,1,0,2:T(8,128)(2,1)}, bf16[2,4,2,48,384]{4,3,1,0,2:T(8,128)(2,1)}, u32[]{:S(2)}, u32[]{:S(2)}) %collective-permute-start.43) | collective-permute-done | bytes 589856 | tf_op jit(solution)/shard_map/ppermute | solution.py:63
  387.1 26.8 %attend_back.4 = (f32[576,768]{1,0:T(8,128)}, bf16[4,768,384]{2,1,0:T(8,128)(2,1)}, bf16[4,768,384]{2,1,0:T(8,128)(2,1)}, f32[8,768]{1,0:T(8,128)}) custom-call(s32[1]{0:T(128)} %bitcast.4.core_ref.refs_0_, f32[576,768]{1,0:T(8,128)} %copy-done.32, f32[576,768]{1,0:T(8,128)} %copy-done.33, f32[576,768]{1,0:T(8,128)} %copy-done.34, ...), custom_call_target="tpu_custom_call" | custom-call | tf_op jit(solution)/shard_map/attend_back/pallas_call | solution.py:699
  417.7 8.5 %collective-permute-start.62 = (bf16[12,2,48,384]{3,2,0,1:T(8,128)(2,1)S(1)}, bf16[12,2,48,384]{3,2,0,1:T(8,128)(2,1)S(1)}, u32[]{:S(2)}, u32[]{:S(2)}) collective-permute-start(bf16[12,2,48,384]{3,2,0,1:T(8,128)(2,1)S(1)} %fusion.26), channel_id=1, source_target_pairs={{0,8},{2,10},{4,12},{6,14},{24,16},{26,18},{28,20},{30,22},{1,9},{... | collective-permute-start | bytes 2654216 | tf_op jit(solution)/shard_map/ppermute | solution.py:250
  439.4 6.3 %collective-permute-done.62 = bf16[12,2,48,384]{3,2,0,1:T(8,128)(2,1)S(1)} collective-permute-done((bf16[12,2,48,384]{3,2,0,1:T(8,128)(2,1)S(1)}, bf16[12,2,48,384]{3,2,0,1:T(8,128)(2,1)S(1)}, u32[]{:S(2)}, u32[]{:S(2)}) %collective-permute-start.62) | collective-permute-done | bytes 884768 | tf_op jit(solution)/shard_map/ppermute | solution.py:250
  446.8 33.9 %attend_back.5 = (f32[320,768]{1,0:T(8,128)}, f32[576,768]{1,0:T(8,128)}, bf16[4,768,384]{2,1,0:T(8,128)(2,1)}, bf16[4,768,384]{2,1,0:T(8,128)(2,1)}, f32[8,768]...) custom-call(s32[1]{0:T(128)} %bitcast.4.core_ref.refs_0_, ...), custom_call_target="tpu_custom_call" | custom-call | tf_op jit(solution)/shard_map/attend_back/pallas_call | solution.py:699
  488.8 7.4 %collective-permute-start.70 = (bf16[2,2,48,1536]{3,2,0,1:T(8,128)(2,1)}, bf16[2,2,48,1536]{3,2,0,1:T(8,128)(2,1)}, u32[]{:S(2)}, u32[]{:S(2)}) collective-permute-start(bf16[2,2,48,1536]{3,2,0,1:T(8,128)(2,1)} %dynamic-slice_bitcast_fusion.2), channel_id=1, source_target_pairs={{0,8},{2,10},{4,12},{6,14},{24,16},{26,18},{28,20},{30,22},{1,9},{... | collective-permute-start | bytes 1769480 | tf_op jit(solution)/shard_map/ppermute | solution.py:250
  505.0 7.5 %cross_inputs.1 = (f32[320,768]{1,0:T(8,128)S(1)}, f32[576,768]{1,0:T(8,128)}) custom-call(bf16[896,768]{1,0:T(8,128)(2,1)S(1)} %copy-done.38, bf16[896,768]{1,0:T(8,128)(2,1)S(1)} %copy-done.39, bf16[896,768]{1,0:T(8,128)(2,1)S(1)} %copy-done.40, bf16[4,768,768]{2,1,0:T(8,128)(2,1)} %copy-done, f32[320,768]{1,0:T(8,128)S(1)} %copy-done.45, ...), custom_call_target="tpu_custom_call" | custom-call | flops 575000000 | bytes 1048576 | tf_op jit(solution)/shard_map/cross_inputs/pallas_call | solution.py:723
  534.7 6.6 %collective-permute-done.76 = f32[2,16,128]{2,1,0:T(8,128)S(1)} collective-permute-done((f32[2,16,128]{2,1,0:T(8,128)S(1)}, f32[2,16,128]{2,1,0:T(8,128)S(1)}, u32[]{:S(2)}, u32[]{:S(2)}) %collective-permute-start.76) | collective-permute-done | bytes 16416 | tf_op jit(solution)/shard_map/ppermute | solution.py:63
  550.5 5.6 collective-permute-start.59
  557.9 5.0 collective-permute-done.64
  567.4 4.8 collective-permute-start.69
  572.4 4.6 collective-permute-done.69
  605.0 4.5 add_multiply_fusion.1
  (688 shorter events, 293.9 us)
Async XLA Ops:
  24.5 23.6 %collective-permute-start.14 = (bf16[1,2,48,1536]{3,2,1,0:T(8,128)(2,1)}, bf16[1,2,48,1536]{3,2,1,0:T(8,128)(2,1)S(1)}, u32[]{:S(2)}, u32[]{:S(2)}) collective-permute-start(bf16[1,2,48,1536]{3,2,1,0:T(8,128)(2,1)} %get-tuple-element.173), channel_id=1, source_target_pairs={{0,8},{2,10},{4,12},{6,14},{8,0},{10,2},{12,4},{14,6},{16,24},{18,... | collective-permute-start | bytes 884744 | tf_op jit(solution)/shard_map/ppermute | solution.py:63
  71.0 37.7 %collective-permute-start.5 = (bf16[12,1,208,384]{3,2,1,0:T(8,128)(2,1)S(1)}, bf16[12,1,208,384]{3,2,1,0:T(8,128)(2,1)S(1)}, u32[]{:S(2)}, u32[]{:S(2)}) collective-permute-start(bf16[12,1,208,384]{3,2,1,0:T(8,128)(2,1)S(1)} %constant_dynamic-update-slice_fusion.2.refs_0_), channel_id=1, source_target_pairs={{0,1},{1,0},{2,3},{3,2},{4,5},{5,4},{6,7},{7,6},{8,9},{9,8},{10,11... | collective-permute-start | bytes 5750792 | tf_op jit(solution)/shard_map/ppermute | solution.py:67
  76.0 30.7 %collective-permute-start.13 = (bf16[4,8,48,384]{3,2,1,0:T(8,128)(2,1)S(1)}, bf16[4,8,48,384]{3,2,1,0:T(8,128)(2,1)S(1)}, u32[]{:S(2)}, u32[]{:S(2)}) collective-permute-start(bf16[4,8,48,384]{3,2,1,0:T(8,128)(2,1)S(1)} %copy-done.104), channel_id=1, source_target_pairs={{0,4},{2,6},{4,0},{6,2},{8,12},{10,14},{12,8},{14,10},{16,20},{18,... | collective-permute-start | bytes 3538952 | tf_op jit(solution)/shard_map/ppermute | solution.py:63
  76.5 27.6 %collective-permute-start.12 = (bf16[4,8,48,384]{3,2,1,0:T(8,128)(2,1)S(1)}, bf16[4,8,48,384]{3,2,1,0:T(8,128)(2,1)S(1)}, u32[]{:S(2)}, u32[]{:S(2)}) collective-permute-start(bf16[4,8,48,384]{3,2,1,0:T(8,128)(2,1)S(1)} %copy-done.104), channel_id=1, source_target_pairs={{0,2},{2,0},{4,6},{6,4},{8,10},{10,8},{12,14},{14,12},{16,18},{18,... | collective-permute-start | bytes 3538952 | tf_op jit(solution)/shard_map/ppermute | solution.py:63
  79.9 28.4 %collective-permute-start.8 = (bf16[4,1,208,384]{3,2,1,0:T(8,128)(2,1)S(1)}, bf16[4,1,208,384]{3,2,1,0:T(8,128)(2,1)S(1)}, u32[]{:S(2)}, u32[]{:S(2)}) collective-permute-start(bf16[4,1,208,384]{3,2,1,0:T(8,128)(2,1)S(1)} %constant_dynamic-update-slice_fusion.7.refs_2_), channel_id=1, source_target_pairs={{0,1},{1,0},{2,3},{3,2},{4,5},{5,4},{6,7},{7,6},{8,9},{9,8},{10,11... | collective-permute-start | bytes 1916936 | tf_op jit(solution)/shard_map/ppermute | solution.py:67
  91.7 52.5 %collective-permute-start.23 = (bf16[2,2,48,1536]{3,2,1,0:T(8,128)(2,1)}, bf16[2,2,48,1536]{3,2,1,0:T(8,128)(2,1)}, u32[]{:S(2)}, u32[]{:S(2)}) collective-permute-start(bf16[2,2,48,1536]{3,2,1,0:T(8,128)(2,1)} %collective-permute-done.18), channel_id=1, source_target_pairs={{8,0},{10,2},{12,4},{14,6},{16,24},{18,26},{20,28},{22,30},{9,1},{... | collective-permute-start | bytes 1769480 | tf_op jit(solution)/shard_map/ppermute | solution.py:153
  104.1 44.3 %collective-permute-start.22 = (bf16[4,2,48,1536]{3,2,1,0:T(8,128)(2,1)}, bf16[4,2,48,1536]{3,2,1,0:T(8,128)(2,1)}, u32[]{:S(2)}, u32[]{:S(2)}) collective-permute-start(bf16[4,2,48,1536]{3,2,1,0:T(8,128)(2,1)} %pad_maximum_fusion.1), channel_id=1, source_target_pairs={{0,4},{2,6},{4,0},{6,2},{8,12},{10,14},{12,8},{14,10},{16,20},{18,... | collective-permute-start | bytes 3538952 | tf_op jit(solution)/shard_map/ppermute | solution.py:63
  106.7 41.8 %collective-permute-start.21 = (bf16[4,2,48,1536]{3,2,1,0:T(8,128)(2,1)}, bf16[4,2,48,1536]{3,2,1,0:T(8,128)(2,1)}, u32[]{:S(2)}, u32[]{:S(2)}) collective-permute-start(bf16[4,2,48,1536]{3,2,1,0:T(8,128)(2,1)} %pad_maximum_fusion.1), channel_id=1, source_target_pairs={{0,2},{2,0},{4,6},{6,4},{8,10},{10,8},{12,14},{14,12},{16,18},{18,... | collective-permute-start | bytes 3538952 | tf_op jit(solution)/shard_map/ppermute | solution.py:63
  108.3 40.1 %collective-permute-start.19 = (bf16[2,8,48,384]{3,2,1,0:T(8,128)(2,1)}, bf16[2,8,48,384]{3,2,1,0:T(8,128)(2,1)}, u32[]{:S(2)}, u32[]{:S(2)}) collective-permute-start(bf16[2,8,48,384]{3,2,1,0:T(8,128)(2,1)} %slice.361), channel_id=1, source_target_pairs={{0,4},{2,6},{4,0},{6,2},{8,12},{10,14},{12,8},{14,10},{16,20},{18,... | collective-permute-start | bytes 1769480 | tf_op jit(solution)/shard_map/ppermute | solution.py:63
  110.2 38.2 %collective-permute-start.20 = (bf16[2,8,48,384]{3,2,1,0:T(8,128)(2,1)}, bf16[2,8,48,384]{3,2,1,0:T(8,128)(2,1)}, u32[]{:S(2)}, u32[]{:S(2)}) collective-permute-start(bf16[2,8,48,384]{3,2,1,0:T(8,128)(2,1)} %slice.362), channel_id=1, source_target_pairs={{0,2},{2,0},{4,6},{6,4},{8,10},{10,8},{12,14},{14,12},{16,18},{18,... | collective-permute-start | bytes 1769480 | tf_op jit(solution)/shard_map/ppermute | solution.py:63
  151.4 45.5 %collective-permute-start.29 = (bf16[4,2,48,1536]{3,2,1,0:T(8,128)(2,1)S(1)}, bf16[4,2,48,1536]{3,2,1,0:T(8,128)(2,1)S(1)}, u32[]{:S(2)}, u32[]{:S(2)}) collective-permute-start(bf16[4,2,48,1536]{3,2,1,0:T(8,128)(2,1)S(1)} %pad_maximum_fusion.2), channel_id=1, source_target_pairs={{0,4},{2,6},{4,0},{6,2},{8,12},{10,14},{12,8},{14,10},{16,20},{18,... | collective-permute-start | bytes 3538952 | tf_op jit(solution)/shard_map/ppermute | solution.py:63
  151.8 45.2 %collective-permute-start.28 = (bf16[4,2,48,1536]{3,2,1,0:T(8,128)(2,1)S(1)}, bf16[4,2,48,1536]{3,2,1,0:T(8,128)(2,1)S(1)}, u32[]{:S(2)}, u32[]{:S(2)}) collective-permute-start(bf16[4,2,48,1536]{3,2,1,0:T(8,128)(2,1)S(1)} %pad_maximum_fusion.2), channel_id=1, source_target_pairs={{0,2},{2,0},{4,6},{6,4},{8,10},{10,8},{12,14},{14,12},{16,18},{18,... | collective-permute-start | bytes 3538952 | tf_op jit(solution)/shard_map/ppermute | solution.py:63
  154.5 42.4 %collective-permute-start.26 = (bf16[2,2,48,1536]{3,2,1,0:T(8,128)(2,1)S(1)}, bf16[2,2,48,1536]{3,2,1,0:T(8,128)(2,1)S(1)}, u32[]{:S(2)}, u32[]{:S(2)}) collective-permute-start(bf16[2,2,48,1536]{3,2,1,0:T(8,128)(2,1)S(1)} %slice.363), channel_id=1, source_target_pairs={{0,4},{2,6},{4,0},{6,2},{8,12},{10,14},{12,8},{14,10},{16,20},{18,... | collective-permute-start | bytes 1769480 | tf_op jit(solution)/shard_map/ppermute | solution.py:63
  156.4 40.5 %collective-permute-start.27 = (bf16[2,2,48,1536]{3,2,1,0:T(8,128)(2,1)S(1)}, bf16[2,2,48,1536]{3,2,1,0:T(8,128)(2,1)S(1)}, u32[]{:S(2)}, u32[]{:S(2)}) collective-permute-start(bf16[2,2,48,1536]{3,2,1,0:T(8,128)(2,1)S(1)} %slice.364), channel_id=1, source_target_pairs={{0,2},{2,0},{4,6},{6,4},{8,10},{10,8},{12,14},{14,12},{16,18},{18,... | collective-permute-start | bytes 1769480 | tf_op jit(solution)/shard_map/ppermute | solution.py:63
  256.0 35.9 %collective-permute-start.34 = (bf16[12,2,48,1536]{3,2,1,0:T(8,128)(2,1)}, bf16[12,2,48,1536]{3,2,1,0:T(8,128)(2,1)}, u32[]{:S(2)}, u32[]{:S(2)}) collective-permute-start(bf16[12,2,48,1536]{3,2,1,0:T(8,128)(2,1)} %constant_dynamic-update-slice_fusion.23.refs_0_), channel_id=1, source_target_pairs={{0,1},{1,0},{2,3},{3,2},{4,5},{5,4},{6,7},{7,6},{8,9},{9,8},{10,11... | collective-permute-start | bytes 10616840 | tf_op jit(solution)/shard_map/ppermute | solution.py:67
  257.4 34.5 %collective-permute-start.35 = (bf16[4,2,48,1536]{3,2,1,0:T(8,128)(2,1)}, bf16[4,2,48,1536]{3,2,1,0:T(8,128)(2,1)S(1)}, u32[]{:S(2)}, u32[]{:S(2)}) collective-permute-start(bf16[4,2,48,1536]{3,2,1,0:T(8,128)(2,1)} %constant_dynamic-update-slice_fusion.28.refs_2_), channel_id=1, source_target_pairs={{0,1},{1,0},{2,3},{3,2},{4,5},{5,4},{6,7},{7,6},{8,9},{9,8},{10,11... | collective-permute-start | bytes 3538952 | tf_op jit(solution)/shard_map/ppermute | solution.py:67
  263.1 35.0 %collective-permute-start.39 = (bf16[1,4,2,48,1536]{4,3,2,1,0:T(8,128)(2,1)}, bf16[1,4,2,48,1536]{4,3,2,1,0:T(8,128)(2,1)}, u32[]{:S(2)}, u32[]{:S(2)}) collective-permute-start(bf16[1,4,2,48,1536]{4,3,2,1,0:T(8,128)(2,1)} %dynamic-slice_bitcast_fusion.1), channel_id=1, source_target_pairs={{0,4},{2,6},{4,0},{6,2},{8,12},{10,14},{12,8},{14,10},{16,20},{18,... | collective-permute-start | bytes 3538952 | tf_op jit(solution)/shard_map/ppermute | solution.py:63
  267.1 31.1 %collective-permute-start.38 = (bf16[1,4,2,48,1536]{4,3,1,2,0:T(8,128)(2,1)}, bf16[1,4,2,48,1536]{4,3,1,2,0:T(8,128)(2,1)}, u32[]{:S(2)}, u32[]{:S(2)}) collective-permute-start(bf16[1,4,2,48,1536]{4,3,1,2,0:T(8,128)(2,1)} %bitcast.221), channel_id=1, source_target_pairs={{0,2},{2,0},{4,6},{6,4},{8,10},{10,8},{12,14},{14,12},{16,18},{18,... | collective-permute-start | bytes 3538952 | tf_op jit(solution)/shard_map/ppermute | solution.py:63
  333.8 40.0 %collective-permute-start.40 = (bf16[2,768,1536]{2,1,0:T(8,128)(2,1)}, bf16[2,768,1536]{2,1,0:T(8,128)(2,1)}, u32[]{:S(2)}, u32[]{:S(2)}) collective-permute-start(bf16[2,768,1536]{2,1,0:T(8,128)(2,1)} %get-tuple-element.241), channel_id=1, source_target_pairs={{0,1},{1,0},{2,3},{3,2},{4,5},{5,4},{6,7},{7,6},{8,9},{9,8},{10,11... | collective-permute-start | bytes 14155784 | tf_op jit(solution)/shard_map/ppermute | solution.py:67
  343.6 26.8 %collective-permute-start.43 = (bf16[2,4,2,48,384]{4,3,1,0,2:T(8,128)(2,1)}, bf16[2,4,2,48,384]{4,3,1,0,2:T(8,128)(2,1)}, u32[]{:S(2)}, u32[]{:S(2)}) collective-permute-start(bf16[2,4,2,48,384]{4,3,1,0,2:T(8,128)(2,1)} %bitcast.224), channel_id=1, source_target_pairs={{0,2},{2,0},{4,6},{6,4},{8,10},{10,8},{12,14},{14,12},{16,18},{18,... | collective-permute-start | bytes 1769480 | tf_op jit(solution)/shard_map/ppermute | solution.py:63
  344.1 28.5 %collective-permute-start.44 = (bf16[2,4,2,48,384]{4,3,2,1,0:T(8,128)(2,1)}, bf16[2,4,2,48,384]{4,3,2,1,0:T(8,128)(2,1)}, u32[]{:S(2)}, u32[]{:S(2)}) collective-permute-start(bf16[2,4,2,48,384]{4,3,2,1,0:T(8,128)(2,1)} %dynamic-slice_bitcast_fusion.7), channel_id=1, source_target_pairs={{0,4},{2,6},{4,0},{6,2},{8,12},{10,14},{12,8},{14,10},{16,20},{18,... | collective-permute-start | bytes 1769480 | tf_op jit(solution)/shard_map/ppermute | solution.py:63
  378.9 36.5 %collective-permute-start.46 = (bf16[1,4,2,48,1536]{4,3,2,1,0:T(8,128)(2,1)}, bf16[1,4,2,48,1536]{4,3,2,1,0:T(8,128)(2,1)}, u32[]{:S(2)}, u32[]{:S(2)}) collective-permute-start(bf16[1,4,2,48,1536]{4,3,2,1,0:T(8,128)(2,1)} %dynamic-slice_bitcast_fusion), channel_id=1, source_target_pairs={{0,4},{2,6},{4,0},{6,2},{8,12},{10,14},{12,8},{14,10},{16,20},{18,... | collective-permute-start | bytes 3538952 | tf_op jit(solution)/shard_map/ppermute | solution.py:63
  381.8 33.6 %collective-permute-start.45 = (bf16[1,4,2,48,1536]{4,3,1,2,0:T(8,128)(2,1)}, bf16[1,4,2,48,1536]{4,3,1,2,0:T(8,128)(2,1)}, u32[]{:S(2)}, u32[]{:S(2)}) collective-permute-start(bf16[1,4,2,48,1536]{4,3,1,2,0:T(8,128)(2,1)} %bitcast.220), channel_id=1, source_target_pairs={{0,2},{2,0},{4,6},{6,4},{8,10},{10,8},{12,14},{14,12},{16,18},{18,... | collective-permute-start | bytes 3538952 | tf_op jit(solution)/shard_map/ppermute | solution.py:63
  384.1 29.8 %collective-permute-start.47 = (bf16[2,4,48,384]{3,2,1,0:T(8,128)(2,1)}, bf16[2,4,48,384]{3,2,1,0:T(8,128)(2,1)}, u32[]{:S(2)}, u32[]{:S(2)}) collective-permute-start(bf16[2,4,48,384]{3,2,1,0:T(8,128)(2,1)} %dynamic-slice_bitcast_fusion.19), channel_id=1, source_target_pairs={{0,4},{2,6},{4,0},{6,2},{8,12},{10,14},{12,8},{14,10},{16,20},{18,... | collective-permute-start | bytes 884744 | tf_op jit(solution)/shard_map/ppermute | solution.py:63
  384.5 30.9 %collective-permute-start.48 = (bf16[2,4,48,384]{3,2,1,0:T(8,128)(2,1)}, bf16[2,4,48,384]{3,2,1,0:T(8,128)(2,1)}, u32[]{:S(2)}, u32[]{:S(2)}) collective-permute-start(bf16[2,4,48,384]{3,2,1,0:T(8,128)(2,1)} %dynamic-slice_bitcast_fusion.18), channel_id=1, source_target_pairs={{0,2},{2,0},{4,6},{6,4},{8,10},{10,8},{12,14},{14,12},{16,18},{18,... | collective-permute-start | bytes 884744 | tf_op jit(solution)/shard_map/ppermute | solution.py:63
  417.7 28.0 %collective-permute-start.62 = (bf16[12,2,48,384]{3,2,0,1:T(8,128)(2,1)S(1)}, bf16[12,2,48,384]{3,2,0,1:T(8,128)(2,1)S(1)}, u32[]{:S(2)}, u32[]{:S(2)}) collective-permute-start(bf16[12,2,48,384]{3,2,0,1:T(8,128)(2,1)S(1)} %fusion.26), channel_id=1, source_target_pairs={{0,8},{2,10},{4,12},{6,14},{24,16},{26,18},{28,20},{30,22},{1,9},{... | collective-permute-start | bytes 2654216 | tf_op jit(solution)/shard_map/ppermute | solution.py:250
  432.9 48.9 %collective-permute-start.53 = (bf16[2,4,2,48,384]{4,3,2,1,0:T(8,128)(2,1)}, bf16[2,4,2,48,384]{4,3,2,1,0:T(8,128)(2,1)}, u32[]{:S(2)}, u32[]{:S(2)}) collective-permute-start(bf16[2,4,2,48,384]{4,3,2,1,0:T(8,128)(2,1)} %dynamic-slice_bitcast_fusion.4), channel_id=1, source_target_pairs={{0,4},{2,6},{4,0},{6,2},{8,12},{10,14},{12,8},{14,10},{16,20},{18,... | collective-permute-start | bytes 1769480 | tf_op jit(solution)/shard_map/ppermute | solution.py:63
  434.4 47.4 %collective-permute-start.52 = (bf16[2,4,2,48,384]{4,3,1,0,2:T(8,128)(2,1)}, bf16[2,4,2,48,384]{4,3,1,0,2:T(8,128)(2,1)S(1)}, u32[]{:S(2)}, u32[]{:S(2)}) collective-permute-start(bf16[2,4,2,48,384]{4,3,1,0,2:T(8,128)(2,1)} %bitcast.223), channel_id=1, source_target_pairs={{0,2},{2,0},{4,6},{6,4},{8,10},{10,8},{12,14},{14,12},{16,18},{18,... | collective-permute-start | bytes 1769480 | tf_op jit(solution)/shard_map/ppermute | solution.py:63
  435.0 46.9 %collective-permute-start.50 = (bf16[1,4,48,1536]{3,2,1,0:T(8,128)(2,1)}, bf16[1,4,48,1536]{3,2,1,0:T(8,128)(2,1)}, u32[]{:S(2)}, u32[]{:S(2)}) collective-permute-start(bf16[1,4,48,1536]{3,2,1,0:T(8,128)(2,1)} %dynamic-slice_bitcast_fusion.6), channel_id=1, source_target_pairs={{0,4},{2,6},{4,0},{6,2},{8,12},{10,14},{12,8},{14,10},{16,20},{18,... | collective-permute-start | bytes 1769480 | tf_op jit(solution)/shard_map/ppermute | solution.py:63
  436.5 45.3 %collective-permute-start.51 = (bf16[1,4,48,1536]{3,2,1,0:T(8,128)(2,1)}, bf16[1,4,48,1536]{3,2,1,0:T(8,128)(2,1)}, u32[]{:S(2)}, u32[]{:S(2)}) collective-permute-start(bf16[1,4,48,1536]{3,2,1,0:T(8,128)(2,1)} %dynamic-slice_bitcast_fusion.5), channel_id=1, source_target_pairs={{0,2},{2,0},{4,6},{6,4},{8,10},{10,8},{12,14},{14,12},{16,18},{18,... | collective-permute-start | bytes 1769480 | tf_op jit(solution)/shard_map/ppermute | solution.py:63
  480.7 21.8 %collective-permute-start.63 = (bf16[12,2,48,384]{3,2,0,1:T(8,128)(2,1)}, bf16[12,2,48,384]{3,2,0,1:T(8,128)(2,1)S(1)}, u32[]{:S(2)}, u32[]{:S(2)}) collective-permute-start(bf16[12,2,48,384]{3,2,0,1:T(8,128)(2,1)} %add_convert_fusion.6), channel_id=1, source_target_pairs={{8,16},{10,18},{12,20},{14,22},{16,8},{18,10},{20,12},{22,14},{9,1... | collective-permute-start | bytes 2654216 | tf_op jit(solution)/shard_map/ppermute | solution.py:255
  488.8 26.8 %collective-permute-start.70 = (bf16[2,2,48,1536]{3,2,0,1:T(8,128)(2,1)}, bf16[2,2,48,1536]{3,2,0,1:T(8,128)(2,1)}, u32[]{:S(2)}, u32[]{:S(2)}) collective-permute-start(bf16[2,2,48,1536]{3,2,0,1:T(8,128)(2,1)} %dynamic-slice_bitcast_fusion.2), channel_id=1, source_target_pairs={{0,8},{2,10},{4,12},{6,14},{24,16},{26,18},{28,20},{30,22},{1,9},{... | collective-permute-start | bytes 1769480 | tf_op jit(solution)/shard_map/ppermute | solution.py:250
  (192 other events, 2204.5 us)

commit v4 on v3

--- a/solution.py
+++ b/solution.py
@@ -671,7 +671,7 @@
         in_specs=vmem(len(args)),
         out_specs=vmem(len(outs)),
         scratch_shapes=[pltpu.VMEM((rows, width), jnp.float32)],
-        compiler_params=params_of(48),
+        compiler_params=params_of(27),
         cost_estimate=cost_of(0.028 * rows),
         name="attend_front",
     )(*args)
@@ -705,7 +705,7 @@
         + [pltpu.VMEM(mat.shape, low) for mat in mats]
         + [pltpu.VMEM((rows, width), low)] * 5
         + [pltpu.SemaphoreType.DMA((5 + len(mats),))],
-        compiler_params=params_of(58),
+        compiler_params=params_of(40),
         name="attend_back",
     )(core, *args)
     many, count = len(counts), len(mats)
@@ -725,7 +725,7 @@
         out_shape=outs,
         in_specs=vmem(4 + len(grads)),
         out_specs=vmem(len(grads)),
-        compiler_params=params_of(48),
+        compiler_params=params_of(28),
         cost_estimate=cost_of(10),
         name="cross_inputs",
     )(*pieces, mat, *grads)
@@ -837,7 +837,7 @@
         ],
         out_specs=[pl.BlockSpec((rows, FEED), wide)] * 2,
         scratch_shapes=[pltpu.VMEM((rows, FEED), jnp.float32)],
-        compiler_params=params_of(32),
+        compiler_params=params_of(24),
         cost_estimate=cost_of(0.033 * rows),
         name="feed_up",
     )(x, mat, biases)
@@ -870,7 +870,7 @@
         ],
         out_specs=[whole(out) for out in outs],
         scratch_shapes=[pltpu.VMEM((rows, width), jnp.float32)] * 2,
-        compiler_params=params_of(40),
+        compiler_params=params_of(31),
         cost_estimate=cost_of(0.022 * rows),
         name="feed_down",
     )(h, mat, gains, biases, unit, cot, live)

time: 624 us -> 616 us (0.987)
  Pallas kernels: 208 us -> 179 us
  local copies, waits for them, and re-layouts: 115 us -> 132 us
  waiting for transfers between devices: 82.3 us -> 95.5 us
  other arithmetic: 74.2 us -> 67.6 us
    unnamed x317 -> x387, local copies, waits for them, and re-layouts: 63.1 us -> 81.3 us
    pallas_call x3, Pallas kernels: 46.1 us -> 33.6 us  [run_front(): pl.pallas_call(functools.partial(attend_front, plan), out_shape=outs, in_...]
    ppermute x52, waiting for transfers between devices: 60.7 us -> 73 us  [send(): return lax.ppermute(values, 'dp', routes[bit])]
    pallas_call x3, Pallas kernels: 79.8 us -> 68 us  [run_back(): pl.pallas_call(functools.partial(attend_back, plan), out_shape=outs + (pi...]
  transfers between devices with their start and end apart: 83 -> 83, of which waited for: 25 -> 30; matrix products, arithmetic and copies ran while one was open for 22% -> 21% of each run, Pallas kernels for 26% -> 22%
where the time goes in v4:
time: 616 us; the launch traced here: 609 us
  Pallas kernels  179 us (29%)
  local copies, waits for them, and re-layouts  132 us (21%)
  starting transfers between devices  125 us (20%)
  waiting for transfers between devices  95.5 us (16%)
  other arithmetic  67.6 us (11%)
  between operations  10.5 us (2%)
    ppermute x52, starting transfers between devices, send(): return lax.ppermute(values, 'dp', routes[bit])  84.7 us
    unnamed x387, local copies, waits for them, and re-layouts  81.3 us
    ppermute x52, waiting for transfers between devices, send(): return lax.ppermute(values, 'dp', routes[bit])  73 us
    pallas_call x3, Pallas kernels, run_back(): pl.pallas_call(functools.partial(attend_back, plan), out_shape=outs + (pi...  68 us
    pallas_call x4, Pallas kernels, run_feed_back(): pl.pallas_call(feed_back, grid_spec=pltpu.PrefetchScalarGridSpec(num_scal...  36.7 us
    pallas_call x3, Pallas kernels, run_front(): pl.pallas_call(functools.partial(attend_front, plan), out_shape=outs, in_...  33.6 us
    ppermute x4, starting transfers between devices, outer(): arrived = lax.ppermute(after(self.far, *gate), 'dp', inwards)  22.7 us
    convert_element_type x20, other arithmetic, side(): parts.append((widen(kept) + widen(arrived)).astype(low))  15.9 us
  transfers between devices with their start and end apart: 83, of which 30 were waited for; matrix products, arithmetic and copies ran while one was open for 21% of the time, Pallas kernels for 22%

profile of v4, /device:TPU:0, one launch (start us, length us, event | category | flops | bytes accessed | tf_op | source)
XLA Modules:
  0.0 608.6 jit_solution(8035816567189669119)
XLA Ops:
  24.8 8.7 %collective-permute-start.14 = (bf16[1,2,48,1536]{3,2,1,0:T(8,128)(2,1)S(1)}, bf16[1,2,48,1536]{3,2,1,0:T(8,128)(2,1)}, u32[]{:S(2)}, u32[]{:S(2)}) collective-permute-start(bf16[1,2,48,1536]{3,2,1,0:T(8,128)(2,1)S(1)} %get-tuple-element.173), channel_id=1, source_target_pairs={{0,8},{2,10},{4,12},{6,14},{8,0},{10,2},{12,4},{14,6},{16,24},{18,... | collective-permute-start | bytes 884744 | tf_op jit(solution)/shard_map/ppermute | solution.py:63
  50.7 7.1 %collective-permute-start.17 = (bf16[1,2,48,1536]{3,2,1,0:T(8,128)(2,1)S(1)}, bf16[1,2,48,1536]{3,2,1,0:T(8,128)(2,1)}, u32[]{:S(2)}, u32[]{:S(2)}) collective-permute-start(bf16[1,2,48,1536]{3,2,1,0:T(8,128)(2,1)S(1)} %get-tuple-element.176), channel_id=1, source_target_pairs={{0,8},{2,10},{4,12},{6,14},{8,0},{10,2},{12,4},{14,6},{16,24},{18,... | collective-permute-start | bytes 884744 | tf_op jit(solution)/shard_map/ppermute | solution.py:63
  82.5 10.1 %collective-permute-done.16 = bf16[2,2,48,1536]{3,2,1,0:T(8,128)(2,1)S(1)} collective-permute-done((bf16[2,2,48,1536]{3,2,1,0:T(8,128)(2,1)}, bf16[2,2,48,1536]{3,2,1,0:T(8,128)(2,1)S(1)}, u32[]{:S(2)}, u32[]{:S(2)}) %collective-permute-start.16) | collective-permute-done | bytes 589856 | tf_op jit(solution)/shard_map/ppermute | solution.py:153
  98.1 9.4 %collective-permute-done.12 = bf16[4,8,48,384]{3,2,1,0:T(8,128)(2,1)S(1)} collective-permute-done((bf16[4,8,48,384]{3,2,1,0:T(8,128)(2,1)S(1)}, bf16[4,8,48,384]{3,2,1,0:T(8,128)(2,1)S(1)}, u32[]{:S(2)}, u32[]{:S(2)}) %collective-permute-start.12) | collective-permute-done | bytes 1179680 | tf_op jit(solution)/shard_map/ppermute | solution.py:63
  124.5 17.8 %attend_front.3 = (bf16[896,768]{1,0:T(8,128)(2,1)S(1)}, bf16[896,768]{1,0:T(8,128)(2,1)S(1)}, bf16[896,768]{1,0:T(8,128)(2,1)S(1)}, bf16[896,768]{1,0:T(8,128)(...) custom-call(bf16[896,768]{1,0:T(8,128)(2,1)S(1)} %constant_dynamic-u, ...), custom_call_target="tpu_custom_call" | custom-call | flops 1442560000 | bytes 1048576 | tf_op jit(solution)/shard_map/attend_front/pallas_call | solution.py:668
  169.8 5.4 attend_front.4
  180.8 10.4 %attend_front.5 = (bf16[576,768]{1,0:T(8,128)(2,1)S(1)}, bf16[576,768]{1,0:T(8,128)(2,1)S(1)}, bf16[576,768]{1,0:T(8,128)(2,1)S(1)}, bf16[576,768]{1,0:T(8,128)(...) custom-call(bf16[576,768]{1,0:T(8,128)(2,1)S(1)} %get-tuple-element., ...), custom_call_target="tpu_custom_call" | custom-call | flops 927360000 | bytes 1048576 | tf_op jit(solution)/shard_map/attend_front/pallas_call | solution.py:668
  203.8 12.3 %collective-permute-done.32 = bf16[2,2,48,1536]{3,2,1,0:T(8,128)(2,1)} collective-permute-done((bf16[2,2,48,1536]{3,2,1,0:T(8,128)(2,1)}, bf16[2,2,48,1536]{3,2,1,0:T(8,128)(2,1)}, u32[]{:S(2)}, u32[]{:S(2)}) %collective-permute-start.32) | collective-permute-done | bytes 589856 | tf_op jit(solution)/shard_map/ppermute | solution.py:63
  216.7 4.1 assemble.6
  220.9 4.4 feed_up.2
  225.3 5.1 feed_down.2
  235.1 8.4 %feed_back.4 = (f32[320,768]{1,0:T(8,128)S(1)}, bf16[2,768,1536]{2,1,0:T(8,128)(2,1)}, f32[8,1536]{1,0:T(8,128)S(1)}) custom-call(s32[1]{0:T(128)} %bitcast.4.core_ref.refs_0_, bf16[320,768]{1,0:T(8,128)(2,1)S(1)} %get-tuple-element.210.do_ref, bf16[320,768]{1,0:T(8,128)(2,1)S(1)} %copy-done.19, bf16[320,3072]{1,0:T(8,128)(2,1)S(1)} %get-tuple-element.202.h_ref, ...), custom_call_target="tpu_custom_call" | custom-call | flops 368000000 | bytes 1048576 | tf_op jit(solution)/shard_map/feed_back/pallas_call | solution.py:895
  250.8 6.7 %feed_back.5 = (f32[320,768]{1,0:T(8,128)S(1)}, bf16[2,768,1536]{2,1,0:T(8,128)(2,1)S(1)}, f32[8,1536]{1,0:T(8,128)S(1)}) custom-call(s32[1]{0:T(128)} %bitcast.4.core_ref.refs_0_, bf16[320,768]{1,0:T(8,128)(2,1)S(1)} %copy-done.41, bf16[320,768]{1,0:T(8,128)(2,1)S(1)} %copy-done.20, bf16[320,3072]{1,0:T(8,128)(2,1)S(1)} %get-tuple-element.202.h_ref, ...), custom_call_target="tpu_custom_call" | custom-call | flops 368000000 | bytes 1048576 | tf_op jit(solution)/shard_map/feed_back/pallas_call | solution.py:895
  269.9 15.3 %attend_back.3 = (f32[320,768]{1,0:T(8,128)S(1)}, bf16[4,768,384]{2,1,0:T(8,128)(2,1)S(1)}, bf16[4,768,384]{2,1,0:T(8,128)(2,1)}, f32[8,768]{1,0:T(8,128)S(1)}) custom-call(s32[1]{0:T(128)} %bitcast.4.core_ref.refs_0_, f32[320,768]{1,0:T(8,128)S(1)} %copy-done.63, f32[320,768]{1,0:T(8,128)S(1)} %copy-done.65, f32[320,768]{1,0:T(8,128)S(1)} %get-tuple-element.223.refs_3_, ...), custom_call_target="tpu_custom_call" | custom-call | tf_op jit(solution)/shard_map/attend_back/pallas_call | solution.py:699
  293.6 4.4 assemble.7
  305.5 7.3 %feed_up.3 = (bf16[576,3072]{1,0:T(8,128)(2,1)S(1)}, bf16[576,3072]{1,0:T(8,128)(2,1)S(1)}) custom-call(bf16[576,768]{1,0:T(8,128)(2,1)S(1)} %get-tuple-element.206.x_ref, bf16[1,768,3072]{2,1,0:T(8,128)(2,1)S(1)} %get-tuple-element.217.mat_ref.up_ref, f32[2,3072]{1,0:T(2,128)S(1)} %copy-done.91), custom_call_target="tpu_custom_call" | custom-call | flops 1092960000 | bytes 1048576 | tf_op jit(solution)/shard_map/feed_up/pallas_call | solution.py:829
  314.6 7.8 %feed_down.3 = (f32[16,36,768]{2,1,0:T(8,128)S(1)}, f32[576,768]{1,0:T(8,128)S(1)}, bf16[576,768]{1,0:T(8,128)(2,1)S(1)}, f32[8,768]{1,0:T(8,128)S(1)}) custom-call(bf16[576,3072]{1,0:T(8,128)(2,1)S(1)} %get-tuple-element.231.h_ref, bf16[1,768,3072]{2,1,0:T(8,128)(2,1)S(1)} %get-tuple-element.232.mat_ref.down_ref, ...), custom_call_target="tpu_custom_call" | custom-call | flops 728640000 | bytes 1048576 | tf_op jit(solution)/shard_map/feed_down/pallas_call | solution.py:858
  323.6 10.6 %feed_back.6 = (f32[576,768]{1,0:T(8,128)S(1)}, bf16[2,768,1536]{2,1,0:T(8,128)(2,1)}, f32[8,1536]{1,0:T(8,128)S(1)}) custom-call(s32[1]{0:T(128)} %bitcast.4.core_ref.refs_0_, bf16[576,768]{1,0:T(8,128)(2,1)S(1)} %get-tuple-element.236.do_ref, bf16[576,768]{1,0:T(8,128)(2,1)S(1)} %get-tuple-element.206.x_ref, ...), custom_call_target="tpu_custom_call" | custom-call | flops 662400000 | bytes 1048576 | tf_op jit(solution)/shard_map/feed_back/pallas_call | solution.py:895
  345.7 11.0 %feed_back.7 = (f32[576,768]{1,0:T(8,128)S(1)}, bf16[2,768,1536]{2,1,0:T(8,128)(2,1)}, f32[8,1536]{1,0:T(8,128)S(1)}) custom-call(s32[1]{0:T(128)} %bitcast.4.core_ref.refs_0_, bf16[576,768]{1,0:T(8,128)(2,1)S(1)} %get-tuple-element.236.do_ref, bf16[576,768]{1,0:T(8,128)(2,1)S(1)} %get-tuple-element.206.x_ref, ...), custom_call_target="tpu_custom_call" | custom-call | flops 662400000 | bytes 1048576 | tf_op jit(solution)/shard_map/feed_back/pallas_call | solution.py:895
  362.4 8.2 %collective-permute-done.43 = bf16[2,4,2,48,384]{4,3,1,0,2:T(8,128)(2,1)} collective-permute-done((bf16[2,4,2,48,384]{4,3,1,0,2:T(8,128)(2,1)}, bf16[2,4,2,48,384]{4,3,1,0,2:T(8,128)(2,1)}, u32[]{:S(2)}, u32[]{:S(2)}) %collective-permute-start.43) | collective-permute-done | bytes 589856 | tf_op jit(solution)/shard_map/ppermute | solution.py:63
  384.8 22.2 %attend_back.4 = (f32[576,768]{1,0:T(8,128)S(1)}, bf16[4,768,384]{2,1,0:T(8,128)(2,1)}, bf16[4,768,384]{2,1,0:T(8,128)(2,1)}, f32[8,768]{1,0:T(8,128)S(1)}) custom-call(s32[1]{0:T(128)} %bitcast.4.core_ref.refs_0_, f32[576,768]{1,0:T(8,128)S(1)} %copy-done.44, f32[576,768]{1,0:T(8,128)S(1)} %get-tuple-element.244.refs_2_, f32[576,768]{1,0:T(8,128)S(1)} %copy-done.46, ...), custom_call_target="tpu_custom_call" | custom-call | tf_op jit(solution)/shard_map/attend_back/pallas_call | solution.py:699
  414.3 5.8 collective-permute-start.62
  430.3 8.6 %collective-permute-done.62 = bf16[12,2,48,384]{3,2,0,1:T(8,128)(2,1)S(1)} collective-permute-done((bf16[12,2,48,384]{3,2,0,1:T(8,128)(2,1)S(1)}, bf16[12,2,48,384]{3,2,0,1:T(8,128)(2,1)S(1)}, u32[]{:S(2)}, u32[]{:S(2)}) %collective-permute-start.62) | collective-permute-done | bytes 884768 | tf_op jit(solution)/shard_map/ppermute | solution.py:250
  439.3 30.5 %attend_back.5 = (f32[320,768]{1,0:T(8,128)S(1)}, f32[576,768]{1,0:T(8,128)}, bf16[4,768,384]{2,1,0:T(8,128)(2,1)}, bf16[4,768,384]{2,1,0:T(8,128)(2,1)}, f32[8,...) custom-call(s32[1]{0:T(128)} %bitcast.4.core_ref.refs_0_, ...), custom_call_target="tpu_custom_call" | custom-call | tf_op jit(solution)/shard_map/attend_back/pallas_call | solution.py:699
  476.1 7.6 %collective-permute-start.70 = (bf16[2,2,48,1536]{3,2,0,1:T(8,128)(2,1)}, bf16[2,2,48,1536]{3,2,0,1:T(8,128)(2,1)}, u32[]{:S(2)}, u32[]{:S(2)}) collective-permute-start(bf16[2,2,48,1536]{3,2,0,1:T(8,128)(2,1)} %dynamic-slice_bitcast_fusion.2), channel_id=1, source_target_pairs={{0,8},{2,10},{4,12},{6,14},{24,16},{26,18},{28,20},{30,22},{1,9},{... | collective-permute-start | bytes 1769480 | tf_op jit(solution)/shard_map/ppermute | solution.py:250
  494.7 5.2 collective-permute-done.56
  513.0 3.9 collective-permute-start.74
  525.0 6.4 %collective-permute-done.76 = f32[2,16,128]{2,1,0:T(8,128)S(1)} collective-permute-done((f32[2,16,128]{2,1,0:T(8,128)S(1)}, f32[2,16,128]{2,1,0:T(8,128)S(1)}, u32[]{:S(2)}, u32[]{:S(2)}) %collective-permute-start.76) | collective-permute-done | bytes 16416 | tf_op jit(solution)/shard_map/ppermute | solution.py:63
  541.6 6.3 %collective-permute-start.59 = (bf16[4,2,48,384]{3,2,0,1:T(8,128)(2,1)S(1)}, bf16[4,2,48,384]{3,2,0,1:T(8,128)(2,1)S(1)}, u32[]{:S(2)}, u32[]{:S(2)}) collective-permute-start(bf16[4,2,48,384]{3,2,0,1:T(8,128)(2,1)S(1)} %dynamic-slice_bitcast_fusion.15), channel_id=1, source_target_pairs={{0,8},{2,10},{4,12},{6,14},{24,16},{26,18},{28,20},{30,22},{1,9},{... | collective-permute-start | bytes 884744 | tf_op jit(solution)/shard_map/ppermute | solution.py:250
  558.5 4.9 collective-permute-start.69
  563.5 4.6 collective-permute-done.69
  597.0 4.5 add_multiply_fusion.1
  (759 shorter events, 312.9 us)
Async XLA Ops:
  24.8 22.6 %collective-permute-start.14 = (bf16[1,2,48,1536]{3,2,1,0:T(8,128)(2,1)S(1)}, bf16[1,2,48,1536]{3,2,1,0:T(8,128)(2,1)}, u32[]{:S(2)}, u32[]{:S(2)}) collective-permute-start(bf16[1,2,48,1536]{3,2,1,0:T(8,128)(2,1)S(1)} %get-tuple-element.173), channel_id=1, source_target_pairs={{0,8},{2,10},{4,12},{6,14},{8,0},{10,2},{12,4},{14,6},{16,24},{18,... | collective-permute-start | bytes 884744 | tf_op jit(solution)/shard_map/ppermute | solution.py:63
  50.7 22.8 %collective-permute-start.17 = (bf16[1,2,48,1536]{3,2,1,0:T(8,128)(2,1)S(1)}, bf16[1,2,48,1536]{3,2,1,0:T(8,128)(2,1)}, u32[]{:S(2)}, u32[]{:S(2)}) collective-permute-start(bf16[1,2,48,1536]{3,2,1,0:T(8,128)(2,1)S(1)} %get-tuple-element.176), channel_id=1, source_target_pairs={{0,8},{2,10},{4,12},{6,14},{8,0},{10,2},{12,4},{14,6},{16,24},{18,... | collective-permute-start | bytes 884744 | tf_op jit(solution)/shard_map/ppermute | solution.py:63
  73.5 38.7 %collective-permute-start.5 = (bf16[12,1,208,384]{3,2,1,0:T(8,128)(2,1)}, bf16[12,1,208,384]{3,2,1,0:T(8,128)(2,1)S(1)}, u32[]{:S(2)}, u32[]{:S(2)}) collective-permute-start(bf16[12,1,208,384]{3,2,1,0:T(8,128)(2,1)} %constant_dynamic-update-slice_fusion.2.refs_0_), channel_id=1, source_target_pairs={{0,1},{1,0},{2,3},{3,2},{4,5},{5,4},{6,7},{7,6},{8,9},{9,8},{10,11... | collective-permute-start | bytes 5750792 | tf_op jit(solution)/shard_map/ppermute | solution.py:67
  79.0 31.1 %collective-permute-start.13 = (bf16[4,8,48,384]{3,2,1,0:T(8,128)(2,1)S(1)}, bf16[4,8,48,384]{3,2,1,0:T(8,128)(2,1)S(1)}, u32[]{:S(2)}, u32[]{:S(2)}) collective-permute-start(bf16[4,8,48,384]{3,2,1,0:T(8,128)(2,1)S(1)} %copy-done.144), channel_id=1, source_target_pairs={{0,4},{2,6},{4,0},{6,2},{8,12},{10,14},{12,8},{14,10},{16,20},{18,... | collective-permute-start | bytes 3538952 | tf_op jit(solution)/shard_map/ppermute | solution.py:63
  79.2 28.4 %collective-permute-start.12 = (bf16[4,8,48,384]{3,2,1,0:T(8,128)(2,1)S(1)}, bf16[4,8,48,384]{3,2,1,0:T(8,128)(2,1)S(1)}, u32[]{:S(2)}, u32[]{:S(2)}) collective-permute-start(bf16[4,8,48,384]{3,2,1,0:T(8,128)(2,1)S(1)} %copy-done.144), channel_id=1, source_target_pairs={{0,2},{2,0},{4,6},{6,4},{8,10},{10,8},{12,14},{14,12},{16,18},{18,... | collective-permute-start | bytes 3538952 | tf_op jit(solution)/shard_map/ppermute | solution.py:63
  82.4 29.4 %collective-permute-start.8 = (bf16[4,1,208,384]{3,2,1,0:T(8,128)(2,1)S(1)}, bf16[4,1,208,384]{3,2,1,0:T(8,128)(2,1)S(1)}, u32[]{:S(2)}, u32[]{:S(2)}) collective-permute-start(bf16[4,1,208,384]{3,2,1,0:T(8,128)(2,1)S(1)} %constant_dynamic-update-slice_fusion.7.refs_2_), channel_id=1, source_target_pairs={{0,1},{1,0},{2,3},{3,2},{4,5},{5,4},{6,7},{7,6},{8,9},{9,8},{10,11... | collective-permute-start | bytes 1916936 | tf_op jit(solution)/shard_map/ppermute | solution.py:67
  92.5 56.7 %collective-permute-start.23 = (bf16[2,2,48,1536]{3,2,1,0:T(8,128)(2,1)}, bf16[2,2,48,1536]{3,2,1,0:T(8,128)(2,1)}, u32[]{:S(2)}, u32[]{:S(2)}) collective-permute-start(bf16[2,2,48,1536]{3,2,1,0:T(8,128)(2,1)} %collective-permute-done.18), channel_id=1, source_target_pairs={{8,0},{10,2},{12,4},{14,6},{16,24},{18,26},{20,28},{22,30},{9,1},{... | collective-permute-start | bytes 1769480 | tf_op jit(solution)/shard_map/ppermute | solution.py:153
  107.5 46.1 %collective-permute-start.22 = (bf16[4,2,48,1536]{3,2,1,0:T(8,128)(2,1)}, bf16[4,2,48,1536]{3,2,1,0:T(8,128)(2,1)}, u32[]{:S(2)}, u32[]{:S(2)}) collective-permute-start(bf16[4,2,48,1536]{3,2,1,0:T(8,128)(2,1)} %pad_maximum_fusion.1), channel_id=1, source_target_pairs={{0,4},{2,6},{4,0},{6,2},{8,12},{10,14},{12,8},{14,10},{16,20},{18,... | collective-permute-start | bytes 3538952 | tf_op jit(solution)/shard_map/ppermute | solution.py:63
  110.1 43.6 %collective-permute-start.21 = (bf16[4,2,48,1536]{3,2,1,0:T(8,128)(2,1)}, bf16[4,2,48,1536]{3,2,1,0:T(8,128)(2,1)}, u32[]{:S(2)}, u32[]{:S(2)}) collective-permute-start(bf16[4,2,48,1536]{3,2,1,0:T(8,128)(2,1)} %pad_maximum_fusion.1), channel_id=1, source_target_pairs={{0,2},{2,0},{4,6},{6,4},{8,10},{10,8},{12,14},{14,12},{16,18},{18,... | collective-permute-start | bytes 3538952 | tf_op jit(solution)/shard_map/ppermute | solution.py:63
  111.8 41.9 %collective-permute-start.19 = (bf16[2,8,48,384]{3,2,1,0:T(8,128)(2,1)}, bf16[2,8,48,384]{3,2,1,0:T(8,128)(2,1)}, u32[]{:S(2)}, u32[]{:S(2)}) collective-permute-start(bf16[2,8,48,384]{3,2,1,0:T(8,128)(2,1)} %slice.361), channel_id=1, source_target_pairs={{0,4},{2,6},{4,0},{6,2},{8,12},{10,14},{12,8},{14,10},{16,20},{18,... | collective-permute-start | bytes 1769480 | tf_op jit(solution)/shard_map/ppermute | solution.py:63
  113.5 40.1 %collective-permute-start.20 = (bf16[2,8,48,384]{3,2,1,0:T(8,128)(2,1)}, bf16[2,8,48,384]{3,2,1,0:T(8,128)(2,1)}, u32[]{:S(2)}, u32[]{:S(2)}) collective-permute-start(bf16[2,8,48,384]{3,2,1,0:T(8,128)(2,1)} %slice.362), channel_id=1, source_target_pairs={{0,2},{2,0},{4,6},{6,4},{8,10},{10,8},{12,14},{14,12},{16,18},{18,... | collective-permute-start | bytes 1769480 | tf_op jit(solution)/shard_map/ppermute | solution.py:63
  156.6 40.7 %collective-permute-start.29 = (bf16[4,2,48,1536]{3,2,1,0:T(8,128)(2,1)S(1)}, bf16[4,2,48,1536]{3,2,1,0:T(8,128)(2,1)S(1)}, u32[]{:S(2)}, u32[]{:S(2)}) collective-permute-start(bf16[4,2,48,1536]{3,2,1,0:T(8,128)(2,1)S(1)} %pad_maximum_fusion.2), channel_id=1, source_target_pairs={{0,4},{2,6},{4,0},{6,2},{8,12},{10,14},{12,8},{14,10},{16,20},{18,... | collective-permute-start | bytes 3538952 | tf_op jit(solution)/shard_map/ppermute | solution.py:63
  157.0 40.3 %collective-permute-start.28 = (bf16[4,2,48,1536]{3,2,1,0:T(8,128)(2,1)S(1)}, bf16[4,2,48,1536]{3,2,1,0:T(8,128)(2,1)S(1)}, u32[]{:S(2)}, u32[]{:S(2)}) collective-permute-start(bf16[4,2,48,1536]{3,2,1,0:T(8,128)(2,1)S(1)} %pad_maximum_fusion.2), channel_id=1, source_target_pairs={{0,2},{2,0},{4,6},{6,4},{8,10},{10,8},{12,14},{14,12},{16,18},{18,... | collective-permute-start | bytes 3538952 | tf_op jit(solution)/shard_map/ppermute | solution.py:63
  159.7 37.5 %collective-permute-start.26 = (bf16[2,2,48,1536]{3,2,1,0:T(8,128)(2,1)S(1)}, bf16[2,2,48,1536]{3,2,1,0:T(8,128)(2,1)S(1)}, u32[]{:S(2)}, u32[]{:S(2)}) collective-permute-start(bf16[2,2,48,1536]{3,2,1,0:T(8,128)(2,1)S(1)} %slice.363), channel_id=1, source_target_pairs={{0,4},{2,6},{4,0},{6,2},{8,12},{10,14},{12,8},{14,10},{16,20},{18,... | collective-permute-start | bytes 1769480 | tf_op jit(solution)/shard_map/ppermute | solution.py:63
  161.7 35.6 %collective-permute-start.27 = (bf16[2,2,48,1536]{3,2,1,0:T(8,128)(2,1)S(1)}, bf16[2,2,48,1536]{3,2,1,0:T(8,128)(2,1)S(1)}, u32[]{:S(2)}, u32[]{:S(2)}) collective-permute-start(bf16[2,2,48,1536]{3,2,1,0:T(8,128)(2,1)S(1)} %slice.364), channel_id=1, source_target_pairs={{0,2},{2,0},{4,6},{6,4},{8,10},{10,8},{12,14},{14,12},{16,18},{18,... | collective-permute-start | bytes 1769480 | tf_op jit(solution)/shard_map/ppermute | solution.py:63
  258.1 35.5 %collective-permute-start.34 = (bf16[12,2,48,1536]{3,2,1,0:T(8,128)(2,1)}, bf16[12,2,48,1536]{3,2,1,0:T(8,128)(2,1)}, u32[]{:S(2)}, u32[]{:S(2)}) collective-permute-start(bf16[12,2,48,1536]{3,2,1,0:T(8,128)(2,1)} %constant_dynamic-update-slice_fusion.23.refs_0_), channel_id=1, source_target_pairs={{0,1},{1,0},{2,3},{3,2},{4,5},{5,4},{6,7},{7,6},{8,9},{9,8},{10,11... | collective-permute-start | bytes 10616840 | tf_op jit(solution)/shard_map/ppermute | solution.py:67
  259.5 34.1 %collective-permute-start.35 = (bf16[4,2,48,1536]{3,2,1,0:T(8,128)(2,1)}, bf16[4,2,48,1536]{3,2,1,0:T(8,128)(2,1)}, u32[]{:S(2)}, u32[]{:S(2)}) collective-permute-start(bf16[4,2,48,1536]{3,2,1,0:T(8,128)(2,1)} %constant_dynamic-update-slice_fusion.28.refs_2_), channel_id=1, source_target_pairs={{0,1},{1,0},{2,3},{3,2},{4,5},{5,4},{6,7},{7,6},{8,9},{9,8},{10,11... | collective-permute-start | bytes 3538952 | tf_op jit(solution)/shard_map/ppermute | solution.py:67
  265.2 32.9 %collective-permute-start.39 = (bf16[1,4,2,48,1536]{4,3,2,1,0:T(8,128)(2,1)}, bf16[1,4,2,48,1536]{4,3,2,1,0:T(8,128)(2,1)}, u32[]{:S(2)}, u32[]{:S(2)}) collective-permute-start(bf16[1,4,2,48,1536]{4,3,2,1,0:T(8,128)(2,1)} %dynamic-slice_bitcast_fusion.1), channel_id=1, source_target_pairs={{0,4},{2,6},{4,0},{6,2},{8,12},{10,14},{12,8},{14,10},{16,20},{18,... | collective-permute-start | bytes 3538952 | tf_op jit(solution)/shard_map/ppermute | solution.py:63
  268.6 29.4 %collective-permute-start.38 = (bf16[1,4,2,48,1536]{4,3,1,2,0:T(8,128)(2,1)}, bf16[1,4,2,48,1536]{4,3,1,2,0:T(8,128)(2,1)}, u32[]{:S(2)}, u32[]{:S(2)}) collective-permute-start(bf16[1,4,2,48,1536]{4,3,1,2,0:T(8,128)(2,1)} %bitcast.221), channel_id=1, source_target_pairs={{0,2},{2,0},{4,6},{6,4},{8,10},{10,8},{12,14},{14,12},{16,18},{18,... | collective-permute-start | bytes 3538952 | tf_op jit(solution)/shard_map/ppermute | solution.py:63
  334.2 39.2 %collective-permute-start.40 = (bf16[2,768,1536]{2,1,0:T(8,128)(2,1)}, bf16[2,768,1536]{2,1,0:T(8,128)(2,1)}, u32[]{:S(2)}, u32[]{:S(2)}) collective-permute-start(bf16[2,768,1536]{2,1,0:T(8,128)(2,1)} %get-tuple-element.241), channel_id=1, source_target_pairs={{0,1},{1,0},{2,3},{3,2},{4,5},{5,4},{6,7},{7,6},{8,9},{9,8},{10,11... | collective-permute-start | bytes 14155784 | tf_op jit(solution)/shard_map/ppermute | solution.py:67
  343.5 27.2 %collective-permute-start.43 = (bf16[2,4,2,48,384]{4,3,1,0,2:T(8,128)(2,1)}, bf16[2,4,2,48,384]{4,3,1,0,2:T(8,128)(2,1)}, u32[]{:S(2)}, u32[]{:S(2)}) collective-permute-start(bf16[2,4,2,48,384]{4,3,1,0,2:T(8,128)(2,1)} %bitcast.224), channel_id=1, source_target_pairs={{0,2},{2,0},{4,6},{6,4},{8,10},{10,8},{12,14},{14,12},{16,18},{18,... | collective-permute-start | bytes 1769480 | tf_op jit(solution)/shard_map/ppermute | solution.py:63
  344.6 27.5 %collective-permute-start.44 = (bf16[2,4,2,48,384]{4,3,2,1,0:T(8,128)(2,1)}, bf16[2,4,2,48,384]{4,3,2,1,0:T(8,128)(2,1)}, u32[]{:S(2)}, u32[]{:S(2)}) collective-permute-start(bf16[2,4,2,48,384]{4,3,2,1,0:T(8,128)(2,1)} %dynamic-slice_bitcast_fusion.7), channel_id=1, source_target_pairs={{0,4},{2,6},{4,0},{6,2},{8,12},{10,14},{12,8},{14,10},{16,20},{18,... | collective-permute-start | bytes 1769480 | tf_op jit(solution)/shard_map/ppermute | solution.py:63
  377.5 35.7 %collective-permute-start.46 = (bf16[1,4,2,48,1536]{4,3,2,1,0:T(8,128)(2,1)S(1)}, bf16[1,4,2,48,1536]{4,3,2,1,0:T(8,128)(2,1)}, u32[]{:S(2)}, u32[]{:S(2)}) collective-permute-start(bf16[1,4,2,48,1536]{4,3,2,1,0:T(8,128)(2,1)S(1)} %dynamic-slice_bitcast_fusion), channel_id=1, source_target_pairs={{0,4},{2,6},{4,0},{6,2},{8,12},{10,14},{12,8},{14,10},{16,20},{18,... | collective-permute-start | bytes 3538952 | tf_op jit(solution)/shard_map/ppermute | solution.py:63
  380.0 33.2 %collective-permute-start.45 = (bf16[1,4,2,48,1536]{4,3,1,2,0:T(8,128)(2,1)}, bf16[1,4,2,48,1536]{4,3,1,2,0:T(8,128)(2,1)S(1)}, u32[]{:S(2)}, u32[]{:S(2)}) collective-permute-start(bf16[1,4,2,48,1536]{4,3,1,2,0:T(8,128)(2,1)} %bitcast.220), channel_id=1, source_target_pairs={{0,2},{2,0},{4,6},{6,4},{8,10},{10,8},{12,14},{14,12},{16,18},{18,... | collective-permute-start | bytes 3538952 | tf_op jit(solution)/shard_map/ppermute | solution.py:63
  381.4 29.4 %collective-permute-start.47 = (bf16[2,4,48,384]{3,2,1,0:T(8,128)(2,1)S(1)}, bf16[2,4,48,384]{3,2,1,0:T(8,128)(2,1)S(1)}, u32[]{:S(2)}, u32[]{:S(2)}) collective-permute-start(bf16[2,4,48,384]{3,2,1,0:T(8,128)(2,1)S(1)} %dynamic-slice_bitcast_fusion.19), channel_id=1, source_target_pairs={{0,4},{2,6},{4,0},{6,2},{8,12},{10,14},{12,8},{14,10},{16,20},{18,... | collective-permute-start | bytes 884744 | tf_op jit(solution)/shard_map/ppermute | solution.py:63
  382.3 30.8 %collective-permute-start.48 = (bf16[2,4,48,384]{3,2,1,0:T(8,128)(2,1)}, bf16[2,4,48,384]{3,2,1,0:T(8,128)(2,1)S(1)}, u32[]{:S(2)}, u32[]{:S(2)}) collective-permute-start(bf16[2,4,48,384]{3,2,1,0:T(8,128)(2,1)} %dynamic-slice_bitcast_fusion.18), channel_id=1, source_target_pairs={{0,2},{2,0},{4,6},{6,4},{8,10},{10,8},{12,14},{14,12},{16,18},{18,... | collective-permute-start | bytes 884744 | tf_op jit(solution)/shard_map/ppermute | solution.py:63
  414.3 24.6 %collective-permute-start.62 = (bf16[12,2,48,384]{3,2,0,1:T(8,128)(2,1)S(1)}, bf16[12,2,48,384]{3,2,0,1:T(8,128)(2,1)S(1)}, u32[]{:S(2)}, u32[]{:S(2)}) collective-permute-start(bf16[12,2,48,384]{3,2,0,1:T(8,128)(2,1)S(1)} %fusion.26), channel_id=1, source_target_pairs={{0,8},{2,10},{4,12},{6,14},{24,16},{26,18},{28,20},{30,22},{1,9},{... | collective-permute-start | bytes 2654216 | tf_op jit(solution)/shard_map/ppermute | solution.py:250
  425.8 44.7 %collective-permute-start.53 = (bf16[2,4,2,48,384]{4,3,2,1,0:T(8,128)(2,1)S(1)}, bf16[2,4,2,48,384]{4,3,2,1,0:T(8,128)(2,1)}, u32[]{:S(2)}, u32[]{:S(2)}) collective-permute-start(bf16[2,4,2,48,384]{4,3,2,1,0:T(8,128)(2,1)S(1)} %dynamic-slice_bitcast_fusion.4), channel_id=1, source_target_pairs={{0,4},{2,6},{4,0},{6,2},{8,12},{10,14},{12,8},{14,10},{16,20},{18,... | collective-permute-start | bytes 1769480 | tf_op jit(solution)/shard_map/ppermute | solution.py:63
  427.0 43.5 %collective-permute-start.52 = (bf16[2,4,2,48,384]{4,3,1,0,2:T(8,128)(2,1)S(1)}, bf16[2,4,2,48,384]{4,3,1,0,2:T(8,128)(2,1)S(1)}, u32[]{:S(2)}, u32[]{:S(2)}) collective-permute-start(bf16[2,4,2,48,384]{4,3,1,0,2:T(8,128)(2,1)S(1)} %bitcast.266), channel_id=1, source_target_pairs={{0,2},{2,0},{4,6},{6,4},{8,10},{10,8},{12,14},{14,12},{16,18},{18,... | collective-permute-start | bytes 1769480 | tf_op jit(solution)/shard_map/ppermute | solution.py:63
  428.6 41.9 %collective-permute-start.50 = (bf16[1,4,48,1536]{3,2,1,0:T(8,128)(2,1)}, bf16[1,4,48,1536]{3,2,1,0:T(8,128)(2,1)S(1)}, u32[]{:S(2)}, u32[]{:S(2)}) collective-permute-start(bf16[1,4,48,1536]{3,2,1,0:T(8,128)(2,1)} %dynamic-slice_bitcast_fusion.6), channel_id=1, source_target_pairs={{0,4},{2,6},{4,0},{6,2},{8,12},{10,14},{12,8},{14,10},{16,20},{18,... | collective-permute-start | bytes 1769480 | tf_op jit(solution)/shard_map/ppermute | solution.py:63
  429.7 40.8 %collective-permute-start.51 = (bf16[1,4,48,1536]{3,2,1,0:T(8,128)(2,1)S(1)}, bf16[1,4,48,1536]{3,2,1,0:T(8,128)(2,1)S(1)}, u32[]{:S(2)}, u32[]{:S(2)}) collective-permute-start(bf16[1,4,48,1536]{3,2,1,0:T(8,128)(2,1)S(1)} %dynamic-slice_bitcast_fusion.5), channel_id=1, source_target_pairs={{0,2},{2,0},{4,6},{6,4},{8,10},{10,8},{12,14},{14,12},{16,18},{18,... | collective-permute-start | bytes 1769480 | tf_op jit(solution)/shard_map/ppermute | solution.py:63
  476.1 27.3 %collective-permute-start.70 = (bf16[2,2,48,1536]{3,2,0,1:T(8,128)(2,1)}, bf16[2,2,48,1536]{3,2,0,1:T(8,128)(2,1)}, u32[]{:S(2)}, u32[]{:S(2)}) collective-permute-start(bf16[2,2,48,1536]{3,2,0,1:T(8,128)(2,1)} %dynamic-slice_bitcast_fusion.2), channel_id=1, source_target_pairs={{0,8},{2,10},{4,12},{6,14},{24,16},{26,18},{28,20},{30,22},{1,9},{... | collective-permute-start | bytes 1769480 | tf_op jit(solution)/shard_map/ppermute | solution.py:250
  (227 other events, 2211.1 us)
